TPU v7x, 32 devices: a whole 2x2x4 slice. The times are simulated.
32 devices in a mesh: blk: 8 (over y, x, core), dp: 4 (over z).
Axes of the slice: x: 2, y: 2, z: 4, core: 2. Of those that a mesh axis runs over, the one named last changes fastest.
Arguments:
- tokens: bfloat16 [8, 2048, 1024], P('dp', 'blk'), may hold values from -6 to 6
- input_weight: bfloat16 [1024, 3072], P(('blk', 'dp')), may hold values from -0.1875 to 0.1875
- output_weight: bfloat16 [1024, 1024], P(('blk', 'dp')), may hold values from -3 to 3
- expand_weight: bfloat16 [1024, 4096], P(('blk', 'dp')), may hold values from -0.1875 to 0.1875
- reduce_weight: bfloat16 [4096, 1024], P(('blk', 'dp')), may hold values from -0.09375 to 0.09375
- gains: bfloat16 [2, 1024], P(None, ('blk', 'dp')), may hold values from 0.5 to 1.5
- biases: bfloat16 [6, 1024], P(None, ('blk', 'dp')), may hold values from -2 to 2
- hidden_bias: bfloat16 [4096], P(('blk', 'dp')), may hold values from -3 to 3
- segment: int32 [8, 2048], P('dp', 'blk'), may hold values from 0 to 3, as said below
- present: int32 [8, 2048], P('dp', 'blk'), may hold values from 0 to 1, as said below
- cotangent: bfloat16 [8, 2048, 1024], P('dp', 'blk'), may hold values from -6 to 6
Outputs:
- output: bfloat16 [8, 2048, 1024], P('dp', 'blk')
- grad_tokens: float32 [8, 2048, 1024], P('dp', 'blk')
- grad_input: float32 [1024, 3072], P(('blk', 'dp'))
- grad_output: float32 [1024, 1024], P(('blk', 'dp'))
- grad_expand: float32 [1024, 4096], P(('blk', 'dp'))
- grad_reduce: float32 [4096, 1024], P(('blk', 'dp'))
- grad_gains: float32 [2, 1024], P(None, ('blk', 'dp'))
- grad_biases: float32 [6, 1024], P(None, ('blk', 'dp'))
- grad_hidden: float32 [4096], P(('blk', 'dp'))
Inputs may be any that keep to these rules, and one draw needn't show every extreme that they name: Each slot row holds either one protein (all segment values 0) or four consecutive ones numbered 0 to 3 in order, protein k beginning within 128 positions of k * 512. Of the 2 slots of each index of dp, one holds a single protein with every position present. Each protein has present = 1 on a leading run of at least half of its positions and 0 after it.
All inputs are finite; a program needn't handle non-finite values.
Results may differ from a plain program's by a relative error of at most 0.017.
Values may be sent and summed in bfloat16 or wider, within the bound.
A program may use at most 192 MiB of HBM per device.

v0:
```python
import jax
import jax.numpy as jnp
from jax import lax
from jax.sharding import PartitionSpec as P

HEADS = 16


EPSILON = 1e-12
HUGE = 1e30


def for_sending(shard):
    return jax.tree.map(lambda a: a.astype(jnp.bfloat16) if a.dtype == jnp.float32 else a, shard)


def from_behind(block, axis, distance):
    devices = range(lax.axis_size(axis))
    route = [((i - distance) % len(devices), i) for i in devices]
    return lax.ppermute(block, axis, route)


def layer_norm(values, gain, shift):
    mean = jnp.mean(values, axis=-1, keepdims=True)
    centred = values - mean
    spread = jnp.mean(centred * centred, axis=-1, keepdims=True)
    return centred * lax.rsqrt(spread + EPSILON) * gain + shift


def exact_gelu(values):
    return jax.nn.gelu(values, approximate=False)


def by_heads(block, heads):
    return block.reshape(block.shape[0], block.shape[1], heads, block.shape[2] // heads)


def visible(segment, tags):
    return (
        segment.astype(jnp.float32)[:, None, :, None] == tags.astype(jnp.float32)[:, None, None, :]
    )


def attend_block(state, queries, segment, block):
    total, top, mass = state
    keys, values, tags = block
    heads = queries.shape[2]
    scale = queries.shape[3] ** (-0.5)
    scores = (
        jnp.einsum(
            "sqhd,skhd->shqk", queries, by_heads(keys, heads), preferred_element_type=jnp.float32
        )
        * scale
    )
    allowed = visible(segment, tags)
    new_top = jnp.maximum(top, jnp.max(jnp.where(allowed, scores, -HUGE), axis=-1))
    weights = jnp.where(allowed, jnp.exp(scores - new_top[..., None]), 0.0)
    factor = jnp.exp(top - new_top)
    mass = mass * factor + jnp.sum(weights, axis=-1)
    total = total * factor[..., None] + jnp.einsum(
        "shqk,skhd->shqd",
        weights.astype(jnp.bfloat16),
        by_heads(values, heads),
        preferred_element_type=jnp.float32,
    )
    return (total, new_top, mass)


def cycle_forward(couriers, segment, turns):

    def fresh(queries):
        slots, rows, heads, size = queries.shape
        return (
            jnp.zeros((slots, heads, rows, size), jnp.float32),
            jnp.full((slots, heads, rows), -HUGE, jnp.float32),
            jnp.zeros((slots, heads, rows), jnp.float32),
        )

    def absorb(states, blocks):
        return [
            attend_block(state, courier[0], segment, block)
            for state, courier, block in zip(states, couriers, blocks)
        ]

    def advance(counter, carry):
        states, blocks = carry
        states = absorb(states, blocks)
        blocks = [courier[2](block) for courier, block in zip(couriers, blocks)]
        return (states, blocks)

    states = [fresh(courier[0]) for courier in couriers]
    blocks = [courier[1] for courier in couriers]
    states, blocks = lax.fori_loop(0, turns - 1, advance, (states, blocks))
    states = absorb(states, blocks)
    return [(total / mass[..., None], top + jnp.log(mass)) for total, top, mass in states]


def block_grads(courier, segment, block):
    queries, grad_out, log_mass, delta = (courier[0], courier[1], courier[2], courier[3])
    keys, values, tags = block
    heads = queries.shape[2]
    scale = queries.shape[3] ** (-0.5)
    key_heads = by_heads(keys, heads)
    value_heads = by_heads(values, heads)
    scores = (
        jnp.einsum("sqhd,skhd->shqk", queries, key_heads, preferred_element_type=jnp.float32)
        * scale
    )
    allowed = visible(segment, tags)
    probs = jnp.where(allowed, jnp.exp(scores - log_mass[..., None]), 0.0)
    pushed = jnp.einsum(
        "sqhd,skhd->shqk", grad_out, value_heads, preferred_element_type=jnp.float32
    )
    grad_scores = (probs * (pushed - delta[..., None])).astype(jnp.bfloat16)
    grad_query = (
        jnp.einsum("shqk,skhd->sqhd", grad_scores, key_heads, preferred_element_type=jnp.float32)
        * scale
    )
    grad_keys = (
        jnp.einsum("shqk,sqhd->skhd", grad_scores, queries, preferred_element_type=jnp.float32)
        * scale
    )
    grad_values = jnp.einsum(
        "shqk,sqhd->skhd", probs.astype(jnp.bfloat16), grad_out, preferred_element_type=jnp.float32
    )
    return (grad_query, grad_keys.reshape(keys.shape), grad_values.reshape(values.shape))


def cycle_backward(couriers, segment, turns):

    def absorb(query_grads, sums, blocks):
        out_grads, out_sums = ([], [])
        for courier, grad_query, partial_value, block in zip(couriers, query_grads, sums, blocks):
            part_query, part_keys, part_values = block_grads(courier, segment, block)
            out_grads.append(grad_query + part_query)
            out_sums.append((partial_value[0] + part_keys, partial_value[1] + part_values))
        return (out_grads, out_sums)

    def advance(counter, carry):
        query_grads, sums, blocks = carry
        query_grads, sums = absorb(query_grads, sums, blocks)
        sums = [courier[6](partial_value) for courier, partial_value in zip(couriers, sums)]
        blocks = [courier[5](block) for courier, block in zip(couriers, blocks)]
        return (query_grads, sums, blocks)

    query_grads = [jnp.zeros(courier[0].shape, jnp.float32) for courier in couriers]
    sums = [
        (jnp.zeros(courier[4][0].shape, jnp.float32), jnp.zeros(courier[4][1].shape, jnp.float32))
        for courier in couriers
    ]
    blocks = [courier[4] for courier in couriers]
    query_grads, sums, blocks = lax.fori_loop(0, turns - 1, advance, (query_grads, sums, blocks))
    query_grads, sums = absorb(query_grads, sums, blocks)
    sums = [courier[6](partial_value) for courier, partial_value in zip(couriers, sums)]
    return (query_grads, sums)


def on_device(
    tokens,
    input_weight,
    output_weight,
    expand_weight,
    reduce_weight,
    gains,
    biases,
    hidden_bias,
    segment,
    present,
    cotangent,
):
    slots, rows, width = tokens.shape
    heads = HEADS
    turns = lax.axis_size("blk")
    full_input, full_output, full_expand, full_reduce, full_gains, full_biases, full_hidden = (
        lax.all_gather(input_weight, ("blk", "dp"), axis=0, tiled=True),
        lax.all_gather(output_weight, ("blk", "dp"), axis=0, tiled=True),
        lax.all_gather(expand_weight, ("blk", "dp"), axis=0, tiled=True),
        lax.all_gather(reduce_weight, ("blk", "dp"), axis=0, tiled=True),
        lax.all_gather(gains, ("blk", "dp"), axis=1, tiled=True),
        lax.all_gather(biases, ("blk", "dp"), axis=1, tiled=True),
        lax.all_gather(hidden_bias, ("blk", "dp"), axis=0, tiled=True),
    )
    gain_rows = full_gains.astype(jnp.float32)
    bias_rows = full_biases.astype(jnp.float32)
    flattened = tokens.reshape(slots * rows, width)
    mixed = jnp.dot(flattened, full_input, preferred_element_type=jnp.float32)
    queries = (
        (mixed[:, :width] + bias_rows[0])
        .astype(jnp.bfloat16)
        .reshape(slots, rows, heads, width // heads)
    )
    keys = mixed[:, width : 2 * width].astype(jnp.bfloat16).reshape(slots, rows, width)
    values = (mixed[:, 2 * width :] + bias_rows[1]).astype(jnp.bfloat16).reshape(slots, rows, width)
    tags = jnp.where(present == 1, segment, -1).astype(jnp.bfloat16)
    forward_couriers = [
        (
            queries,
            (keys, values, tags),
            lambda moved: jax.tree.map(
                lambda part, own: part.astype(own.dtype),
                from_behind(for_sending(moved), "blk", 1),
                moved,
            ),
        )
    ]
    pieces = cycle_forward(forward_couriers, segment, turns)
    attended = jnp.concatenate([piece[0] for piece in pieces], axis=1)
    log_mass = jnp.concatenate([piece[1] for piece in pieces], axis=1)
    attended_rows = attended.transpose(0, 2, 1, 3).reshape(slots * rows, width).astype(jnp.bfloat16)
    branch = jnp.dot(attended_rows, full_output, preferred_element_type=jnp.float32) + bias_rows[2]
    first_sum = flattened.astype(jnp.float32) + branch
    normed, first_back = jax.vjp(layer_norm, first_sum, gain_rows[0], bias_rows[3])
    normed_low = normed.astype(jnp.bfloat16)
    pre = jnp.dot(normed_low, full_expand, preferred_element_type=jnp.float32) + full_hidden.astype(
        jnp.float32
    )
    act, gelu_back = jax.vjp(exact_gelu, pre)
    act_low = act.astype(jnp.bfloat16)
    ffn_out = jnp.dot(act_low, full_reduce, preferred_element_type=jnp.float32) + bias_rows[4]
    result, second_back = jax.vjp(layer_norm, normed + ffn_out, gain_rows[1], bias_rows[5])
    output = result.astype(jnp.bfloat16).reshape(slots, rows, width)
    back_input, back_output, back_expand, back_reduce = (
        lax.all_gather(input_weight, ("blk", "dp"), axis=0, tiled=True),
        lax.all_gather(output_weight, ("blk", "dp"), axis=0, tiled=True),
        lax.all_gather(expand_weight, ("blk", "dp"), axis=0, tiled=True),
        lax.all_gather(reduce_weight, ("blk", "dp"), axis=0, tiled=True),
    )
    d_second, d_gain_two, d_shift_two = second_back(
        cotangent.reshape(slots * rows, width).astype(jnp.float32)
    )
    d_ffn = d_second.astype(jnp.bfloat16)
    grad_reduce = jnp.einsum("ti,tj->ij", act_low, d_ffn, preferred_element_type=jnp.float32)
    d_ffn_bias = jnp.sum(d_ffn.astype(jnp.float32), axis=0)
    d_act = jnp.einsum("tj,ij->ti", d_ffn, back_reduce, preferred_element_type=jnp.float32)
    (d_pre,) = gelu_back(d_act)
    d_pre_low = d_pre.astype(jnp.bfloat16)
    grad_expand = jnp.einsum("ti,tj->ij", normed_low, d_pre_low, preferred_element_type=jnp.float32)
    grad_hidden = jnp.sum(d_pre_low.astype(jnp.float32), axis=0)
    d_normed = d_second + jnp.einsum(
        "tj,ij->ti", d_pre_low, back_expand, preferred_element_type=jnp.float32
    )
    d_first, d_gain_one, d_shift_one = first_back(d_normed)
    d_branch = d_first.astype(jnp.bfloat16)
    grad_output = jnp.einsum(
        "ti,tj->ij", attended_rows, d_branch, preferred_element_type=jnp.float32
    )
    d_branch_bias = jnp.sum(d_branch.astype(jnp.float32), axis=0)
    d_att = jnp.einsum(
        "tj,ij->ti", d_branch, back_output, preferred_element_type=jnp.float32
    ).astype(jnp.bfloat16)
    grad_heads = d_att.reshape(slots, rows, heads, width // heads)
    delta = jnp.einsum("sqhd,shqd->shq", grad_heads, attended, preferred_element_type=jnp.float32)
    backward_couriers = [
        (
            queries,
            grad_heads,
            log_mass,
            delta,
            (keys, values, tags),
            lambda moved: jax.tree.map(
                lambda part, own: part.astype(own.dtype),
                from_behind(for_sending(moved), "blk", 1),
                moved,
            ),
            lambda moved: jax.tree.map(
                lambda part, own: part.astype(own.dtype),
                from_behind(for_sending(moved), "blk", 1),
                moved,
            ),
        )
    ]
    query_grads, sums = cycle_backward(backward_couriers, segment, turns)
    grad_query_rows = jnp.concatenate(query_grads, axis=2).reshape(slots * rows, width)
    grad_key_rows = jnp.concatenate([partial_value[0] for partial_value in sums], axis=-1).reshape(
        slots * rows, width
    )
    grad_value_rows = jnp.concatenate(
        [partial_value[1] for partial_value in sums], axis=-1
    ).reshape(slots * rows, width)
    grad_mixed = jnp.concatenate([grad_query_rows, grad_key_rows, grad_value_rows], axis=1).astype(
        jnp.bfloat16
    )
    grad_input = jnp.einsum("ti,tj->ij", flattened, grad_mixed, preferred_element_type=jnp.float32)
    mixed_sums = jnp.sum(grad_mixed.astype(jnp.float32), axis=0)
    grad_tokens = d_first + jnp.einsum(
        "tj,ij->ti", grad_mixed, back_input, preferred_element_type=jnp.float32
    )
    grad_gains = jnp.stack([d_gain_one, d_gain_two], axis=0)
    grad_biases = jnp.stack(
        [
            mixed_sums[:width],
            mixed_sums[2 * width :],
            d_branch_bias,
            d_shift_one,
            d_ffn_bias,
            d_shift_two,
        ],
        axis=0,
    )
    summed = (
        lax.psum_scatter(grad_input, ("blk", "dp"), scatter_dimension=0, tiled=True),
        lax.psum_scatter(grad_output, ("blk", "dp"), scatter_dimension=0, tiled=True),
        lax.psum_scatter(grad_expand, ("blk", "dp"), scatter_dimension=0, tiled=True),
        lax.psum_scatter(grad_reduce, ("blk", "dp"), scatter_dimension=0, tiled=True),
        lax.psum_scatter(grad_gains, ("blk", "dp"), scatter_dimension=1, tiled=True),
        lax.psum_scatter(grad_biases, ("blk", "dp"), scatter_dimension=1, tiled=True),
        lax.psum_scatter(grad_hidden, ("blk", "dp"), scatter_dimension=0, tiled=True),
    )
    return (
        output,
        grad_tokens.reshape(slots, rows, width),
        summed[0],
        summed[1],
        summed[2],
        summed[3],
        summed[4],
        summed[5],
        summed[6],
    )


def solution(mesh):
    in_specs = (
        P("dp", "blk", None),
        P(("blk", "dp"), None),
        P(("blk", "dp"), None),
        P(("blk", "dp"), None),
        P(("blk", "dp"), None),
        P(None, ("blk", "dp")),
        P(None, ("blk", "dp")),
        P(("blk", "dp")),
        P("dp", "blk"),
        P("dp", "blk"),
        P("dp", "blk", None),
    )
    out_specs = (
        P("dp", "blk", None),
        P("dp", "blk", None),
        P(("blk", "dp"), None),
        P(("blk", "dp"), None),
        P(("blk", "dp"), None),
        P(("blk", "dp"), None),
        P(None, ("blk", "dp")),
        P(None, ("blk", "dp")),
        P(("blk", "dp")),
    )
    return jax.shard_map(
        on_device, mesh=mesh, in_specs=in_specs, out_specs=out_specs, check_vma=False
    )
```

profile of v0, /device:TPU:0, one launch (start us, length us, event | category | flops | bytes accessed | tf_op | source)
XLA Modules:
  0.0 2345.4 jit_solution(16225562622323669291)
XLA Ops:
  10.1 71.3 %all-gather = bf16[32,32,6]{1,2,0:T(8,128)(2,1)S(1)} all-gather(bf16[1,32,6]{1,2,0:T(8,128)(2,1)} %bitcast.248), channel_id=1, replica_groups=mesh['blk'=8,'dp'=4] {'blk','dp'}, dimensions={0}, use_global_device_ids=true | all-gather | bytes 12672 | tf_op jit(solution)/shard_map/all_gather | solution.py:180
  82.1 63.2 %all-gather.2 = bf16[32,1,128]{2,1,0:T(2,128)(2,1)S(1)} all-gather(bf16[1,1,128]{2,1,0:T(2,128)(2,1)} %bitcast.249), channel_id=1, replica_groups=mesh['blk'=8,'dp'=4] {'blk','dp'}, dimensions={0}, use_global_device_ids=true | all-gather | bytes 8448 | tf_op jit(solution)/shard_map/all_gather | solution.py:181
  146.6 65.9 %all-gather.1 = bf16[32,32,2]{1,2,0:T(2,128)(2,1)S(1)} all-gather(bf16[1,32,2]{1,2,0:T(2,128)(2,1)} %bitcast.250), channel_id=1, replica_groups=mesh['blk'=8,'dp'=4] {'blk','dp'}, dimensions={0}, use_global_device_ids=true | all-gather | bytes 4224 | tf_op jit(solution)/shard_map/all_gather | solution.py:179
  234.3 208.7 %while.46 = (s32[]{:T(128)}, f32[2,16,256,64]{2,3,1,0:T(8,128)}, f32[2,16,256]{2,1,0:T(8,128)S(1)}, f32[2,16,256]{2,1,0:T(8,128)S(1)}, bf16[2,256,1024]{1,2,0:T(...) while((s32[]{:T(128)}, f32[2,16,256,64]{2,3,1,0:T(8,128)}, ...), condition=%wide.region_3.4_spmd.clone, body=%wide.region_0.3_spmd.clone.sunk | while | flops 561684992 | bytes 62928164 | solution.py:93
  244.9 23.5 %collective-permute-done.2 = bf16[2,256]{1,0:T(2,128)(2,1)S(1)} collective-permute-done((bf16[2,256]{1,0:T(2,128)(2,1)S(1)}, bf16[2,256]{1,0:T(2,128)(2,1)S(1)}, u32[]{:S(2)}, u32[]{:S(2)}) %collective-permute-start.2) | collective-permute-done | bytes 1056 | tf_op jit(solution)/shard_map/while/body/eval_jaxpr/ppermute | solution.py:20
  278.9 31.0 %collective-permute-done.2 = bf16[2,256]{1,0:T(2,128)(2,1)S(1)} collective-permute-done((bf16[2,256]{1,0:T(2,128)(2,1)S(1)}, bf16[2,256]{1,0:T(2,128)(2,1)S(1)}, u32[]{:S(2)}, u32[]{:S(2)}) %collective-permute-start.2) | collective-permute-done | bytes 1056 | tf_op jit(solution)/shard_map/while/body/eval_jaxpr/ppermute | solution.py:20
  320.4 16.1 collective-permute-done.2
  347.0 16.1 collective-permute-done.2
  373.6 16.1 collective-permute-done.2
  400.2 16.1 collective-permute-done.2
  426.8 16.1 collective-permute-done.2
  457.4 27.8 %multiply_convert_fusion.2 = (bf16[512,4096]{1,0:T(8,128)(2,1)}, f32[512,4096]{1,0:T(8,128)}, f32[512,4096]{1,0:T(8,128)}) fusion(f32[4096]{0:T(1024)S(1)} %bitcast.234, bf16[1024,4096]{1,0:T(8,128)(2,1)} %all-gather.12.cloned.1.call-done, f32[512,1024]{1,0:T(8,128)S(1)} %get-tuple-element.548, f32[1024]{0:T(1024)S(1)} %bitcast.243, ...), kind=kOutput, calls=%fused_computation.41 | convolution fusion | flops 4436000768 | bytes 31485952 | tf_op jit(solution)/shard_map/dot_general | solution.py:214
  498.3 14.4 convert_reduce_fusion
  530.1 465.0 %while.47 = (s32[]{:T(128)}, f32[2,256,16,64]{1,3,2,0:T(8,128)}, f32[2,256,1024]{1,2,0:T(8,128)}, f32[2,256,1024]{1,2,0:T(8,128)}, bf16[2,256,1024]{1,2,0:T(8,12...) while((s32[]{:T(128)}, f32[2,256,16,64]{1,3,2,0:T(8,128)}, ...), condition=%wide.region_15.16_spmd.clone, body=%wide.region_14.15_spmd.clone.sunk | while | flops 1369571840 | bytes 171423168 | solution.py:152
  576.4 19.8 collective-permute-done.7
  642.9 19.8 collective-permute-done.7
  709.4 19.8 collective-permute-done.7
  775.9 19.8 collective-permute-done.7
  842.4 19.8 collective-permute-done.7
  908.9 19.8 collective-permute-done.7
  975.3 19.8 collective-permute-done.7
  1052.1 11.2 convolution_bitcast_fusion
  1063.3 12.6 copy.148
  1077.5 10.8 fusion.65
  1089.5 10.4 fusion.82
  1100.6 37.7 %all-reduce = f32[4096]{0:T(1024)S(1)} all-reduce(f32[4096]{0:T(1024)S(1)} %copy-done.38), channel_id=8, replica_groups=mesh['blk'=8,'dp'=4] {'blk','dp'}, use_global_device_ids=true, to_apply=%region_30.31.clone | all-reduce | flops 4096 | bytes 32768
  1138.8 27.8 %reduce-scatter.21.cloned.1.call-done = f32[32,2]{1,0:T(8,128)} async-done(((f32[1024,2]{1,0:T(8,128)}), f32[32,2]{1,0:T(8,128)}) %reduce-scatter.21.cloned.1.call-update) | async-done | bytes 272
  1176.3 122.9 %reduce-scatter.23.cloned.1.call-done = f32[32,6]{1,0:T(8,128)} async-done(((f32[1024,6]{1,0:T(8,128)}), f32[32,6]{1,0:T(8,128)}) %reduce-scatter.23.cloned.1.call-update) | async-done | bytes 784
  1300.6 145.3 %reduce-scatter.13.cloned.1.call-done = f32[32,1024]{1,0:T(8,128)} async-done(((f32[1024,1024]{1,0:T(8,128)}), f32[32,1024]{1,0:T(8,128)}) %reduce-scatter.13.cloned.1.call-update) | async-done | bytes 131088 | tf_op jit(solution)/shard_map/reduce_scatter | solution.py:302
  1445.9 160.9 %reduce-scatter.19.cloned.1.call-done = f32[32,3072]{1,0:T(8,128)} async-done(((f32[1024,3072]{1,0:T(8,128)}), f32[32,3072]{1,0:T(8,128)}) %reduce-scatter.19.cloned.1.call-update) | async-done | bytes 393232
  1606.8 366.3 %reduce-scatter.15.cloned.1.call-done = f32[32,4096]{1,0:T(8,128)} async-done(((f32[1024,4096]{1,0:T(8,128)}), f32[32,4096]{1,0:T(8,128)}) %reduce-scatter.15.cloned.1.call-update) | async-done | bytes 524304 | tf_op jit(solution)/shard_map/reduce_scatter | solution.py:303
  1973.1 365.0 %reduce-scatter.17.cloned.1.call-done = f32[128,1024]{1,0:T(8,128)} async-done(((f32[4096,1024]{1,0:T(8,128)}), f32[128,1024]{1,0:T(8,128)}) %reduce-scatter.17.cloned.1.call-update) | async-done | bytes 524304 | tf_op jit(solution)/shard_map/reduce_scatter | solution.py:304
  (573 shorter events, 541.4 us)
Async XLA Ops:
  7.2 206.1 %all-gather.8.cloned.1.call-start = ((), (), s32[]{:S(2)}) async-start(), calls=%async_computation.6 | async-start | bytes 6488064 | tf_op jit(solution)/shard_map/all_gather | solution.py:175
  7.9 445.6 %all-gather.10.cloned.1.call-start = ((), (), s32[]{:S(2)}) async-start(), calls=%async_computation.7 | async-start | bytes 2162688 | tf_op jit(solution)/shard_map/all_gather | solution.py:176
  8.7 448.8 %all-gather.12.cloned.1.call-start = ((), (), s32[]{:S(2)}) async-start(), calls=%async_computation.8 | async-start | bytes 8650752 | tf_op jit(solution)/shard_map/all_gather | solution.py:177
  9.4 475.8 %all-gather.14.cloned.1.call-start = ((), (), s32[]{:S(2)}) async-start(), calls=%async_computation.9 | async-start | bytes 8650752 | tf_op jit(solution)/shard_map/all_gather | solution.py:178
  10.0 1156.6 %reduce-scatter.21.cloned.1.call-start = ((), (), s32[]{:S(2)}) async-start(), calls=%async_computation.14 | async-start | bytes 540672
  268.5 41.4 %collective-permute-start = (bf16[2,256,1024]{1,2,0:T(8,128)(2,1)S(1)}, bf16[2,256,1024]{1,2,0:T(8,128)(2,1)S(1)}, u32[]{:S(2)}, u32[]{:S(2)}) collective-permute-start(bf16[2,256,1024]{1,2,0:T(8,128)(2,1)S(1)} %copy.176), channel_id=1, source_target_pairs={{28,0},{0,4},{4,8},{8,12},{12,16},{16,20},{20,24},{24,28},{29,1},{... | collective-permute-start | bytes 3145736 | tf_op jit(solution)/shard_map/while/body/eval_jaxpr/ppermute | solution.py:20
  552.9 43.3 %collective-permute-start.5 = (bf16[2,256,1024]{1,2,0:T(8,128)(2,1)S(1)}, bf16[2,256,1024]{1,2,0:T(8,128)(2,1)S(1)}, u32[]{:S(2)}, u32[]{:S(2)}) collective-permute-start(bf16[2,256,1024]{1,2,0:T(8,128)(2,1)S(1)} %copy.197), channel_id=1, source_target_pairs={{28,0},{0,4},{4,8},{8,12},{12,16},{16,20},{20,24},{24,28},{29,1},{... | collective-permute-start | bytes 3145736 | tf_op jit(solution)/shard_map/while/body/eval_jaxpr/ppermute | solution.py:20
  552.9 43.3 %collective-permute-start.6 = (bf16[2,256,1024]{1,2,0:T(8,128)(2,1)}, bf16[2,256,1024]{1,2,0:T(8,128)(2,1)}, u32[]{:S(2)}, u32[]{:S(2)}) collective-permute-start(bf16[2,256,1024]{1,2,0:T(8,128)(2,1)} %copy.198), channel_id=1, source_target_pairs={{28,0},{0,4},{4,8},{8,12},{12,16},{16,20},{20,24},{24,28},{29,1},{... | collective-permute-start | bytes 3145736 | tf_op jit(solution)/shard_map/while/body/eval_jaxpr/ppermute | solution.py:20
  554.8 41.4 %collective-permute-start.7 = (bf16[2,256]{1,0:T(2,128)(2,1)S(1)}, bf16[2,256]{1,0:T(2,128)(2,1)S(1)}, u32[]{:S(2)}, u32[]{:S(2)}) collective-permute-start(bf16[2,256]{1,0:T(2,128)(2,1)S(1)} %copy.199), channel_id=1, source_target_pairs={{28,0},{0,4},{4,8},{8,12},{12,16},{16,20},{20,24},{24,28},{29,1},{... | collective-permute-start | bytes 3080 | tf_op jit(solution)/shard_map/while/body/eval_jaxpr/ppermute | solution.py:20
  619.4 43.3 %collective-permute-start.5 = (bf16[2,256,1024]{1,2,0:T(8,128)(2,1)S(1)}, bf16[2,256,1024]{1,2,0:T(8,128)(2,1)S(1)}, u32[]{:S(2)}, u32[]{:S(2)}) collective-permute-start(bf16[2,256,1024]{1,2,0:T(8,128)(2,1)S(1)} %copy.197), channel_id=1, source_target_pairs={{28,0},{0,4},{4,8},{8,12},{12,16},{16,20},{20,24},{24,28},{29,1},{... | collective-permute-start | bytes 3145736 | tf_op jit(solution)/shard_map/while/body/eval_jaxpr/ppermute | solution.py:20
  619.4 43.3 %collective-permute-start.6 = (bf16[2,256,1024]{1,2,0:T(8,128)(2,1)}, bf16[2,256,1024]{1,2,0:T(8,128)(2,1)}, u32[]{:S(2)}, u32[]{:S(2)}) collective-permute-start(bf16[2,256,1024]{1,2,0:T(8,128)(2,1)} %copy.198), channel_id=1, source_target_pairs={{28,0},{0,4},{4,8},{8,12},{12,16},{16,20},{20,24},{24,28},{29,1},{... | collective-permute-start | bytes 3145736 | tf_op jit(solution)/shard_map/while/body/eval_jaxpr/ppermute | solution.py:20
  621.3 41.4 %collective-permute-start.7 = (bf16[2,256]{1,0:T(2,128)(2,1)S(1)}, bf16[2,256]{1,0:T(2,128)(2,1)S(1)}, u32[]{:S(2)}, u32[]{:S(2)}) collective-permute-start(bf16[2,256]{1,0:T(2,128)(2,1)S(1)} %copy.199), channel_id=1, source_target_pairs={{28,0},{0,4},{4,8},{8,12},{12,16},{16,20},{20,24},{24,28},{29,1},{... | collective-permute-start | bytes 3080 | tf_op jit(solution)/shard_map/while/body/eval_jaxpr/ppermute | solution.py:20
  685.9 43.3 %collective-permute-start.5 = (bf16[2,256,1024]{1,2,0:T(8,128)(2,1)S(1)}, bf16[2,256,1024]{1,2,0:T(8,128)(2,1)S(1)}, u32[]{:S(2)}, u32[]{:S(2)}) collective-permute-start(bf16[2,256,1024]{1,2,0:T(8,128)(2,1)S(1)} %copy.197), channel_id=1, source_target_pairs={{28,0},{0,4},{4,8},{8,12},{12,16},{16,20},{20,24},{24,28},{29,1},{... | collective-permute-start | bytes 3145736 | tf_op jit(solution)/shard_map/while/body/eval_jaxpr/ppermute | solution.py:20
  685.9 43.3 %collective-permute-start.6 = (bf16[2,256,1024]{1,2,0:T(8,128)(2,1)}, bf16[2,256,1024]{1,2,0:T(8,128)(2,1)}, u32[]{:S(2)}, u32[]{:S(2)}) collective-permute-start(bf16[2,256,1024]{1,2,0:T(8,128)(2,1)} %copy.198), channel_id=1, source_target_pairs={{28,0},{0,4},{4,8},{8,12},{12,16},{16,20},{20,24},{24,28},{29,1},{... | collective-permute-start | bytes 3145736 | tf_op jit(solution)/shard_map/while/body/eval_jaxpr/ppermute | solution.py:20
  687.8 41.4 %collective-permute-start.7 = (bf16[2,256]{1,0:T(2,128)(2,1)S(1)}, bf16[2,256]{1,0:T(2,128)(2,1)S(1)}, u32[]{:S(2)}, u32[]{:S(2)}) collective-permute-start(bf16[2,256]{1,0:T(2,128)(2,1)S(1)} %copy.199), channel_id=1, source_target_pairs={{28,0},{0,4},{4,8},{8,12},{12,16},{16,20},{20,24},{24,28},{29,1},{... | collective-permute-start | bytes 3080 | tf_op jit(solution)/shard_map/while/body/eval_jaxpr/ppermute | solution.py:20
  752.4 43.3 %collective-permute-start.5 = (bf16[2,256,1024]{1,2,0:T(8,128)(2,1)S(1)}, bf16[2,256,1024]{1,2,0:T(8,128)(2,1)S(1)}, u32[]{:S(2)}, u32[]{:S(2)}) collective-permute-start(bf16[2,256,1024]{1,2,0:T(8,128)(2,1)S(1)} %copy.197), channel_id=1, source_target_pairs={{28,0},{0,4},{4,8},{8,12},{12,16},{16,20},{20,24},{24,28},{29,1},{... | collective-permute-start | bytes 3145736 | tf_op jit(solution)/shard_map/while/body/eval_jaxpr/ppermute | solution.py:20
  752.4 43.3 %collective-permute-start.6 = (bf16[2,256,1024]{1,2,0:T(8,128)(2,1)}, bf16[2,256,1024]{1,2,0:T(8,128)(2,1)}, u32[]{:S(2)}, u32[]{:S(2)}) collective-permute-start(bf16[2,256,1024]{1,2,0:T(8,128)(2,1)} %copy.198), channel_id=1, source_target_pairs={{28,0},{0,4},{4,8},{8,12},{12,16},{16,20},{20,24},{24,28},{29,1},{... | collective-permute-start | bytes 3145736 | tf_op jit(solution)/shard_map/while/body/eval_jaxpr/ppermute | solution.py:20
  754.3 41.4 %collective-permute-start.7 = (bf16[2,256]{1,0:T(2,128)(2,1)S(1)}, bf16[2,256]{1,0:T(2,128)(2,1)S(1)}, u32[]{:S(2)}, u32[]{:S(2)}) collective-permute-start(bf16[2,256]{1,0:T(2,128)(2,1)S(1)} %copy.199), channel_id=1, source_target_pairs={{28,0},{0,4},{4,8},{8,12},{12,16},{16,20},{20,24},{24,28},{29,1},{... | collective-permute-start | bytes 3080 | tf_op jit(solution)/shard_map/while/body/eval_jaxpr/ppermute | solution.py:20
  818.9 43.3 %collective-permute-start.5 = (bf16[2,256,1024]{1,2,0:T(8,128)(2,1)S(1)}, bf16[2,256,1024]{1,2,0:T(8,128)(2,1)S(1)}, u32[]{:S(2)}, u32[]{:S(2)}) collective-permute-start(bf16[2,256,1024]{1,2,0:T(8,128)(2,1)S(1)} %copy.197), channel_id=1, source_target_pairs={{28,0},{0,4},{4,8},{8,12},{12,16},{16,20},{20,24},{24,28},{29,1},{... | collective-permute-start | bytes 3145736 | tf_op jit(solution)/shard_map/while/body/eval_jaxpr/ppermute | solution.py:20
  818.9 43.3 %collective-permute-start.6 = (bf16[2,256,1024]{1,2,0:T(8,128)(2,1)}, bf16[2,256,1024]{1,2,0:T(8,128)(2,1)}, u32[]{:S(2)}, u32[]{:S(2)}) collective-permute-start(bf16[2,256,1024]{1,2,0:T(8,128)(2,1)} %copy.198), channel_id=1, source_target_pairs={{28,0},{0,4},{4,8},{8,12},{12,16},{16,20},{20,24},{24,28},{29,1},{... | collective-permute-start | bytes 3145736 | tf_op jit(solution)/shard_map/while/body/eval_jaxpr/ppermute | solution.py:20
  820.8 41.4 %collective-permute-start.7 = (bf16[2,256]{1,0:T(2,128)(2,1)S(1)}, bf16[2,256]{1,0:T(2,128)(2,1)S(1)}, u32[]{:S(2)}, u32[]{:S(2)}) collective-permute-start(bf16[2,256]{1,0:T(2,128)(2,1)S(1)} %copy.199), channel_id=1, source_target_pairs={{28,0},{0,4},{4,8},{8,12},{12,16},{16,20},{20,24},{24,28},{29,1},{... | collective-permute-start | bytes 3080 | tf_op jit(solution)/shard_map/while/body/eval_jaxpr/ppermute | solution.py:20
  885.4 43.3 %collective-permute-start.5 = (bf16[2,256,1024]{1,2,0:T(8,128)(2,1)S(1)}, bf16[2,256,1024]{1,2,0:T(8,128)(2,1)S(1)}, u32[]{:S(2)}, u32[]{:S(2)}) collective-permute-start(bf16[2,256,1024]{1,2,0:T(8,128)(2,1)S(1)} %copy.197), channel_id=1, source_target_pairs={{28,0},{0,4},{4,8},{8,12},{12,16},{16,20},{20,24},{24,28},{29,1},{... | collective-permute-start | bytes 3145736 | tf_op jit(solution)/shard_map/while/body/eval_jaxpr/ppermute | solution.py:20
  885.4 43.3 %collective-permute-start.6 = (bf16[2,256,1024]{1,2,0:T(8,128)(2,1)}, bf16[2,256,1024]{1,2,0:T(8,128)(2,1)}, u32[]{:S(2)}, u32[]{:S(2)}) collective-permute-start(bf16[2,256,1024]{1,2,0:T(8,128)(2,1)} %copy.198), channel_id=1, source_target_pairs={{28,0},{0,4},{4,8},{8,12},{12,16},{16,20},{20,24},{24,28},{29,1},{... | collective-permute-start | bytes 3145736 | tf_op jit(solution)/shard_map/while/body/eval_jaxpr/ppermute | solution.py:20
  887.3 41.4 %collective-permute-start.7 = (bf16[2,256]{1,0:T(2,128)(2,1)S(1)}, bf16[2,256]{1,0:T(2,128)(2,1)S(1)}, u32[]{:S(2)}, u32[]{:S(2)}) collective-permute-start(bf16[2,256]{1,0:T(2,128)(2,1)S(1)} %copy.199), channel_id=1, source_target_pairs={{28,0},{0,4},{4,8},{8,12},{12,16},{16,20},{20,24},{24,28},{29,1},{... | collective-permute-start | bytes 3080 | tf_op jit(solution)/shard_map/while/body/eval_jaxpr/ppermute | solution.py:20
  951.9 43.3 %collective-permute-start.5 = (bf16[2,256,1024]{1,2,0:T(8,128)(2,1)S(1)}, bf16[2,256,1024]{1,2,0:T(8,128)(2,1)S(1)}, u32[]{:S(2)}, u32[]{:S(2)}) collective-permute-start(bf16[2,256,1024]{1,2,0:T(8,128)(2,1)S(1)} %copy.197), channel_id=1, source_target_pairs={{28,0},{0,4},{4,8},{8,12},{12,16},{16,20},{20,24},{24,28},{29,1},{... | collective-permute-start | bytes 3145736 | tf_op jit(solution)/shard_map/while/body/eval_jaxpr/ppermute | solution.py:20
  951.9 43.3 %collective-permute-start.6 = (bf16[2,256,1024]{1,2,0:T(8,128)(2,1)}, bf16[2,256,1024]{1,2,0:T(8,128)(2,1)}, u32[]{:S(2)}, u32[]{:S(2)}) collective-permute-start(bf16[2,256,1024]{1,2,0:T(8,128)(2,1)} %copy.198), channel_id=1, source_target_pairs={{28,0},{0,4},{4,8},{8,12},{12,16},{16,20},{20,24},{24,28},{29,1},{... | collective-permute-start | bytes 3145736 | tf_op jit(solution)/shard_map/while/body/eval_jaxpr/ppermute | solution.py:20
  953.7 41.4 %collective-permute-start.7 = (bf16[2,256]{1,0:T(2,128)(2,1)S(1)}, bf16[2,256]{1,0:T(2,128)(2,1)S(1)}, u32[]{:S(2)}, u32[]{:S(2)}) collective-permute-start(bf16[2,256]{1,0:T(2,128)(2,1)S(1)} %copy.199), channel_id=1, source_target_pairs={{28,0},{0,4},{4,8},{8,12},{12,16},{16,20},{20,24},{24,28},{29,1},{... | collective-permute-start | bytes 3080 | tf_op jit(solution)/shard_map/while/body/eval_jaxpr/ppermute | solution.py:20
  1033.1 266.1 %reduce-scatter.23.cloned.1.call-start = ((), (), s32[]{:S(2)}) async-start(), calls=%async_computation.15 | async-start | bytes 540672
  1047.1 398.8 %reduce-scatter.13.cloned.1.call-start = ((), (), s32[]{:S(2)}) async-start(), calls=%async_computation.10 | async-start | bytes 4325376 | tf_op jit(solution)/shard_map/reduce_scatter | solution.py:302
  1052.0 554.8 %reduce-scatter.19.cloned.1.call-start = ((), (), s32[]{:S(2)}) async-start(), calls=%async_computation.13 | async-start | bytes 12976128
  1075.9 897.2 %reduce-scatter.15.cloned.1.call-start = ((), (), s32[]{:S(2)}) async-start(), calls=%async_computation.11 | async-start | bytes 17301504 | tf_op jit(solution)/shard_map/reduce_scatter | solution.py:303
  1088.3 1249.9 %reduce-scatter.17.cloned.1.call-start = ((), (), s32[]{:S(2)}) async-start(), calls=%async_computation.12 | async-start | bytes 17301504 | tf_op jit(solution)/shard_map/reduce_scatter | solution.py:304
  (129 other events, 2470.6 us)
Sparse Core Ops, SparseCore 0:
  10.9 72.3 all-gather.7
  86.2 55.0 all-gather.9
  144.2 76.2 all-gather.11
  223.3 90.0 all-gather.13
  1033.2 133.3 reduce-scatter.20
  1168.8 130.3 reduce-scatter.22
  1302.1 143.8 reduce-scatter.12
  1452.5 154.2 reduce-scatter.18
  1609.8 363.2 reduce-scatter.14
  1976.0 362.1 reduce-scatter.16
where the time goes:
time: 2360 us; the launch traced here: 2350 us
  waiting for transfers between devices  1560 us (66%)
  matrix products  295 us (12%)
  blocking collectives  238 us (10%)
  local copies, waits for them, and re-layouts  116 us (5%)
  other arithmetic  108 us (5%)
    reduce_scatter x1, waiting for transfers between devices, on_device(): lax.psum_scatter(grad_expand, ('blk', 'dp'), scatter_dimension=0, tiled=T...  366 us
    ppermute x58, waiting for transfers between devices, from_behind(): return lax.ppermute(block, axis, route)  365 us
    reduce_scatter x1, waiting for transfers between devices, on_device(): lax.psum_scatter(grad_reduce, ('blk', 'dp'), scatter_dimension=0, tiled=T...  365 us
    unnamed x13, waiting for transfers between devices  314 us
    reduce_scatter x1, waiting for transfers between devices, on_device(): lax.psum_scatter(grad_output, ('blk', 'dp'), scatter_dimension=0, tiled=T...  145 us
    all_gather x1, blocking collectives, on_device(): lax.all_gather(biases, ('blk', 'dp'), axis=1, tiled=True)  71.3 us
    all_gather x1, blocking collectives, on_device(): lax.all_gather(gains, ('blk', 'dp'), axis=1, tiled=True)  65.9 us
    all_gather x1, blocking collectives, on_device(): lax.all_gather(hidden_bias, ('blk', 'dp'), axis=0, tiled=True)  63.2 us
  transfers between devices with their start and end apart: 68, of which 35 were waited for; matrix products, arithmetic and copies ran while one was open for 14% of the time, Pallas kernels for 0%

commit v1 on v0

v1 whole, which is shorter than its diff:
```python
import functools

import jax
import jax.numpy as jnp
from jax import lax
from jax.experimental import pallas as pl
from jax.experimental.pallas import tpu as pltpu
from jax.sharding import PartitionSpec as P

HEADS = 16
EPSILON = 1e-12
FAR = 2.0**60
BOTH = ("blk", "dp")
MESH = pl.DeviceIdType.MESH
LOW = jnp.bfloat16
HIGH = jnp.float32
VMEM_LIMIT = 60 * 2**20


def product(left, right):
    return jnp.dot(left, right, preferred_element_type=HIGH)


def product_nt(left, right):
    return lax.dot_general(left, right, (((1,), (1,)), ((), ())), preferred_element_type=HIGH)


def product_tn(left, right):
    return lax.dot_general(left, right, (((0,), (0,)), ((), ())), preferred_element_type=HIGH)


class Sender:
    def __init__(self, send, recv):
        self.send, self.recv, self.started = send, recv, []

    def go(self, src, dst, device, landing):
        at = len(self.started)

        def copy(a, b):
            return pltpu.make_async_remote_copy(
                src_ref=a,
                dst_ref=b,
                send_sem=self.send.at[at],
                recv_sem=self.recv.at[at],
                device_id=device,
                device_id_type=MESH,
            )

        out = copy(src, dst)
        out.start()
        self.started.append(out)
        return copy(landing, landing)

    def drain(self):
        for out in self.started:
            out.wait_send()


def greet(peers):
    barrier = pltpu.get_barrier_semaphore()
    for peer in peers:
        pl.semaphore_signal(barrier, inc=1, device_id=peer, device_id_type=MESH)
    pl.semaphore_wait(barrier, len(peers))


def half(ref, which):
    rows = ref.shape[0]
    cut = rows // 32 * 16
    return ref.at[pl.ds(0, cut)] if which == 0 else ref.at[pl.ds(cut, rows - cut)]


def position():
    return lax.axis_index("blk"), lax.axis_index("dp")


def gather_kernel(x, win, w1, w2, X, W, W1, W2, send, recv, lsem):
    b, z = position()
    bx, by, bd, bc = b ^ 2, b ^ 4, b ^ 6, b ^ 1
    greet([(b ^ d, z) for d in range(1, 8)] + [(b, z ^ d) for d in range(1, 4)])
    s = Sender(send, recv)
    locs = []

    def local(src, dst):
        copy = pltpu.make_async_copy(src, dst, lsem.at[len(locs)])
        copy.start()
        locs.append(copy)

    local(win.at[b], W.at[z, b])
    local(x, X.at[b])
    local(w1, W1.at[b, z])
    local(w2, W2.at[b, z])
    to_x, to_y, to_core = (bx, z), (by, z), (bc, z)
    cores = []

    def core(src, full, bb, zz):
        cores.append(s.go(src, full.at[bb, zz], to_core, full.at[bb ^ 1, zz]))

    def along_z(src, full):
        return [s.go(src, full.at[b, z], (b, z ^ d), full.at[b, z ^ d]) for d in (1, 2, 3)]

    def first_hop(src, full, zz):
        return [
            s.go(src, full.at[b, zz], to_x, full.at[bx, zz]),
            s.go(src, full.at[b, zz], to_y, full.at[by, zz]),
        ]

    def second_hop(full, zz, arriving):
        arriving[0].wait_recv()
        piece = half(full.at[bx, zz], 0)
        one = s.go(piece, piece, to_y, half(full.at[bd, zz], 0))
        core(full.at[bx, zz], full, bx, zz)
        arriving[1].wait_recv()
        piece = half(full.at[by, zz], 1)
        two = s.go(piece, piece, to_x, half(full.at[bd, zz], 1))
        core(full.at[by, zz], full, by, zz)
        return [one, two]

    columns = [
        s.go(win.at[b ^ d], W.at[z, b], (b ^ d, z), W.at[z, b ^ d]) for d in range(1, 8)
    ]
    token_x = s.go(x, X.at[b], to_x, X.at[bx])
    token_y = s.go(x, X.at[b], to_y, X.at[by])
    z1, z2 = along_z(w1, W1), along_z(w2, W2)
    cores.append(s.go(x, X.at[b], to_core, X.at[bc]))
    core(w1, W1, b, z)
    core(w2, W2, b, z)
    hop1, hop2 = {0: first_hop(w1, W1, z)}, {0: first_hop(w2, W2, z)}
    for copy in columns:
        copy.wait_recv()
    locs[0].wait()
    columns = [s.go(W.at[z], W.at[z], (b, z ^ d), W.at[z ^ d]) for d in (1, 2, 3)]
    token_x.wait_recv()
    piece = half(X.at[bx], 0)
    token_one = s.go(piece, piece, to_y, half(X.at[bd], 0))
    cores.append(s.go(X.at[bx], X.at[bx], to_core, X.at[bx ^ 1]))
    token_y.wait_recv()
    piece = half(X.at[by], 1)
    token_two = s.go(piece, piece, to_x, half(X.at[bd], 1))
    cores.append(s.go(X.at[by], X.at[by], to_core, X.at[by ^ 1]))
    for i, d in enumerate((1, 2, 3)):
        for hop, arriving, full in ((hop1, z1, W1), (hop2, z2, W2)):
            arriving[i].wait_recv()
            hop[d] = first_hop(full.at[b, z ^ d], full, z ^ d)
            core(full.at[b, z ^ d], full, b, z ^ d)
    last1, last2 = {}, {}
    for d in range(4):
        for hop, last, full in ((hop1, last1, W1), (hop2, last2, W2)):
            last[d] = second_hop(full, z ^ d, hop[d])
        if d == 0:
            token_one.wait_recv()
            token_two.wait_recv()
            cores.append(s.go(X.at[bd], X.at[bd], to_core, X.at[bd ^ 1]))
    for d in range(4):
        for last, full in ((last1, W1), (last2, W2)):
            for copy in last[d]:
                copy.wait_recv()
            core(full.at[bd, z ^ d], full, bd, z ^ d)
    for copy in cores + columns:
        copy.wait_recv()
    s.drain()
    for copy in locs[1:]:
        copy.wait()


def in_hbm(count):
    return [pl.BlockSpec(memory_space=pl.ANY)] * count


def pair_of_semaphores(count):
    return [pltpu.SemaphoreType.DMA((count,)), pltpu.SemaphoreType.DMA((count,))]


def gather(x, win, w1, w2):
    shape = lambda *s: jax.ShapeDtypeStruct(s, LOW)
    return pl.pallas_call(
        gather_kernel,
        out_shape=(
            shape(8, *x.shape),
            shape(4, *win.shape),
            shape(8, 4, *w1.shape),
            shape(8, 4, *w2.shape),
        ),
        in_specs=in_hbm(4),
        out_specs=tuple(in_hbm(4)),
        scratch_shapes=pair_of_semaphores(100) + [pltpu.SemaphoreType.DMA((4,))],
        compiler_params=pltpu.CompilerParams(collective_id=1, has_side_effects=True),
        name="gather",
    )(x, win, w1, w2)


def add_rows(out, one, two):
    @pl.loop(0, one.shape[0] // 16)
    def _(i):
        rows = pl.ds(pl.multiple_of(i * 16, 16), 16)
        out[rows, :] = one[rows, :] + two[rows, :]


def reduce_kernel(g1, g2, o1, o2, *scratch):
    C, S, H, Q, Z = [scratch[2 * i : 2 * i + 2] for i in range(5)]
    send, recv, lsem = scratch[10:]
    G, O = (g1, g2), (o1, o2)
    b, z = position()
    greet([(b ^ d, z) for d in (1, 2, 4)] + [(b, z ^ d) for d in (1, 2, 3)])
    to_x, to_y, to_core = (b ^ 2, z), (b ^ 4, z), (b ^ 1, z)
    s = Sender(send, recv)
    own, other = {}, {}
    order = (1, 2, 3, 0)
    for d in order:
        for e in (3, 1, 2, 0):
            for a in (0, 1):
                at = (d * 4 + e) * 2 + a
                copy = pltpu.make_async_copy(G[a].at[b ^ (2 * e), z ^ d], S[a].at[e, d], lsem.at[at])
                copy.start()
                own[a, d, e] = copy
                other[a, d, e] = s.go(
                    G[a].at[b ^ 1 ^ (2 * e), z ^ d], C[a].at[e, d], to_core, C[a].at[e, d]
                )
    halves, pieces, last = {}, {}, {}

    def fold(d):
        for e in (3, 1, 2, 0):
            for a in (0, 1):
                own[a, d, e].wait()
                other[a, d, e].wait_recv()
                add_rows(S[a].at[e, d], S[a].at[e, d], C[a].at[e, d])
                if e == 3:
                    halves[a, d] = [
                        s.go(half(S[a].at[3, d], 0), H[a].at[d, 0], to_x, H[a].at[d, 0]),
                        s.go(half(S[a].at[3, d], 1), H[a].at[d, 1], to_y, H[a].at[d, 1]),
                    ]

    def relay(d):
        for a in (0, 1):
            halves[a, d][0].wait_recv()
            part = half(S[a].at[2, d], 0)
            add_rows(part, part, H[a].at[d, 0])
            one = s.go(S[a].at[2, d], Q[a].at[d, 1], to_y, Q[a].at[d, 1])
            halves[a, d][1].wait_recv()
            part = half(S[a].at[1, d], 1)
            add_rows(part, part, H[a].at[d, 1])
            two = s.go(S[a].at[1, d], Q[a].at[d, 0], to_x, Q[a].at[d, 0])
            pieces[a, d] = [one, two]

    def collect(d):
        for a in (0, 1):
            for copy in pieces[a, d]:
                copy.wait_recv()
            add_rows(S[a].at[0, d], S[a].at[0, d], Q[a].at[d, 0])
            add_rows(S[a].at[0, d], S[a].at[0, d], Q[a].at[d, 1])
            if d:
                last[a, d] = s.go(S[a].at[0, d], Z[a].at[d - 1], (b, z ^ d), Z[a].at[d - 1])

    fold(1)
    fold(2)
    relay(1)
    fold(3)
    relay(2)
    collect(1)
    fold(0)
    relay(3)
    collect(2)
    relay(0)
    collect(3)
    collect(0)
    for a in (0, 1):
        for d in (1, 2, 3):
            last[a, d].wait_recv()

        @pl.loop(0, O[a].shape[0] // 16)
        def _(i, a=a):
            rows = pl.ds(pl.multiple_of(i * 16, 16), 16)
            total = S[a][0, 0, rows, :].astype(HIGH)
            for d in range(3):
                total = total + Z[a][d, rows, :].astype(HIGH)
            O[a][rows, :] = total

    s.drain()


def reduce(g1, g2):
    shapes = [g1.shape[2:], g2.shape[2:]]
    scratch = []
    for lead, cut in (((4, 4), 1), ((4, 4), 1), ((4, 2), 2), ((4, 2), 1), ((3,), 1)):
        for rows, columns in shapes:
            scratch.append(pltpu.VMEM((*lead, rows // cut, columns), LOW))
    return pl.pallas_call(
        reduce_kernel,
        out_shape=tuple(jax.ShapeDtypeStruct(s, HIGH) for s in shapes),
        in_specs=in_hbm(2),
        out_specs=(pl.BlockSpec(memory_space=pltpu.VMEM),) * 2,
        scratch_shapes=scratch + pair_of_semaphores(80) + [pltpu.SemaphoreType.DMA((32,))],
        compiler_params=pltpu.CompilerParams(
            collective_id=2, has_side_effects=True, vmem_limit_bytes=VMEM_LIMIT
        ),
        name="reduce",
    )(g1, g2)


def first_lanes(shape):
    return lax.broadcasted_iota(jnp.int32, shape, len(shape) - 1) < 64


def marked(block, marks, head):
    mine = first_lanes(block.shape)
    return jnp.where(mine if head == 0 else jnp.logical_not(mine), block, marks)


def rows_of(ref, slot=0):
    block = ref[:, slot]
    return block.reshape(-1, block.shape[-1])


def attend_kernel(q_ref, qm_ref, k_ref, km_ref, v_ref, out_ref, lse_ref):
    queries, q_marks = q_ref[0, 0], qm_ref[0, 0]
    keys, k_marks, values = rows_of(k_ref), rows_of(km_ref), rows_of(v_ref)
    ones = jnp.ones_like(values)
    rows = queries.shape[0]
    outs, logs = [], []
    for head in (0, 1):
        scores = product_nt(marked(queries, q_marks, head), marked(keys, k_marks, head))
        top = jnp.max(scores, axis=-1, keepdims=True)
        weights = jnp.exp(scores - top).astype(LOW)
        total = product(weights, marked(values, ones, head))
        mass = pltpu.roll(total, 64, 1)
        outs.append(total / mass)
        logs.append(top + jnp.log(mass))
    out_ref[0, 0] = jnp.where(first_lanes((rows, 128)), outs[0], outs[1]).astype(LOW)
    both = jnp.where(first_lanes((rows, 128)), logs[0], logs[1])
    flipped = both.T
    lse_ref[0, 0] = jnp.concatenate(
        [flipped[0:1], flipped[64:65], jnp.zeros((6, rows), HIGH)], axis=0
    )


def attend(q, qm, k, km, v):
    blocks, slots, rows, lanes = q.shape
    tile = pl.BlockSpec((1, 1, rows, lanes), lambda s, i: (i, s, 0, 0))
    whole = pl.BlockSpec((blocks, 1, rows, lanes), lambda s, i: (0, s, 0, 0))
    return pl.pallas_call(
        attend_kernel,
        grid=(slots, blocks),
        out_shape=(
            jax.ShapeDtypeStruct(q.shape, LOW),
            jax.ShapeDtypeStruct((slots, blocks, 8, rows), HIGH),
        ),
        in_specs=[tile, tile, whole, whole, whole],
        out_specs=(tile, pl.BlockSpec((1, 1, 8, rows), lambda s, i: (s, i, 0, 0))),
        compiler_params=pltpu.CompilerParams(vmem_limit_bytes=VMEM_LIMIT),
        name="attend",
    )(q, qm, k, km, v)


def attend_back_kernel(
    q_ref, qm_ref, o_ref, g_ref, lse_ref, k_ref, km_ref, v_ref, dq_ref, dk_ref, dv_ref, acc, delta
):
    tile = pl.program_id(1)
    blocks, _, rows, _ = q_ref.shape
    keys, k_marks, values = k_ref[0, 0], km_ref[0, 0], v_ref[0, 0]
    mine = first_lanes((rows, 128))

    @pl.when(tile == 0)
    def _():
        acc[...] = jnp.zeros_like(acc)
        pick = (lax.broadcasted_iota(jnp.int32, (8, 128), 0) == 0) == first_lanes((8, 128))
        pick = pick.astype(HIGH)
        for i in range(blocks):
            inner = o_ref[i, 0].astype(HIGH) * g_ref[i, 0].astype(HIGH)
            delta[i] = lax.dot_general(
                pick,
                inner,
                (((1,), (1,)), ((), ())),
                precision=lax.Precision.HIGHEST,
                preferred_element_type=HIGH,
            )

    zeros = jnp.zeros((rows, 128), LOW)
    key_heads = [marked(keys, k_marks, head) for head in (0, 1)]

    def step(i, carry):
        dk, dv = carry
        queries, q_marks, grads = q_ref[i, 0], qm_ref[i, 0], g_ref[i, 0]
        dk_parts, dq_parts = [], []
        for head in (0, 1):
            query = marked(queries, q_marks, head)
            grad = marked(grads, zeros, head)
            scores = product_nt(key_heads[head], query)
            probs = jnp.exp(scores - lse_ref[0, i, head : head + 1, :])
            pushed = product_nt(values, grad)
            d_scores = (probs * (pushed - delta[i, head : head + 1, :])).astype(LOW)
            dv = dv + product(probs.astype(LOW), grad)
            dk_parts.append(product(d_scores, query))
            dq_parts.append(product_tn(d_scores, keys))
        acc[i] += jnp.where(mine, dq_parts[0], dq_parts[1])
        return dk + jnp.where(mine, dk_parts[0], dk_parts[1]), dv

    start = jnp.zeros((rows, 128), HIGH)
    dk, dv = lax.fori_loop(0, blocks, step, (start, start))
    dk_ref[0, 0] = dk.astype(LOW)
    dv_ref[0, 0] = dv.astype(LOW)

    @pl.when(tile == blocks - 1)
    def _():
        for i in range(blocks):
            dq_ref[i, 0] = (acc[i] * 0.125).astype(LOW)


def attend_back(q, qm, o, g, lse, k, km, v):
    blocks, slots, rows, lanes = q.shape
    tile = pl.BlockSpec((1, 1, rows, lanes), lambda s, i: (i, s, 0, 0))
    whole = pl.BlockSpec((blocks, 1, rows, lanes), lambda s, i: (0, s, 0, 0))
    logs = pl.BlockSpec((1, blocks, 8, rows), lambda s, i: (s, 0, 0, 0))
    shape = jax.ShapeDtypeStruct(q.shape, LOW)
    return pl.pallas_call(
        attend_back_kernel,
        grid=(slots, blocks),
        out_shape=(shape,) * 3,
        in_specs=[whole, whole, whole, whole, logs, tile, tile, tile],
        out_specs=(whole, tile, tile),
        scratch_shapes=[pltpu.VMEM((blocks, rows, lanes), HIGH), pltpu.VMEM((blocks, 8, rows), HIGH)],
        compiler_params=pltpu.CompilerParams(vmem_limit_bytes=VMEM_LIMIT),
        name="attend_back",
    )(q, qm, o, g, lse, k, km, v)


def by_position(rows, cols):
    return lax.broadcasted_iota(jnp.int32, (1, cols), 1) % 64


def normalize(values):
    mean = jnp.mean(values, axis=-1, keepdims=True)
    centred = values - mean
    spread = jnp.mean(centred * centred, axis=-1, keepdims=True)
    inverse = lax.rsqrt(spread + EPSILON)
    return centred * inverse, inverse


def normalize_back(grad, normal, inverse):
    return inverse * (
        grad
        - jnp.mean(grad, axis=-1, keepdims=True)
        - normal * jnp.mean(grad * normal, axis=-1, keepdims=True)
    )


def swap(pieces):
    return lax.all_to_all(pieces, "blk", 0, 0)


def gelu_parts(pre):
    phi_sum = 0.5 * lax.erfc(-pre * (0.5**0.5))
    density = jnp.exp(-0.5 * pre * pre) * 0.3989422804014327
    return pre * phi_sum, phi_sum + pre * density


def on_device(
    tokens,
    input_weight,
    output_weight,
    expand_weight,
    reduce_weight,
    gains,
    biases,
    hidden_bias,
    segment,
    present,
    cotangent,
):
    slots, rows, width = tokens.shape
    n_blk, n_dp = lax.axis_size("blk"), lax.axis_size("dp")
    shards = n_blk * n_dp
    fast = (n_blk, n_dp) == (8, 4)
    held = width // n_blk
    shard = input_weight.shape[0]
    hidden = expand_weight.shape[1]
    count = slots * rows
    flat = tokens.reshape(count, width)

    code = segment + 4 * (1 - present)
    code_rows = jnp.zeros((16, width), LOW).at[0, :count].set(code.reshape(count).astype(LOW))
    sent_tokens = jnp.concatenate([flat, code_rows], axis=0)
    columns = input_weight.reshape(shard, 3, n_blk, held).transpose(2, 0, 1, 3)
    columns = columns.reshape(n_blk, shard, 3 * held)
    small = jnp.concatenate([gains.reshape(-1), biases.reshape(-1), hidden_bias])
    both = jnp.concatenate([expand_weight, output_weight], axis=1)
    if fast:
        small = jnp.concatenate([small[None], jnp.zeros((15, small.shape[0]), LOW)], axis=0)
        small = jnp.broadcast_to(small, (n_blk, *small.shape))
        X, W, W1, W2 = gather(
            sent_tokens, jnp.concatenate([columns, small], axis=1), both, reduce_weight
        )
        W = W.transpose(1, 0, 2, 3).reshape(shards, -1, 3 * held)
        small = W[:, shard]
        W = W[:, :shard].reshape(width, 3 * held)
        W1, W2 = W1.reshape(width, -1), W2.reshape(hidden, width)
    else:
        X = lax.all_gather(sent_tokens, "blk")
        W = lax.all_gather(swap(columns), "dp", axis=1).reshape(width, 3 * held)
        small = lax.all_gather(small, BOTH)
        W1 = lax.all_gather(both, BOTH, axis=0, tiled=True)
        W2 = lax.all_gather(reduce_weight, BOTH, axis=0, tiled=True)
    expand, out_w = W1[:, :hidden], W1[:, hidden:]
    part = width // shards
    cuts = small[:, : 8 * part].reshape(shards, 8, part).transpose(1, 0, 2).reshape(8, width)
    cuts = cuts.astype(HIGH)
    gain, bias = cuts[:2], cuts[2:]
    hidden_full = small[:, 8 * part :].reshape(hidden).astype(HIGH)

    codes = X[:, count, :count].reshape(n_blk, slots, rows, 1).astype(jnp.int32)
    lanes = lax.broadcasted_iota(jnp.int32, (1, 1, 1, 128), 3) % 64
    q_marks = jnp.where((lanes < 5) & (lanes != codes % 4), -FAR, 0.0).astype(LOW)
    k_marks = jnp.where(lanes == jnp.minimum(codes, 4), 1.0, 0.0).astype(LOW)

    all_tokens = X[:, :count]
    me = lax.axis_index("blk")
    mixed = jnp.einsum("brd,dc->brc", all_tokens, W, preferred_element_type=HIGH)
    own_bias = lax.dynamic_slice(bias[:2], (0, me * held), (2, held))
    q = (mixed[..., :held] + own_bias[0]).astype(LOW) * LOW(0.125)
    k = mixed[..., held : 2 * held].astype(LOW)
    v = (mixed[..., 2 * held :] + own_bias[1]).astype(LOW)

    def heads(block):
        block = block.reshape(n_blk, slots, rows, held)
        return jnp.pad(block, ((0, 0),) * 3 + ((0, 128 - held),))

    q, k, v = heads(q), heads(k), heads(v)
    att, lse = attend(q, q_marks, k, k_marks, v)
    rows_att = swap(att[..., :held].reshape(n_blk, count, held))
    attended = rows_att.transpose(1, 0, 2).reshape(count, width)

    branch = product(attended, out_w) + bias[2]
    n1, r1 = normalize(flat.astype(HIGH) + branch)
    normed = n1 * gain[0] + bias[3]
    normed_low = normed.astype(LOW)
    pre = product(normed_low, expand) + hidden_full
    act, slope = gelu_parts(pre)
    act = act.astype(LOW)
    ffn = product(act, W2) + bias[4]
    n2, r2 = normalize(normed + ffn)
    output = (n2 * gain[1] + bias[5]).astype(LOW).reshape(slots, rows, width)

    cot = cotangent.reshape(count, width).astype(HIGH)
    d_second = normalize_back(cot * gain[1], n2, r2)
    d_ffn = d_second.astype(LOW)
    grad_reduce = product_tn(act, d_ffn).astype(LOW)
    d_pre = (product_nt(d_ffn, W2) * slope).astype(LOW)
    grad_expand = product_tn(normed_low, d_pre).astype(LOW)
    d_normed = d_second + product_nt(d_pre, expand)
    d_first = normalize_back(d_normed * gain[0], n1, r1)
    d_branch = d_first.astype(LOW)
    grad_output = product_tn(attended, d_branch).astype(LOW)
    d_att = product_nt(d_branch, out_w).astype(LOW)

    g = swap(d_att.reshape(count, n_blk, held).transpose(1, 0, 2))
    grad_both = jnp.concatenate([grad_expand, grad_output], axis=1)
    if fast:
        sum_both, sum_reduce = reduce(
            grad_both.reshape(n_blk, n_dp, shard, -1), grad_reduce.reshape(n_blk, n_dp, -1, width)
        )
    else:
        sum_both = lax.psum_scatter(grad_both, BOTH, scatter_dimension=0, tiled=True).astype(HIGH)
        sum_reduce = lax.psum_scatter(grad_reduce, BOTH, scatter_dimension=0, tiled=True)
        sum_reduce = sum_reduce.astype(HIGH)

    dq, dk, dv = attend_back(q, q_marks, att, heads(g), lse, k, k_marks, v)
    d_mixed = jnp.concatenate([dq[..., :held], dk[..., :held], dv[..., :held]], axis=-1)
    d_mixed = d_mixed.reshape(n_blk * count, 3 * held)
    d_input = product_tn(all_tokens.reshape(n_blk * count, width), d_mixed).astype(LOW)
    d_tokens = product_nt(d_mixed, W).astype(LOW)
    d_tokens = lax.psum_scatter(d_tokens, "blk", scatter_dimension=0, tiled=True)
    grad_tokens = (d_first + d_tokens.astype(HIGH)).reshape(slots, rows, width)
    d_input = swap(d_input.reshape(n_blk, n_dp * shard, 3 * held))
    d_input = d_input.reshape(n_blk, n_dp, shard, 3, held).transpose(1, 2, 3, 0, 4)
    d_input = d_input.reshape(n_dp, shard, 3 * width).astype(HIGH)
    grad_input = lax.psum_scatter(d_input, "dp", scatter_dimension=0, tiled=False)

    col = lambda a: jnp.sum(a.astype(HIGH), axis=0)
    own_cols = jnp.stack([col(d_mixed[:, :held]), col(d_mixed[:, 2 * held :])])
    own_cols = lax.psum_scatter(own_cols, "dp", scatter_dimension=1, tiled=True)
    small_rows = jnp.stack(
        [
            col(d_normed * n1),
            col(cot * n2),
            col(d_branch),
            col(d_normed),
            col(d_ffn),
            col(cot),
        ]
    )
    small_rows = small_rows.reshape(6, shards, part).transpose(1, 0, 2).reshape(shards, 6 * part)
    small_rows = jnp.concatenate([small_rows, col(d_pre).reshape(shards, -1)], axis=1)
    small_sum = lax.psum_scatter(small_rows, BOTH, scatter_dimension=0, tiled=False)
    vectors = small_sum[: 6 * part].reshape(6, part)
    return (
        output,
        grad_tokens,
        grad_input,
        sum_both[:, hidden:],
        sum_both[:, :hidden],
        sum_reduce,
        vectors[:2],
        jnp.concatenate([own_cols, vectors[2:]], axis=0),
        small_sum[6 * part :],
    )


def solution(mesh):
    rows, sharded = P("dp", "blk", None), P(BOTH, None)
    in_specs = (rows, sharded, sharded, sharded, sharded, P(None, BOTH), P(None, BOTH), P(BOTH))
    in_specs += (P("dp", "blk"), P("dp", "blk"), rows)
    out_specs = (rows, rows, sharded, sharded, sharded, sharded)
    out_specs += (P(None, BOTH), P(None, BOTH), P(BOTH))
    return jax.shard_map(
        on_device, mesh=mesh, in_specs=in_specs, out_specs=out_specs, check_vma=False
    )
```

time: 2360 us -> 664 us (0.28)
  waiting for transfers between devices: 1560 us -> 14.5 us
  Pallas kernels: 0 us -> 380 us
  matrix products: 295 us -> 105 us
  blocking collectives: 238 us -> 69.5 us
  local copies, waits for them, and re-layouts: 116 us -> 31.5 us
  other arithmetic: 108 us -> 34.4 us
    reduce_scatter x3 -> x2, waiting for transfers between devices: 877 us -> 0.01 us  [the longest x1 0.01 us: on_device(): lax.psum_scatter(d_input, 'dp', scatter_dimension=0, tiled=False)]
    pallas_call x0 -> x4, Pallas kernels: none -> 380 us  [the longest x1 125 us: gather(): pl.pallas_call(gather_kernel, out_shape=(shape(8, *x.shape), shape(4, *wi...]
    ppermute x58 -> x0, waiting for transfers between devices: 365 us -> none  [from_behind(): return lax.ppermute(block, axis, route)]
    unnamed x13 -> x4, waiting for transfers between devices: 314 us -> 0.05 us
    all_gather x3 -> x0, blocking collectives: 200 us -> none  [the longest x1 71.3 us: on_device(): lax.all_gather(biases, ('blk', 'dp'), axis=1, tiled=True)]
    dot_general x68 -> x12, matrix products: 295 us -> 105 us  [the longest x3 35.2 us: product(): return jnp.dot(left, right, preferred_element_type=HIGH)]
    convert_element_type x52 -> x5, other arithmetic: 82.4 us -> 4.79 us  [the longest x1 2.6 us: on_device(): k_marks = jnp.where(lanes == jnp.minimum(codes, 4), 1.0, 0.0).astype(LOW)]
    while x149 -> x0, local copies, waits for them, and re-layouts: 62.3 us -> none
  transfers between devices with their start and end apart: 68 -> 5, of which waited for: 35 -> 2; matrix products, arithmetic and copies ran while one was open for 14% -> 11% of each run, Pallas kernels for 0% -> 18%
where the time goes in v1:
time: 664 us; the launch traced here: 656 us
  Pallas kernels  380 us (57%)
  matrix products  105 us (16%)
  blocking collectives  69.5 us (10%)
  other arithmetic  34.4 us (5%)
  local copies, waits for them, and re-layouts  31.5 us (5%)
  between operations  14.7 us (2%)
  waiting for transfers between devices  14.5 us (2%)
  starting transfers between devices  7.24 us (1%)
    pallas_call x1, Pallas kernels, gather(): pl.pallas_call(gather_kernel, out_shape=(shape(8, *x.shape), shape(4, *wi...  125 us
    pallas_call x1, Pallas kernels, reduce(): pl.pallas_call(reduce_kernel, out_shape=tuple((jax.ShapeDtypeStruct(s, HI...  116 us
    pallas_call x1, Pallas kernels, attend_back(): pl.pallas_call(attend_back_kernel, grid=(slots, blocks), out_shape=(shape...  107 us
    unnamed x1, blocking collectives  51 us
    dot_general x3, matrix products, product(): return jnp.dot(left, right, preferred_element_type=HIGH)  35.2 us
    dot_general x4, matrix products, product_nt(): lax.dot_general(left, right, (((1,), (1,)), ((), ())), preferred_element_...  34.3 us
    pallas_call x1, Pallas kernels, attend(): pl.pallas_call(attend_kernel, grid=(slots, blocks), out_shape=(jax.ShapeD...  31.8 us
    dot_general x4, matrix products, product_tn(): lax.dot_general(left, right, (((0,), (0,)), ((), ())), preferred_element_...  28.3 us
  transfers between devices with their start and end apart: 5, of which 2 were waited for; matrix products, arithmetic and copies ran while one was open for 11% of the time, Pallas kernels for 18%

profile of v1, /device:TPU:0, one launch (start us, length us, event | category | flops | bytes accessed | tf_op | source)
XLA Modules:
  0.0 656.4 jit_solution(10527363539604391393)
XLA Ops:
  13.9 2.3 fusion.44.x
  16.2 124.7 %gather.1 = (bf16[8,528,1024]{2,1,0:T(8,128)(2,1)}, bf16[4,8,48,384]{3,2,1,0:T(8,128)(2,1)}, bf16[8,4,32,5120]{3,2,1,0:T(8,128)(2,1)}, bf16[8,4,128,1024]{3,2,1,0:T(8,128)(2,1)}) custom-call(bf16[528,1024]{1,0:T(8,128)(2,1)} %fusion.44.x, bf16[8,48,384]{2,1,0:T(8,128)(2,1)} %pad_maximum_fusion.3.win, bf16[32,5120]{1,0:T(8,128)(2,1)} %pad_maximum_fusion.2.w1, ...), custom_call_target="tpu_custom_call" | custom-call | tf_op jit(solution)/shard_map/gather/pallas_call | solution.py:175
  143.8 6.9 %fusion.55 = f32[8,512,384]{2,1,0:T(8,128)S(1)} fusion(bf16[1024,384,1]{1,0,2:T(8,128)(2,1)S(1)} %bitcast.125, bf16[8,528,1024]{2,1,0:T(8,128)(2,1)} %get-tuple-element.32), kind=kOutput, calls=%fused_computation.130 | convolution fusion | flops 3221225472 | bytes 15466496 | tf_op jit(solution)/shard_map/brd,dc->brc/dot_general | solution.py:515
  153.7 2.6 select_convert_fusion
  156.3 31.8 %attend.1 = (bf16[8,2,256,128]{3,2,1,0:T(8,128)(2,1)}, f32[2,8,8,256]{3,2,1,0:T(8,128)}) custom-call(bf16[8,2,256,128]{3,2,1,0:T(8,128)(2,1)} %bitcast.103, bf16[8,2,256,128]{3,2,1,0:T(8,128)(2,1)} %get-tuple-element.75.qm_ref, bf16[8,2,256,128]{3,2,1,0:T(8,128)(2,1)} %bitcast.101, bf16[8,2,256,128]{3,2,1,0:T(8,128)(2,1)} %get-tuple-element.74.km_ref, ...), custom_call_target="tpu_custom_call" | custom-call | tf_op jit(solution)/shard_map/attend/pallas_call | solution.py:339
  188.1 2.3 copy.41
  190.4 3.6 all-to-all-start
  195.3 14.0 %all-to-all-done = bf16[8,512,128]{1,2,0:T(8,128)(2,1)S(1)} async-done(((bf16[8,512,128]{1,2,0:T(8,128)(2,1)}), bf16[8,512,128]{1,2,0:T(8,128)(2,1)S(1)}, u32[]{:S(2)}, u32[]{:S(2)}) %all-to-all-start) | async-done | bytes 1048608 | tf_op jit(solution)/shard_map/all_to_all | solution.py:446
  209.3 3.4 fusion.60
  213.1 27.0 %multiply_convert_fusion = (bf16[512,4096]{1,0:T(8,128)(2,1)S(1)}, f32[512,4096]{1,0:T(8,128)}, f32[512,4096]{1,0:T(8,128)}) fusion(f32[4096]{0:T(1024)S(1)} %fusion.47, bf16[1024,5120]{1,0:T(8,128)(2,1)} %bitcast.142, f32[512,1024]{1,0:T(8,128)S(1)} %get-tuple-element.77, f32[1024]{0:T(1024)S(1)} %add.163, f32[1024]{0:T(1024)S(1)} %mul.158, ...), kind=kOutput, calls=%fused_computation.12 | convolution fusion | flops 4436000768 | bytes 31485952 | tf_op jit(solution)/shard_map/dot_general | solution.py:21
  240.1 4.8 fusion.61
  246.1 1.9 convert_reduce_fusion.4
  248.0 12.8 %convert_reduce_fusion = (f32[4096]{0:T(1024)S(1)}, bf16[512,4096]{1,0:T(8,128)(2,1)S(1)}) fusion(f32[512,4096]{1,0:T(8,128)} %get-tuple-element.64, f32[512,4096]{1,0:T(8,128)} %get-tuple-element.78, f32[4096]{0:T(1024)S(1)} %fusion.47, bf16[4096,1024]{1,0:T(8,128)(2,1)} %bitcast.145, f32[512,1024]{1,0:T(8,128)S(1)} %get-tuple-element.60), kind=kOutput, calls=%fused_computation.11 | convolution fusion | flops 4316459008 | bytes 31490048 | tf_op jit(solution)/shard_map/dot_general | solution.py:25
  260.9 9.7 %multiply_reduce_fusion = (f32[1024]{0:T(1024)S(1)}, f32[512]{0:T(512)S(1)}, f32[512]{0:T(512)S(1)}, f32[1024]{0:T(1024)S(1)}, f32[512,1024]{1,0:T(8,128)S(1)}) fusion(f32[512,1024]{1,0:T(8,128)S(1)} %get-tuple-element.77, f32[512]{0:T(512)S(1)} %add_rsqrt_fusion.1, f32[512]{0:T(512)S(1)} %broadcast_multiply_fusion.4, f32[1024]{0:T(1024)S(1)} %mul.158, ...), kind=kOutput, calls=%fused_computation.57 | convolution fusion | flops 4300207104 | bytes 18894848 | tf_op jit(solution)/shard_map/dot_general | solution.py:25
  271.2 3.7 fusion.41
  275.1 18.5 %all_to_all.15 = bf16[8,512,128]{2,1,0:T(8,128)(2,1)} all-to-all(bf16[8,512,128]{2,1,0:T(8,128)(2,1)S(1)} %bitcast.113), channel_id=1, replica_groups=mesh['blk'=8,'dp'=4] {'blk'}, dimensions={0} | all-to-all | bytes 2097152 | tf_op jit(solution)/shard_map/all_to_all | solution.py:446
  293.6 107.4 %attend_back.1 = (bf16[8,2,256,128]{3,2,1,0:T(8,128)(2,1)}, bf16[8,2,256,128]{3,2,1,0:T(8,128)(2,1)}, bf16[8,2,256,128]{3,2,1,0:T(8,128)(2,1)}) custom-call(bf16[8,2,256,128]{3,2,1,0:T(8,128)(2,1)} %bitcast.104, bf16[8,2,256,128]{3,2,1,0:T(8,128)(2,1)} %get-tuple-element.75.qm_ref, bf16[8,2,256,128]{3,2,1,0:T(8,128)(2,1)} %get-tuple-element.34.o_ref, ...), custom_call_target="tpu_custom_call" | custom-call | tf_op jit(solution)/shard_map/attend_back/pallas_call | solution.py:413
  401.0 2.3 pad_maximum_fusion.1
  404.8 8.2 %convolution_convert_fusion.2 = bf16[4096,1024]{1,0:T(8,128)(2,1)} fusion(bf16[4096,384]{1,0:T(8,128)(2,1)S(1)} %bitcast.106, bf16[1024,384]{1,0:T(8,128)(2,1)} %bitcast.126), kind=kOutput, calls=%fused_computation.29 | convolution fusion | flops 3225419776 | bytes 12320768 | tf_op jit(solution)/shard_map/dot_general | solution.py:25
  412.9 7.6 %slice.131 = bf16[8,512,1024]{2,1,0:T(8,128)(2,1)} slice(bf16[8,528,1024]{2,1,0:T(8,128)(2,1)} %get-tuple-element.32), slice={[0:8], [0:512], [0:1024]} | slice | bytes 16777216 | tf_op jit(solution)/shard_map/slice | solution.py:513
  420.7 8.0 %convolution_convert_fusion.4 = bf16[1024,384]{1,0:T(8,128)(2,1)} fusion(bf16[4096,1024]{1,0:T(8,128)(2,1)} %bitcast.109, bf16[4096,384]{1,0:T(8,128)(2,1)S(1)} %bitcast.107), kind=kOutput, calls=%fused_computation.80 | convolution fusion | flops 3221618688 | bytes 12320768 | tf_op jit(solution)/shard_map/dot_general | solution.py:29
  428.6 3.6 all-to-all-start.2
  432.2 12.1 %convolution_convert_fusion.1 = bf16[1024,4096]{1,0:T(8,128)(2,1)} fusion(bf16[512,4096]{1,0:T(8,128)(2,1)} %copy-done.11, f32[512,1024]{1,0:T(8,128)} %copy-done.3, f32[1024]{0:T(1024)S(1)} %add.163, f32[1024]{0:T(1024)S(1)} %mul.158, f32[512]{0:T(512)S(1)} %add_rsqrt_fusion.1, f32[512]{0:T(512)S(1)} %broadcast_multiply_fusion.4), kind=kOutput, calls=%fused_computation.28 | convolution fusion | flops 4301783040 | bytes 14692352 | tf_op jit(solution)/shard_map/dot_general | solution.py:29
  444.7 1.9 reshape.316
  446.6 3.8 copy.43
  450.4 2.6 reshape.314
  454.3 10.6 %pad_maximum_fusion = bf16[1024,5120]{1,0:T(8,128)(2,1)} fusion(bf16[1024,1024]{1,0:T(8,128)(2,1)S(1)} %convolution_convert_fusion.3, bf16[1024,4096]{1,0:T(8,128)(2,1)} %convolution_convert_fusion.1), kind=kLoop, calls=%fused_computation.2 | loop fusion | flops 20971520 | bytes 20971520 | tf_op jit(solution)/shard_map/concatenate | solution.py:554
  464.9 7.0 %convolution_convert_fusion = bf16[4096,1024]{1,0:T(8,128)(2,1)} fusion(bf16[512,4096]{1,0:T(8,128)(2,1)S(1)} %copy-done.13, f32[512,1024]{1,0:T(8,128)S(1)} %copy-done.5), kind=kOutput, calls=%fused_computation.27 | convolution fusion | flops 4299685888 | bytes 14680064 | tf_op jit(solution)/shard_map/dot_general | solution.py:29
  471.9 115.9 %reduce.39 = (f32[32,5120]{1,0:T(8,128)}, f32[128,1024]{1,0:T(8,128)}) custom-call(bf16[8,4,32,5120]{3,2,1,0:T(8,128)(2,1)} %bitcast.98, bf16[8,4,128,1024]{3,2,1,0:T(8,128)(2,1)} %bitcast.110), custom_call_target="tpu_custom_call" | custom-call | tf_op jit(solution)/shard_map/reduce/pallas_call | solution.py:286
  589.4 1.9 slice.153
  592.1 51.0 %all-reduce.2 = f32[32,320]{1,0:T(8,128)S(1)} all-reduce(f32[32,320]{1,0:T(8,128)S(1)} %pad_maximum_fusion.4), channel_id=4, replica_groups=mesh['blk'=8,'dp'=4] {'blk','dp'}, use_global_device_ids=true, to_apply=%region_17.18.clone | all-reduce | flops 10240 | bytes 81920
  645.8 2.8 convert_add_fusion
  (117 shorter events, 25.3 us)
Async XLA Ops:
  142.4 8.3 %copy-start.9 = (bf16[32,32,384]{2,1,0:T(8,128)(2,1)}, bf16[32,32,384]{2,1,0:T(8,128)(2,1)S(1)}, u32[]{:S(2)}) copy-start(bf16[32,32,384]{2,1,0:T(8,128)(2,1)S(1)} %slice.162) | copy-start | bytes 2359300
  156.3 38.4 %copy-start = (bf16[2,256,1024]{2,1,0:T(8,128)(2,1)S(1)}, bf16[2,256,1024]{2,1,0:T(8,128)(2,1)}, u32[]{:S(2)}) copy-start(bf16[2,256,1024]{2,1,0:T(8,128)(2,1)} %param.23) | copy-start | bytes 3145732
  156.3 53.0 %copy-start.6 = (bf16[2,256,1024]{2,1,0:T(8,128)(2,1)S(1)}, bf16[2,256,1024]{2,1,0:T(8,128)(2,1)}, u32[]{:S(2)}) copy-start(bf16[2,256,1024]{2,1,0:T(8,128)(2,1)} %param.13) | copy-start | bytes 3145732
  190.4 18.9 %all-to-all-start = ((bf16[8,512,128]{1,2,0:T(8,128)(2,1)}), bf16[8,512,128]{1,2,0:T(8,128)(2,1)S(1)}, u32[]{:S(2)}, u32[]{:S(2)}) async-start(bf16[8,512,128]{1,2,0:T(8,128)(2,1)} %copy.41), calls=%async_computation | async-start | bytes 2097152 | tf_op jit(solution)/shard_map/all_to_all | solution.py:446
  194.0 450.5 %reduce-scatter.10.cloned.1.call-start = ((), (), s32[]{:S(2)}) async-start(), calls=%async_computation.8 | async-start | bytes 81920
  209.3 3.4 copy-start.7
  209.3 30.8 %slice-start = ((s8[8388608]{0:T(1024)(128)(4,1)}), s8[4194304]{0:T(1024)(128)(4,1)S(1)}, s32[]{:S(2)}) async-start(s8[8388608]{0:T(1024)(128)(4,1)} %bitcast.146), calls=%async_computation.9 | async-start | bytes 8388608
  212.7 57.8 %copy-start.3 = (f32[512,1024]{1,0:T(8,128)}, f32[512,1024]{1,0:T(8,128)S(1)}, u32[]{:S(2)}) copy-start(f32[512,1024]{1,0:T(8,128)S(1)} %get-tuple-element.77) | copy-start | bytes 6291460
  213.1 27.0 %slice-start.1 = ((s8[8388608]{0:T(1024)(128)(4,1)}), s8[4194304]{0:T(1024)(128)(4,1)S(1)}, s32[]{:S(2)}) async-start(s8[8388608]{0:T(1024)(128)(4,1)} %bitcast.146), calls=%async_computation.10 | async-start | bytes 8388608
  240.1 4.8 copy-start.12
  248.0 12.9 %copy-start.4 = (f32[512,1024]{1,0:T(8,128)}, f32[512,1024]{1,0:T(8,128)S(1)}, u32[]{:S(2)}) copy-start(f32[512,1024]{1,0:T(8,128)S(1)} %get-tuple-element.60) | copy-start | bytes 6291460
  260.8 9.7 %copy-start.11 = (bf16[512,4096]{1,0:T(8,128)(2,1)}, bf16[512,4096]{1,0:T(8,128)(2,1)S(1)}, u32[]{:S(2)}) copy-start(bf16[512,4096]{1,0:T(8,128)(2,1)S(1)} %get-tuple-element.83) | copy-start | bytes 12582916
  271.2 3.9 copy-start.1
  404.7 241.1 %reduce-scatter.6.cloned.1.call-start = ((), (), s32[]{:S(2)}) async-start(), calls=%async_computation.6 | async-start | bytes 9437184 | tf_op jit(solution)/shard_map/reduce_scatter | solution.py:569
  428.6 16.1 %all-to-all-start.2 = ((bf16[8,128,384]{2,1,0:T(8,128)(2,1)}), bf16[8,128,384]{2,1,0:T(8,128)(2,1)S(1)}, u32[]{:S(2)}, u32[]{:S(2)}) async-start(bf16[8,128,384]{2,1,0:T(8,128)(2,1)} %bitcast.127), calls=%async_computation.3 | async-start | bytes 1572864 | tf_op jit(solution)/shard_map/all_to_all | solution.py:446
  432.2 216.5 %reduce-scatter.8.cloned.1.call-start = ((), (), s32[]{:S(2)}) async-start(), calls=%async_computation.7 | async-start | bytes 1966080 | tf_op jit(solution)/shard_map/reduce_scatter | solution.py:574
  446.6 6.4 copy-start.2
  446.6 6.4 copy-start.8
  454.3 10.6 %copy-start.5 = (f32[512,1024]{1,0:T(8,128)S(1)}, f32[512,1024]{1,0:T(8,128)}, u32[]{:S(2)}) copy-start(f32[512,1024]{1,0:T(8,128)} %copy-done.4) | copy-start | bytes 6291460
  454.3 10.6 %copy-start.13 = (bf16[512,4096]{1,0:T(8,128)(2,1)S(1)}, bf16[512,4096]{1,0:T(8,128)(2,1)}, u32[]{:S(2)}) copy-start(bf16[512,4096]{1,0:T(8,128)(2,1)} %copy-done.12) | copy-start | bytes 12582916
  587.8 60.9 %copy-start.10 = (f32[128,1024]{1,0:T(8,128)S(1)}, f32[128,1024]{1,0:T(8,128)}, u32[]{:S(2)}) copy-start(f32[128,1024]{1,0:T(8,128)} %get-tuple-element.100) | copy-start | bytes 1572868
Sparse Core Ops, SparseCore 0:
  404.8 16.8 reduce-scatter.9
  425.5 80.9 reduce-scatter.5
  509.4 57.9 reduce-scatter.7

commit v2 on v1

--- a/solution.py
+++ b/solution.py
@@ -327,7 +327,7 @@
     out_ref[0, 0] = jnp.where(first_lanes((rows, 128)), outs[0], outs[1]).astype(LOW)
     both = jnp.where(first_lanes((rows, 128)), logs[0], logs[1])
     flipped = both.T
-    lse_ref[0, 0] = jnp.concatenate(
+    lse_ref[0] = jnp.concatenate(
         [flipped[0:1], flipped[64:65], jnp.zeros((6, rows), HIGH)], axis=0
     )
 
@@ -341,10 +341,10 @@
         grid=(slots, blocks),
         out_shape=(
             jax.ShapeDtypeStruct(q.shape, LOW),
-            jax.ShapeDtypeStruct((slots, blocks, 8, rows), HIGH),
+            jax.ShapeDtypeStruct((slots, 8, blocks * rows), HIGH),
         ),
         in_specs=[tile, tile, whole, whole, whole],
-        out_specs=(tile, pl.BlockSpec((1, 1, 8, rows), lambda s, i: (s, i, 0, 0))),
+        out_specs=(tile, pl.BlockSpec((1, 8, rows), lambda s, i: (s, 0, i))),
         compiler_params=pltpu.CompilerParams(vmem_limit_bytes=VMEM_LIMIT),
         name="attend",
     )(q, qm, k, km, v)
@@ -355,60 +355,48 @@
 ):
     tile = pl.program_id(1)
     blocks, _, rows, _ = q_ref.shape
+    count = blocks * rows
+    queries, q_marks, grads = rows_of(q_ref), rows_of(qm_ref), rows_of(g_ref)
     keys, k_marks, values = k_ref[0, 0], km_ref[0, 0], v_ref[0, 0]
-    mine = first_lanes((rows, 128))
 
     @pl.when(tile == 0)
     def _():
         acc[...] = jnp.zeros_like(acc)
         pick = (lax.broadcasted_iota(jnp.int32, (8, 128), 0) == 0) == first_lanes((8, 128))
-        pick = pick.astype(HIGH)
-        for i in range(blocks):
-            inner = o_ref[i, 0].astype(HIGH) * g_ref[i, 0].astype(HIGH)
-            delta[i] = lax.dot_general(
-                pick,
-                inner,
-                (((1,), (1,)), ((), ())),
-                precision=lax.Precision.HIGHEST,
-                preferred_element_type=HIGH,
-            )
-
-    zeros = jnp.zeros((rows, 128), LOW)
-    key_heads = [marked(keys, k_marks, head) for head in (0, 1)]
-
-    def step(i, carry):
-        dk, dv = carry
-        queries, q_marks, grads = q_ref[i, 0], qm_ref[i, 0], g_ref[i, 0]
-        dk_parts, dq_parts = [], []
-        for head in (0, 1):
-            query = marked(queries, q_marks, head)
-            grad = marked(grads, zeros, head)
-            scores = product_nt(key_heads[head], query)
-            probs = jnp.exp(scores - lse_ref[0, i, head : head + 1, :])
-            pushed = product_nt(values, grad)
-            d_scores = (probs * (pushed - delta[i, head : head + 1, :])).astype(LOW)
-            dv = dv + product(probs.astype(LOW), grad)
-            dk_parts.append(product(d_scores, query))
-            dq_parts.append(product_tn(d_scores, keys))
-        acc[i] += jnp.where(mine, dq_parts[0], dq_parts[1])
-        return dk + jnp.where(mine, dk_parts[0], dk_parts[1]), dv
-
-    start = jnp.zeros((rows, 128), HIGH)
-    dk, dv = lax.fori_loop(0, blocks, step, (start, start))
-    dk_ref[0, 0] = dk.astype(LOW)
+        inner = rows_of(o_ref).astype(HIGH) * grads.astype(HIGH)
+        delta[...] = lax.dot_general(
+            pick.astype(HIGH),
+            inner,
+            (((1,), (1,)), ((), ())),
+            precision=lax.Precision.HIGHEST,
+            preferred_element_type=HIGH,
+        )
+
+    zeros = jnp.zeros((count, 128), LOW)
+    keys_t = keys.T
+    dk, dv = [], 0.0
+    for head in (0, 1):
+        query, grad = marked(queries, q_marks, head), marked(grads, zeros, head)
+        probs = jnp.exp(product_nt(marked(keys, k_marks, head), query) - lse_ref[0, head : head + 1])
+        pushed = product_nt(values, grad)
+        d_scores = (probs * (pushed - delta[head : head + 1])).astype(LOW)
+        dv = dv + product(probs.astype(LOW), grad)
+        dk.append(product(d_scores, query))
+        lanes = pl.ds(head * 64, 64)
+        acc[lanes, :] += product(keys_t[head * 64 : head * 64 + 64], d_scores)
+    dk_ref[0, 0] = jnp.where(first_lanes((rows, 128)), dk[0], dk[1]).astype(LOW)
     dv_ref[0, 0] = dv.astype(LOW)
 
     @pl.when(tile == blocks - 1)
     def _():
-        for i in range(blocks):
-            dq_ref[i, 0] = (acc[i] * 0.125).astype(LOW)
+        dq_ref[:, 0] = (acc[...].T * 0.125).astype(LOW).reshape(blocks, rows, 128)
 
 
 def attend_back(q, qm, o, g, lse, k, km, v):
     blocks, slots, rows, lanes = q.shape
     tile = pl.BlockSpec((1, 1, rows, lanes), lambda s, i: (i, s, 0, 0))
     whole = pl.BlockSpec((blocks, 1, rows, lanes), lambda s, i: (0, s, 0, 0))
-    logs = pl.BlockSpec((1, blocks, 8, rows), lambda s, i: (s, 0, 0, 0))
+    logs = pl.BlockSpec((1, 8, blocks * rows), lambda s, i: (s, 0, 0))
     shape = jax.ShapeDtypeStruct(q.shape, LOW)
     return pl.pallas_call(
         attend_back_kernel,
@@ -416,14 +404,10 @@
         out_shape=(shape,) * 3,
         in_specs=[whole, whole, whole, whole, logs, tile, tile, tile],
         out_specs=(whole, tile, tile),
-        scratch_shapes=[pltpu.VMEM((blocks, rows, lanes), HIGH), pltpu.VMEM((blocks, 8, rows), HIGH)],
+        scratch_shapes=[pltpu.VMEM((lanes, blocks * rows), HIGH), pltpu.VMEM((8, blocks * rows), HIGH)],
         compiler_params=pltpu.CompilerParams(vmem_limit_bytes=VMEM_LIMIT),
         name="attend_back",
     )(q, qm, o, g, lse, k, km, v)
-
-
-def by_position(rows, cols):
-    return lax.broadcasted_iota(jnp.int32, (1, cols), 1) % 64
 
 
 def normalize(values):
@@ -442,14 +426,343 @@
     )
 
 
+def gelu_parts(u):
+    bell = jnp.exp(-0.5 * u * u)
+    t = 1.0 / (1.0 + (0.3275911 * 0.5**0.5) * jnp.abs(u))
+    poly = 1.061405429 * t - 1.453152027
+    poly = poly * t + 1.421413741
+    poly = poly * t - 0.284496736
+    poly = poly * t + 0.254829592
+    tail = 0.5 * poly * t * bell
+    below = jnp.where(u < 0.0, tail, 1.0 - tail)
+    return u * below, below + u * bell * 0.3989422804014327
+
+
+def column_sum(block):
+    return jnp.sum(block.astype(HIGH), axis=0, keepdims=True)
+
+
+def middle_kernel(
+    chunk,
+    tok_ref,
+    att_ref,
+    cot_ref,
+    par_ref,
+    hid_ref,
+    w1_hbm,
+    w2_hbm,
+    out_ref,
+    first_ref,
+    d_att_ref,
+    sums_ref,
+    d_hid_ref,
+    g1_hbm,
+    g2_hbm,
+    w1,
+    w2,
+    att,
+    normed_low,
+    n1,
+    n2,
+    act,
+    slope,
+    acc,
+    low,
+    wsem,
+    gsem,
+):
+    hidden, width = w2.shape
+    steps = hidden // chunk
+    pieces, _, held = att_ref.shape
+
+    def columns(c):
+        return pl.ds(pl.multiple_of(c * chunk, chunk), chunk)
+
+    def load1(c):
+        return pltpu.make_async_copy(w1_hbm.at[:, columns(c)], w1.at[:, columns(c)], wsem.at[0, c])
+
+    def load2(c):
+        return pltpu.make_async_copy(w2_hbm.at[columns(c)], w2.at[columns(c)], wsem.at[1, c])
+
+    last = pl.ds(hidden, width)
+    load_out = pltpu.make_async_copy(w1_hbm.at[:, last], w1.at[:, last], wsem.at[0, steps])
+    load_out.start()
+    for c in range(steps):
+        load1(c).start()
+        load2(c).start()
+    gain1, gain2 = par_ref[0:1], par_ref[1:2]
+    bias = lambda i: par_ref[2 + i : 3 + i]
+    for i in range(pieces):
+        att[:, i * held : (i + 1) * held] = att_ref[i]
+    load_out.wait()
+    first_sum = tok_ref[...].astype(HIGH) + product(att[...], w1[:, hidden:]) + bias(2)
+    normal, inverse1 = normalize(first_sum)
+    n1[...] = normal
+    normed = normal * gain1 + bias(3)
+    normed_low[...] = normed.astype(LOW)
+    acc[...] = normed + bias(4)
+
+    @pl.loop(0, steps)
+    def _(c):
+        load1(c).wait()
+        pre = product(normed_low[...], w1[:, columns(c)]) + hid_ref[:, columns(c)]
+        value, rate = gelu_parts(pre)
+        act[:, columns(c)] = value.astype(LOW)
+        slope[:, columns(c)] = rate.astype(LOW)
+        load2(c).wait()
+        acc[...] += product(value.astype(LOW), w2[columns(c), :])
+
+    normal, inverse2 = normalize(acc[...])
+    n2[...] = normal
+    out_ref[...] = (normal * gain2 + bias(5)).astype(LOW)
+    cot = cot_ref[...].astype(HIGH)
+    d_second = normalize_back(cot * gain2, normal, inverse2)
+    low[...] = d_second.astype(LOW)
+    acc[...] = d_second
+    sums_ref[1:2] = column_sum(cot * normal)
+    sums_ref[4:5] = column_sum(low[...])
+    sums_ref[5:6] = column_sum(cot)
+
+    def store1(c):
+        return pltpu.make_async_copy(w1.at[:, columns(c)], g1_hbm.at[:, columns(c)], gsem.at[0, c])
+
+    def store2(c):
+        return pltpu.make_async_copy(w2.at[columns(c)], g2_hbm.at[columns(c)], gsem.at[1, c])
+
+    @pl.loop(0, steps)
+    def _(c):
+        d_act = product_nt(low[...], w2[columns(c), :])
+        d_pre = (d_act * slope[:, columns(c)].astype(HIGH)).astype(LOW)
+        d_hid_ref[:, columns(c)] = column_sum(d_pre)
+        acc[...] += product_nt(d_pre, w1[:, columns(c)])
+        w2[columns(c), :] = product_tn(act[:, columns(c)], low[...]).astype(LOW)
+        store2(c).start()
+        w1[:, columns(c)] = product_tn(normed_low[...], d_pre).astype(LOW)
+        store1(c).start()
+
+    d_normed = acc[...]
+    normal = n1[...]
+    d_first = normalize_back(d_normed * gain1, normal, inverse1)
+    first_ref[...] = d_first
+    low[...] = d_first.astype(LOW)
+    sums_ref[0:1] = column_sum(d_normed * normal)
+    sums_ref[2:3] = column_sum(low[...])
+    sums_ref[3:4] = column_sum(d_normed)
+    d_att = product_nt(low[...], w1[:, hidden:]).astype(LOW)
+    for i in range(pieces):
+        d_att_ref[i] = d_att[:, i * held : (i + 1) * held]
+    w1[:, hidden:] = product_tn(att[...], low[...]).astype(LOW)
+    store_out = pltpu.make_async_copy(w1.at[:, last], g1_hbm.at[:, last], gsem.at[0, steps])
+    store_out.start()
+    for c in range(steps):
+        store1(c).wait()
+        store2(c).wait()
+    store_out.wait()
+
+
+def middle(tokens, att, cot, par, hid, w1, w2):
+    count, width = tokens.shape
+    hidden = w2.shape[0]
+    pieces = att.shape[0]
+    chunk = 512
+    shape = jax.ShapeDtypeStruct
+    vmem = pl.BlockSpec(memory_space=pltpu.VMEM)
+    return pl.pallas_call(
+        functools.partial(middle_kernel, chunk),
+        out_shape=(
+            shape((count, width), LOW),
+            shape((count, width), HIGH),
+            shape(att.shape, LOW),
+            shape((8, width), HIGH),
+            shape((1, hidden), HIGH),
+            shape(w1.shape, LOW),
+            shape(w2.shape, LOW),
+        ),
+        in_specs=[vmem] * 5 + in_hbm(2),
+        out_specs=(vmem,) * 5 + tuple(in_hbm(2)),
+        scratch_shapes=[
+            pltpu.VMEM(w1.shape, LOW),
+            pltpu.VMEM(w2.shape, LOW),
+            pltpu.VMEM((count, width), LOW),
+            pltpu.VMEM((count, width), LOW),
+            pltpu.VMEM((count, width), HIGH),
+            pltpu.VMEM((count, width), HIGH),
+            pltpu.VMEM((count, hidden), LOW),
+            pltpu.VMEM((count, hidden), LOW),
+            pltpu.VMEM((count, width), HIGH),
+            pltpu.VMEM((count, width), LOW),
+            pltpu.SemaphoreType.DMA((2, hidden // chunk + 1)),
+            pltpu.SemaphoreType.DMA((2, hidden // chunk + 1)),
+        ],
+        compiler_params=pltpu.CompilerParams(vmem_limit_bytes=VMEM_LIMIT),
+        name="middle",
+    )(tokens, att, cot, par, hid, w1, w2)
+
+
+def finish_kernel(
+    dq,
+    dk,
+    dv,
+    w,
+    d_first,
+    small,
+    x_hbm,
+    tok_out,
+    in_out,
+    small_out,
+    x,
+    sent,
+    C,
+    S,
+    A,
+    H,
+    Q,
+    D,
+    R,
+    Z,
+    M,
+    N,
+    T,
+    send,
+    recv,
+    lsem,
+):
+    b, z = position()
+    count, width = d_first.shape
+    blocks = dq.shape[0]
+    to_x, to_y, to_core = (b ^ 2, z), (b ^ 4, z), (b ^ 1, z)
+    loads = []
+    for i in range(blocks):
+        load = pltpu.make_async_copy(x_hbm.at[i, pl.ds(0, count)], x.at[i], lsem.at[i])
+        load.start()
+        loads.append(load)
+    greet([(b ^ d, z) for d in range(1, 8)] + [(b, z ^ d) for d in (1, 2, 3)])
+    s = Sender(send, recv)
+    small_in = [
+        s.go(small.at[b ^ d], M.at[d - 1], (b ^ d, z), M.at[d - 1]) for d in range(1, 8)
+    ]
+
+    def mixed(i):
+        return jnp.concatenate([ref[i].reshape(count, -1) for ref in (dq, dk, dv)], axis=-1)
+
+    def piece(i):
+        return product_nt(mixed(i), w[...])
+
+    other = {}
+    for e in (3, 1, 2, 0):
+        sent[e] = piece(b ^ 1 ^ (2 * e)).astype(LOW)
+        other[e] = s.go(sent.at[e], C.at[e], to_core, C.at[e])
+
+    def own(e):
+        mine = piece(b ^ (2 * e))
+        other[e].wait_recv()
+        return mine + C[e].astype(HIGH)
+
+    S[3] = own(3).astype(LOW)
+    halves = [
+        s.go(half(S.at[3], 0), H.at[0], to_x, H.at[0]),
+        s.go(half(S.at[3], 1), H.at[1], to_y, H.at[1]),
+    ]
+    S[2] = own(2).astype(LOW)
+    pieces = [s.go(half(S.at[2], 1), half(Q.at[1], 1), to_y, half(Q.at[1], 1))]
+    S[1] = own(1).astype(LOW)
+    pieces.append(s.go(half(S.at[1], 0), half(Q.at[0], 0), to_x, half(Q.at[0], 0)))
+    A[...] = own(0) + d_first[...]
+
+    total = jnp.zeros((width, w.shape[1]), HIGH)
+    for i in range(blocks):
+        loads[i].wait()
+        total = total + product_tn(x[i], mixed(i))
+    D[...] = total.astype(LOW).reshape(D.shape)
+    grads_in = [
+        s.go(D.at[b ^ d], R.at[b], (b ^ d, z), R.at[b ^ d]) for d in range(1, 8)
+    ]
+    R[b] = D[b]
+
+    halves[0].wait_recv()
+    part = half(S.at[2], 0)
+    part[...] = part[...] + H[0]
+    pieces.append(s.go(part, half(Q.at[1], 0), to_y, half(Q.at[1], 0)))
+    halves[1].wait_recv()
+    part = half(S.at[1], 1)
+    part[...] = part[...] + H[1]
+    pieces.append(s.go(part, half(Q.at[0], 1), to_x, half(Q.at[0], 1)))
+
+    N[...] = small[b]
+    for i in range(7):
+        small_in[i].wait_recv()
+        N[...] += M[i]
+    for row, ref in ((4, dq), (5, dv)):
+        sums = jnp.zeros((1, 128), HIGH)
+        for i in range(blocks):
+            sums = sums + column_sum(ref[i].reshape(count, -1))
+        N[row : row + 1, 0:128] = sums
+    small_z = [s.go(N, T.at[d - 1], (b, z ^ d), T.at[d - 1]) for d in (1, 2, 3)]
+
+    for copy in grads_in:
+        copy.wait_recv()
+    rows = R.shape[1] // 4
+
+    def share(d):
+        return R.at[:, pl.ds(pl.multiple_of((z ^ d) * rows, rows), rows)]
+
+    in_z = [s.go(share(d), Z.at[d - 1], (b, z ^ d), Z.at[d - 1]) for d in (1, 2, 3)]
+    for copy in small_z:
+        copy.wait_recv()
+    small_out[...] = ((N[...] + T[0]) + T[1]) + T[2]
+    for copy in in_z:
+        copy.wait_recv()
+    in_out[...] = ((share(0)[...].astype(HIGH) + Z[0].astype(HIGH)) + Z[1].astype(HIGH)) + Z[
+        2
+    ].astype(HIGH)
+    for copy in pieces:
+        copy.wait_recv()
+    tok_out[...] = A[...] + Q[0].astype(HIGH) + Q[1].astype(HIGH)
+    s.drain()
+
+
+def finish(dq, dk, dv, w, d_first, small, x):
+    count, width = d_first.shape
+    blocks, columns = dq.shape[0], w.shape[1]
+    share = width // (4 * blocks)
+    vmem = pl.BlockSpec(memory_space=pltpu.VMEM)
+    shape = jax.ShapeDtypeStruct
+    low = lambda *s: pltpu.VMEM(s, LOW)
+    return pl.pallas_call(
+        finish_kernel,
+        out_shape=(
+            shape((count, width), HIGH),
+            shape((blocks, share, columns), HIGH),
+            shape(small.shape[1:], HIGH),
+        ),
+        in_specs=[vmem] * 6 + in_hbm(1),
+        out_specs=(vmem,) * 3,
+        scratch_shapes=[
+            low(blocks, count, width),
+            low(4, count, width),
+            low(4, count, width),
+            low(4, count, width),
+            pltpu.VMEM((count, width), HIGH),
+            low(2, count // 2, width),
+            low(2, count, width),
+            low(blocks, 4 * share, columns),
+            low(blocks, 4 * share, columns),
+            low(3, blocks, share, columns),
+            pltpu.VMEM((7, *small.shape[1:]), HIGH),
+            pltpu.VMEM(small.shape[1:], HIGH),
+            pltpu.VMEM((3, *small.shape[1:]), HIGH),
+        ]
+        + pair_of_semaphores(32)
+        + [pltpu.SemaphoreType.DMA((blocks,))],
+        compiler_params=pltpu.CompilerParams(
+            collective_id=3, has_side_effects=True, vmem_limit_bytes=VMEM_LIMIT
+        ),
+        name="finish",
+    )(dq, dk, dv, w, d_first, small, x)
+
+
 def swap(pieces):
     return lax.all_to_all(pieces, "blk", 0, 0)
-
-
-def gelu_parts(pre):
-    phi_sum = 0.5 * lax.erfc(-pre * (0.5**0.5))
-    density = jnp.exp(-0.5 * pre * pre) * 0.3989422804014327
-    return pre * phi_sum, phi_sum + pre * density
 
 
 def on_device(
@@ -498,7 +811,6 @@
         small = lax.all_gather(small, BOTH)
         W1 = lax.all_gather(both, BOTH, axis=0, tiled=True)
         W2 = lax.all_gather(reduce_weight, BOTH, axis=0, tiled=True)
-    expand, out_w = W1[:, :hidden], W1[:, hidden:]
     part = width // shards
     cuts = small[:, : 8 * part].reshape(shards, 8, part).transpose(1, 0, 2).reshape(8, width)
     cuts = cuts.astype(HIGH)
@@ -525,33 +837,18 @@
     q, k, v = heads(q), heads(k), heads(v)
     att, lse = attend(q, q_marks, k, k_marks, v)
     rows_att = swap(att[..., :held].reshape(n_blk, count, held))
-    attended = rows_att.transpose(1, 0, 2).reshape(count, width)
-
-    branch = product(attended, out_w) + bias[2]
-    n1, r1 = normalize(flat.astype(HIGH) + branch)
-    normed = n1 * gain[0] + bias[3]
-    normed_low = normed.astype(LOW)
-    pre = product(normed_low, expand) + hidden_full
-    act, slope = gelu_parts(pre)
-    act = act.astype(LOW)
-    ffn = product(act, W2) + bias[4]
-    n2, r2 = normalize(normed + ffn)
-    output = (n2 * gain[1] + bias[5]).astype(LOW).reshape(slots, rows, width)
-
-    cot = cotangent.reshape(count, width).astype(HIGH)
-    d_second = normalize_back(cot * gain[1], n2, r2)
-    d_ffn = d_second.astype(LOW)
-    grad_reduce = product_tn(act, d_ffn).astype(LOW)
-    d_pre = (product_nt(d_ffn, W2) * slope).astype(LOW)
-    grad_expand = product_tn(normed_low, d_pre).astype(LOW)
-    d_normed = d_second + product_nt(d_pre, expand)
-    d_first = normalize_back(d_normed * gain[0], n1, r1)
-    d_branch = d_first.astype(LOW)
-    grad_output = product_tn(attended, d_branch).astype(LOW)
-    d_att = product_nt(d_branch, out_w).astype(LOW)
-
-    g = swap(d_att.reshape(count, n_blk, held).transpose(1, 0, 2))
-    grad_both = jnp.concatenate([grad_expand, grad_output], axis=1)
+    middle_out = middle(
+        flat,
+        rows_att,
+        cotangent.reshape(count, width),
+        cuts,
+        hidden_full[None],
+        W1,
+        W2,
+    )
+    output, d_first, d_att, sums, d_hidden, grad_both, grad_reduce = middle_out
+    output = output.reshape(slots, rows, width)
+    g = swap(d_att)
     if fast:
         sum_both, sum_reduce = reduce(
             grad_both.reshape(n_blk, n_dp, shard, -1), grad_reduce.reshape(n_blk, n_dp, -1, width)
@@ -562,37 +859,37 @@
         sum_reduce = sum_reduce.astype(HIGH)
 
     dq, dk, dv = attend_back(q, q_marks, att, heads(g), lse, k, k_marks, v)
-    d_mixed = jnp.concatenate([dq[..., :held], dk[..., :held], dv[..., :held]], axis=-1)
-    d_mixed = d_mixed.reshape(n_blk * count, 3 * held)
-    d_input = product_tn(all_tokens.reshape(n_blk * count, width), d_mixed).astype(LOW)
-    d_tokens = product_nt(d_mixed, W).astype(LOW)
-    d_tokens = lax.psum_scatter(d_tokens, "blk", scatter_dimension=0, tiled=True)
-    grad_tokens = (d_first + d_tokens.astype(HIGH)).reshape(slots, rows, width)
-    d_input = swap(d_input.reshape(n_blk, n_dp * shard, 3 * held))
-    d_input = d_input.reshape(n_blk, n_dp, shard, 3, held).transpose(1, 2, 3, 0, 4)
-    d_input = d_input.reshape(n_dp, shard, 3 * width).astype(HIGH)
-    grad_input = lax.psum_scatter(d_input, "dp", scatter_dimension=0, tiled=False)
-
-    col = lambda a: jnp.sum(a.astype(HIGH), axis=0)
-    own_cols = jnp.stack([col(d_mixed[:, :held]), col(d_mixed[:, 2 * held :])])
-    own_cols = lax.psum_scatter(own_cols, "dp", scatter_dimension=1, tiled=True)
-    small_rows = jnp.stack(
-        [
-            col(d_normed * n1),
-            col(cot * n2),
-            col(d_branch),
-            col(d_normed),
-            col(d_ffn),
-            col(cot),
-        ]
-    )
-    small_rows = small_rows.reshape(6, shards, part).transpose(1, 0, 2).reshape(shards, 6 * part)
-    small_rows = jnp.concatenate([small_rows, col(d_pre).reshape(shards, -1)], axis=1)
-    small_sum = lax.psum_scatter(small_rows, BOTH, scatter_dimension=0, tiled=False)
+    small_rows = sums[:6].reshape(6, shards, part).transpose(1, 0, 2).reshape(shards, 6 * part)
+    small_rows = jnp.concatenate([small_rows, d_hidden.reshape(shards, -1)], axis=1)
+    if fast:
+        lanes = small_rows.shape[1]
+        small_rows = small_rows.reshape(n_blk, n_dp, lanes)
+        small_rows = jnp.pad(small_rows, ((0, 0), (0, 4), (0, 3 * held - lanes)))
+        grad_tokens, d_input, small_sum = finish(dq, dk, dv, W, d_first, small_rows, X)
+        grad_input = d_input.reshape(n_blk, shard, 3, held).transpose(1, 2, 0, 3)
+        grad_input = grad_input.reshape(shard, 3 * width)
+        me_dp = lax.axis_index("dp")
+        own_cols = lax.dynamic_slice(small_sum, (4, me_dp * part), (2, part))
+        small_sum = lax.dynamic_slice(small_sum, (me_dp, 0), (1, lanes))[0]
+    else:
+        d_mixed = jnp.concatenate([dq[..., :held], dk[..., :held], dv[..., :held]], axis=-1)
+        d_mixed = d_mixed.reshape(n_blk * count, 3 * held)
+        d_input = product_tn(all_tokens.reshape(n_blk * count, width), d_mixed).astype(LOW)
+        d_tokens = product_nt(d_mixed, W).astype(LOW)
+        d_tokens = lax.psum_scatter(d_tokens, "blk", scatter_dimension=0, tiled=True)
+        grad_tokens = d_first + d_tokens.astype(HIGH)
+        d_input = swap(d_input.reshape(n_blk, n_dp * shard, 3 * held))
+        d_input = d_input.reshape(n_blk, n_dp, shard, 3, held).transpose(1, 2, 3, 0, 4)
+        d_input = d_input.reshape(n_dp, shard, 3 * width).astype(HIGH)
+        grad_input = lax.psum_scatter(d_input, "dp", scatter_dimension=0, tiled=False)
+        col = lambda a: jnp.sum(a.astype(HIGH), axis=0)
+        own_cols = jnp.stack([col(d_mixed[:, :held]), col(d_mixed[:, 2 * held :])])
+        own_cols = lax.psum_scatter(own_cols, "dp", scatter_dimension=1, tiled=True)
+        small_sum = lax.psum_scatter(small_rows, BOTH, scatter_dimension=0, tiled=False)
     vectors = small_sum[: 6 * part].reshape(6, part)
     return (
         output,
-        grad_tokens,
+        grad_tokens.reshape(slots, rows, width),
         grad_input,
         sum_both[:, hidden:],
         sum_both[:, :hidden],

time: 664 us -> 494 us (0.74)
  matrix products: 105 us -> 6.95 us
  blocking collectives: 69.5 us -> 0 us
  Pallas kernels: 380 us -> 430 us
  other arithmetic: 34.4 us -> 13.7 us
  between operations: 14.7 us -> 0.93 us
  local copies, waits for them, and re-layouts: 31.5 us -> 19 us
    pallas_call x0 -> x2, Pallas kernels: none -> 123 us  [the longest x1 71 us: finish(): pl.pallas_call(finish_kernel, out_shape=(shape((count, width), HIGH), sha...]
    dot_general x11 -> x0, matrix products: 97.8 us -> none  [the longest x3 35.2 us: product(): return jnp.dot(left, right, preferred_element_type=HIGH)]
    pallas_call x1, Pallas kernels: 107 us -> 54.2 us  [attend_back(): pl.pallas_call(attend_back_kernel, grid=(slots, blocks), out_shape=(shape...]
    unnamed x1 -> x0, blocking collectives: 51 us -> none
    pallas_call x1, Pallas kernels: 116 us -> 96.6 us  [reduce(): pl.pallas_call(reduce_kernel, out_shape=tuple((jax.ShapeDtypeStruct(s, HI...]
    all_to_all x1 -> x0, blocking collectives: 18.5 us -> none  [swap(): return lax.all_to_all(pieces, 'blk', 0, 0)]
    concatenate x3 -> x1, other arithmetic: 13 us -> 0.73 us  [on_device(): jnp.concatenate([small_rows, d_hidden.reshape(shards, -1)], axis=1)]
    convert_element_type x3 -> x0, local copies, waits for them, and re-layouts: 8.25 us -> none  [on_device(): d_input = d_input.reshape(n_dp, shard, 3 * width).astype(HIGH)]
  transfers between devices with their start and end apart: 5 -> 2, of which waited for: 2 -> 1; matrix products, arithmetic and copies ran while one was open for 11% -> 1% of each run, Pallas kernels for 18% -> 20%
where the time goes in v2:
time: 494 us; the launch traced here: 492 us
  Pallas kernels  430 us (87%)
  local copies, waits for them, and re-layouts  19 us (4%)
  waiting for transfers between devices  13.8 us (3%)
  other arithmetic  13.7 us (3%)
  starting transfers between devices  7.53 us (2%)
  matrix products  6.95 us (1%)
    pallas_call x1, Pallas kernels, gather(): pl.pallas_call(gather_kernel, out_shape=(shape(8, *x.shape), shape(4, *wi...  125 us
    pallas_call x1, Pallas kernels, reduce(): pl.pallas_call(reduce_kernel, out_shape=tuple((jax.ShapeDtypeStruct(s, HI...  96.6 us
    pallas_call x1, Pallas kernels, finish(): pl.pallas_call(finish_kernel, out_shape=(shape((count, width), HIGH), sha...  71 us
    pallas_call x1, Pallas kernels, attend_back(): pl.pallas_call(attend_back_kernel, grid=(slots, blocks), out_shape=(shape...  54.2 us
    pallas_call x1, Pallas kernels, middle(): pl.pallas_call(functools.partial(middle_kernel, chunk), out_shape=(shape(...  51.7 us
    pallas_call x1, Pallas kernels, attend(): pl.pallas_call(attend_kernel, grid=(slots, blocks), out_shape=(jax.ShapeD...  31.7 us
    all_to_all x2, waiting for transfers between devices, swap(): return lax.all_to_all(pieces, 'blk', 0, 0)  13.8 us
  transfers between devices with their start and end apart: 2, of which 1 were waited for; matrix products, arithmetic and copies ran while one was open for 1% of the time, Pallas kernels for 20%

profile of v2, /device:TPU:0, one launch (start us, length us, event | category | flops | bytes accessed | tf_op | source)
XLA Modules:
  0.0 491.8 jit_solution(17832177850876271399)
XLA Ops:
  0.7 0.8 fusion.8
  1.4 1.0 copy.35
  3.4 0.8 reshape.208
  4.9 2.3 fusion.5.x
  7.2 0.7 pad_maximum_fusion.1.win
  8.0 0.7 pad_maximum_fusion.w1
  8.7 124.7 %gather.1 = (bf16[8,528,1024]{2,1,0:T(8,128)(2,1)}, bf16[4,8,48,384]{3,2,1,0:T(8,128)(2,1)}, bf16[8,4,32,5120]{3,2,1,0:T(8,128)(2,1)}, bf16[8,4,128,1024]{3,2,1,0:T(8,128)(2,1)}) custom-call(bf16[528,1024]{1,0:T(8,128)(2,1)} %fusion.5.x, bf16[8,48,384]{2,1,0:T(8,128)(2,1)} %pad_maximum_fusion.1.win, bf16[32,5120]{1,0:T(8,128)(2,1)} %pad_maximum_fusion.w1, ...), custom_call_target="tpu_custom_call" | custom-call | tf_op jit(solution)/shard_map/gather/pallas_call | solution.py:175
  133.4 1.4 copy.29
  135.3 0.9 convert_reduce_fusion
  136.2 6.9 %fusion = f32[8,512,384]{2,1,0:T(8,128)S(1)} fusion(bf16[1024,384,1]{1,0,2:T(8,128)(2,1)S(1)} %bitcast.69, bf16[8,528,1024]{2,1,0:T(8,128)(2,1)} %get-tuple-element.42.x_hbm), kind=kOutput, calls=%fused_computation | convolution fusion | flops 3221225472 | bytes 15466496 | tf_op jit(solution)/shard_map/brd,dc->brc/dot_general | solution.py:827
  143.1 1.8 fusion.9
  144.9 1.2 fusion.3
  146.2 2.6 select_convert_fusion
  148.8 31.7 %attend.1 = (bf16[8,2,256,128]{3,2,1,0:T(8,128)(2,1)}, f32[2,8,2048]{2,1,0:T(8,128)}) custom-call(bf16[8,2,256,128]{3,2,1,0:T(8,128)(2,1)} %bitcast.59, bf16[8,2,256,128]{3,2,1,0:T(8,128)(2,1)} %get-tuple-element.72.qm_ref, bf16[8,2,256,128]{3,2,1,0:T(8,128)(2,1)} %bitcast.57, bf16[8,2,256,128]{3,2,1,0:T(8,128)(2,1)} %get-tuple-element.71.km_ref, ...), custom_call_target="tpu_custom_call" | custom-call | tf_op jit(solution)/shard_map/attend/pallas_call | solution.py:339
  180.4 3.7 all-to-all-start
  185.5 13.8 %all-to-all-done.att_ref = bf16[8,512,128]{2,1,0:T(8,128)(2,1)S(1)} async-done(((bf16[8,512,128]{2,1,0:T(8,128)(2,1)}), bf16[8,512,128]{2,1,0:T(8,128)(2,1)S(1)}, u32[]{:S(2)}, u32[]{:S(2)}) %all-to-all-start) | async-done | bytes 1048608 | tf_op jit(solution)/shard_map/all_to_all | solution.py:765
  199.4 1.0 copy-done.1
  200.3 51.7 %middle.1 = (bf16[512,1024]{1,0:T(8,128)(2,1)}, f32[512,1024]{1,0:T(8,128)}, bf16[8,512,128]{2,1,0:T(8,128)(2,1)}, f32[8,1024]{1,0:T(8,128)}, f32[1,4096]{1,0:T(...) custom-call(bf16[512,1024]{1,0:T(8,128)(2,1)} %bitcast.64, bf16[8,512,128]{2,1,0:T(8,128)(2,1)} %copy-done.1, ...), custom_call_target="tpu_custom_call" | custom-call | tf_op jit(solution)/shard_map/middle/pallas_call | solution.py:570
  252.0 3.8 all-to-all-start.1
  255.8 96.6 %reduce.13 = (f32[32,5120]{1,0:T(8,128)}, f32[128,1024]{1,0:T(8,128)}) custom-call(bf16[8,4,32,5120]{3,2,1,0:T(8,128)(2,1)} %bitcast.54, bf16[8,4,128,1024]{3,2,1,0:T(8,128)(2,1)} %bitcast.62), custom_call_target="tpu_custom_call" | custom-call | tf_op jit(solution)/shard_map/reduce/pallas_call | solution.py:286
  352.4 1.9 slice.104
  354.3 1.6 slice.103
  356.9 1.0 copy-done
  357.9 54.2 %attend_back.1 = (bf16[8,2,256,128]{3,2,1,0:T(8,128)(2,1)}, bf16[8,2,256,128]{3,2,1,0:T(8,128)(2,1)}, bf16[8,2,256,128]{3,2,1,0:T(8,128)(2,1)}) custom-call(bf16[8,2,256,128]{3,2,1,0:T(8,128)(2,1)} %bitcast.60, bf16[8,2,256,128]{3,2,1,0:T(8,128)(2,1)} %get-tuple-element.72.qm_ref, bf16[8,2,256,128]{3,2,1,0:T(8,128)(2,1)} %get-tuple-element.44.o_ref, ...), custom_call_target="tpu_custom_call" | custom-call | tf_op jit(solution)/shard_map/attend_back/pallas_call | solution.py:401
  412.1 71.0 %finish.1 = (f32[512,1024]{1,0:T(8,128)}, f32[8,32,384]{2,1,0:T(8,128)}, f32[8,384]{1,0:T(8,128)}) custom-call(bf16[8,2,256,128]{3,2,1,0:T(8,128)(2,1)} %get-tuple-element.50.dq, bf16[8,2,256,128]{3,2,1,0:T(8,128)(2,1)} %get-tuple-element.51.dk, bf16[8,2,256,128]{3,2,1,0:T(8,128)(2,1)} %get-tuple-element.52.dv, bf16[1024,384]{1,0:T(8,128)(2,1)} %bitcast.70, ...), custom_call_target="tpu_custom_call" | custom-call | tf_op jit(solution)/shard_map/finish/pallas_call | solution.py:731
  483.1 0.9 dynamic-slice_reduce_fusion.1
  484.0 1.4 dynamic-slice_bitcast_fusion
  485.4 0.8 constant_dynamic-slice_fusion.1
  486.2 1.1 reshape.222
  487.6 0.8 copy.42
  489.6 1.3 copy.49
  491.0 0.8 copy.50
  (49 shorter events, 6.1 us)
Async XLA Ops:
  0.6 7.3 %copy-start.6 = (bf16[32,1024]{1,0:T(8,128)(2,1)S(1)}, bf16[32,1024]{1,0:T(8,128)(2,1)}, u32[]{:S(2)}) copy-start(bf16[32,1024]{1,0:T(8,128)(2,1)} %param.15) | copy-start | bytes 196612
  0.7 7.3 %copy-start.5 = (bf16[32,4096]{1,0:T(8,128)(2,1)S(1)}, bf16[32,4096]{1,0:T(8,128)(2,1)}, u32[]{:S(2)}) copy-start(bf16[32,4096]{1,0:T(8,128)(2,1)} %param.16) | copy-start | bytes 786436
  135.0 8.2 %copy-start.2 = (bf16[32,32,384]{2,1,0:T(8,128)(2,1)}, bf16[32,32,384]{2,1,0:T(8,128)(2,1)S(1)}, u32[]{:S(2)}) copy-start(bf16[32,32,384]{2,1,0:T(8,128)(2,1)S(1)} %slice.111) | copy-start | bytes 2359300
  180.4 18.9 %all-to-all-start = ((bf16[8,512,128]{2,1,0:T(8,128)(2,1)}), bf16[8,512,128]{2,1,0:T(8,128)(2,1)S(1)}, u32[]{:S(2)}, u32[]{:S(2)}) async-start(bf16[8,512,128]{2,1,0:T(8,128)(2,1)} %bitcast.65), calls=%async_computation | async-start | bytes 2097152 | tf_op jit(solution)/shard_map/all_to_all | solution.py:765
  199.3 1.0 copy-start.1
  252.0 104.9 %all-to-all-start.1 = ((bf16[8,512,128]{2,1,0:T(8,128)(2,1)}), bf16[8,512,128]{2,1,0:T(8,128)(2,1)S(1)}, u32[]{:S(2)}, u32[]{:S(2)}) async-start(bf16[8,512,128]{2,1,0:T(8,128)(2,1)} %get-tuple-element.48), calls=%async_computation.1 | async-start | bytes 2097152 | tf_op jit(solution)/shard_map/all_to_all | solution.py:765
  255.8 100.1 %copy-start.7 = (f32[8,1024]{1,0:T(8,128)S(1)}, f32[8,1024]{1,0:T(8,128)}, u32[]{:S(2)}) copy-start(f32[8,1024]{1,0:T(8,128)} %get-tuple-element.54) | copy-start | bytes 98308
  255.8 100.3 %copy-start.8 = (f32[1,4096]{1,0:T(1,128)S(1)}, f32[1,4096]{1,0:T(1,128)}, u32[]{:S(2)}) copy-start(f32[1,4096]{1,0:T(1,128)} %get-tuple-element.55) | copy-start | bytes 49156
  356.9 1.0 copy-start
  483.1 6.5 %copy-start.3 = (f32[512,1024]{1,0:T(8,128)S(1)}, f32[512,1024]{1,0:T(8,128)}, u32[]{:S(2)}) copy-start(f32[512,1024]{1,0:T(8,128)} %get-tuple-element.56) | copy-start | bytes 6291460
  489.6 1.4 copy-start.4

commit v3 on v2

--- a/solution.py
+++ b/solution.py
@@ -31,10 +31,10 @@
 
 class Sender:
     def __init__(self, send, recv):
-        self.send, self.recv, self.started = send, recv, []
-
-    def go(self, src, dst, device, landing):
-        at = len(self.started)
+        self.send, self.recv, self.planned = send, recv, []
+
+    def plan(self, src, dst, device, landing):
+        at = len(self.planned)
 
         def copy(a, b):
             return pltpu.make_async_remote_copy(
@@ -47,12 +47,18 @@
             )
 
         out = copy(src, dst)
-        out.start()
-        self.started.append(out)
-        return copy(landing, landing)
+        self.planned.append(out)
+        landed = copy(landing, landing)
+        landed.go = out.start
+        return landed
+
+    def go(self, *what):
+        landed = self.plan(*what)
+        landed.go()
+        return landed
 
     def drain(self):
-        for out in self.started:
+        for out in self.planned:
             out.wait_send()
 
 
@@ -73,9 +79,79 @@
     return lax.axis_index("blk"), lax.axis_index("dp")
 
 
-def gather_kernel(x, win, w1, w2, X, W, W1, W2, send, recv, lsem):
+def first_lanes(shape):
+    return lax.broadcasted_iota(jnp.int32, shape, len(shape) - 1) < 64
+
+
+def rows_of(block):
+    return block.reshape(-1, block.shape[-1])
+
+
+def attend_tile(queries, keys, values):
+    rows = queries[0].shape[0]
+    ones = jnp.ones_like(values)
+    mine = first_lanes(values.shape)
+    outs, logs = [], []
+    for head in (0, 1):
+        scores = product_nt(queries[head], keys[head])
+        top = jnp.max(scores, axis=-1, keepdims=True)
+        weights = jnp.exp(scores - top).astype(LOW)
+        total = product(weights, jnp.where(mine == (head == 0), values, ones))
+        mass = pltpu.roll(total, 64, 1)
+        outs.append(total / mass)
+        logs.append(top + jnp.log(mass))
+    mine = first_lanes((rows, 128))
+    flipped = jnp.where(mine, logs[0], logs[1]).T
+    logs = jnp.concatenate([flipped[0:1], flipped[64:65], jnp.zeros((6, rows), HIGH)], axis=0)
+    return jnp.where(mine, outs[0], outs[1]).astype(LOW), logs
+
+
+def split_heads(mixed, bias, codes):
+    rows = mixed.shape[0]
+    q = (mixed[:, :128] + bias[0]).astype(LOW) * LOW(0.125)
+    k = mixed[:, 128:256].astype(LOW)
+    v = (mixed[:, 256:] + bias[1]).astype(LOW)
+    lanes = lax.broadcasted_iota(jnp.int32, (rows, 128), 1) % 64
+    protein = jnp.where(codes >= 4, codes - 4, codes)
+    q_marks = jnp.where((lanes < 5) & (lanes != protein), -FAR, 0.0).astype(LOW)
+    k_marks = jnp.where(lanes == jnp.minimum(codes, 4), 1.0, 0.0).astype(LOW)
+    mine = first_lanes((rows, 128))
+    return (
+        (jnp.where(mine, q, q_marks), jnp.where(mine, q_marks, q)),
+        (jnp.where(mine, k, k_marks), jnp.where(mine, k_marks, k)),
+        v,
+    )
+
+
+def front_kernel(
+    x,
+    win,
+    w1,
+    w2,
+    X_out,
+    raw,
+    W1,
+    W2,
+    rows_att,
+    wfull,
+    qh,
+    kh,
+    v,
+    att,
+    lse,
+    X,
+    W,
+    send,
+    recv,
+    asend,
+    arecv,
+    lsem,
+    osem,
+):
     b, z = position()
     bx, by, bd, bc = b ^ 2, b ^ 4, b ^ 6, b ^ 1
+    count = X.shape[1] - 16
+    slots, rows = qh.shape[2:4]
     greet([(b ^ d, z) for d in range(1, 8)] + [(b, z ^ d) for d in range(1, 4)])
     s = Sender(send, recv)
     locs = []
@@ -90,41 +166,71 @@
     local(w1, W1.at[b, z])
     local(w2, W2.at[b, z])
     to_x, to_y, to_core = (bx, z), (by, z), (bc, z)
-    cores = []
-
-    def core(src, full, bb, zz):
-        cores.append(s.go(src, full.at[bb, zz], to_core, full.at[bb ^ 1, zz]))
-
-    def along_z(src, full):
-        return [s.go(src, full.at[b, z], (b, z ^ d), full.at[b, z ^ d]) for d in (1, 2, 3)]
-
-    def first_hop(src, full, zz):
-        return [
-            s.go(src, full.at[b, zz], to_x, full.at[bx, zz]),
-            s.go(src, full.at[b, zz], to_y, full.at[by, zz]),
-        ]
-
-    def second_hop(full, zz, arriving):
-        arriving[0].wait_recv()
-        piece = half(full.at[bx, zz], 0)
-        one = s.go(piece, piece, to_y, half(full.at[bd, zz], 0))
-        core(full.at[bx, zz], full, bx, zz)
-        arriving[1].wait_recv()
-        piece = half(full.at[by, zz], 1)
-        two = s.go(piece, piece, to_x, half(full.at[bd, zz], 1))
-        core(full.at[by, zz], full, by, zz)
-        return [one, two]
+
+    def token_core(src, bb):
+        return s.plan(src, X.at[bb], to_core, X.at[bb ^ 1])
 
     columns = [
         s.go(win.at[b ^ d], W.at[z, b], (b ^ d, z), W.at[z, b ^ d]) for d in range(1, 8)
     ]
     token_x = s.go(x, X.at[b], to_x, X.at[bx])
     token_y = s.go(x, X.at[b], to_y, X.at[by])
-    z1, z2 = along_z(w1, W1), along_z(w2, W2)
-    cores.append(s.go(x, X.at[b], to_core, X.at[bc]))
-    core(w1, W1, b, z)
-    core(w2, W2, b, z)
-    hop1, hop2 = {0: first_hop(w1, W1, z)}, {0: first_hop(w2, W2, z)}
+    token_c = token_core(x, b)
+    token_c.go()
+
+    own, full = (w1, w2), (W1, W2)
+    ways = {}
+    for a in (0, 1):
+        F = full[a]
+        for d in range(4):
+            zz = z ^ d
+            src = F.at[b, zz] if d else own[a]
+            way = {}
+            if d:
+                way["z"] = s.plan(own[a], F.at[b, z], (b, zz), F.at[b, zz])
+            way["x"] = s.plan(src, F.at[b, zz], to_x, F.at[bx, zz])
+            way["y"] = s.plan(src, F.at[b, zz], to_y, F.at[by, zz])
+            piece = half(F.at[bx, zz], 0)
+            way["xy"] = s.plan(piece, piece, to_y, half(F.at[bd, zz], 0))
+            piece = half(F.at[by, zz], 1)
+            way["yx"] = s.plan(piece, piece, to_x, half(F.at[bd, zz], 1))
+            way["core"] = [
+                s.plan(src if bb is b else F.at[bb, zz], F.at[bb, zz], to_core, F.at[bb ^ 1, zz])
+                for bb in (b, bx, by, bd)
+            ]
+            ways[a, d] = way
+    for a in (0, 1):
+        for d in (1, 2, 3):
+            ways[a, d]["z"].go()
+
+    def first(d, a):
+        way = ways[a, d]
+        if d:
+            way["z"].wait_recv()
+        way["x"].go()
+        way["y"].go()
+        way["core"][0].go()
+
+    def second(d, a):
+        way = ways[a, d]
+        way["x"].wait_recv()
+        way["xy"].go()
+        way["core"][1].go()
+        way["y"].wait_recv()
+        way["yx"].go()
+        way["core"][2].go()
+
+    def third(d, a):
+        way = ways[a, d]
+        way["xy"].wait_recv()
+        way["yx"].wait_recv()
+        way["core"][3].go()
+
+    def both(stage, d):
+        stage(d, 0)
+        stage(d, 1)
+
+    both(first, 0)
     for copy in columns:
         copy.wait_recv()
     locs[0].wait()
@@ -132,34 +238,124 @@
     token_x.wait_recv()
     piece = half(X.at[bx], 0)
     token_one = s.go(piece, piece, to_y, half(X.at[bd], 0))
-    cores.append(s.go(X.at[bx], X.at[bx], to_core, X.at[bx ^ 1]))
+    token_xc = token_core(X.at[bx], bx)
+    token_xc.go()
     token_y.wait_recv()
     piece = half(X.at[by], 1)
     token_two = s.go(piece, piece, to_x, half(X.at[bd], 1))
-    cores.append(s.go(X.at[by], X.at[by], to_core, X.at[by ^ 1]))
-    for i, d in enumerate((1, 2, 3)):
-        for hop, arriving, full in ((hop1, z1, W1), (hop2, z2, W2)):
-            arriving[i].wait_recv()
-            hop[d] = first_hop(full.at[b, z ^ d], full, z ^ d)
-            core(full.at[b, z ^ d], full, b, z ^ d)
-    last1, last2 = {}, {}
-    for d in range(4):
-        for hop, last, full in ((hop1, last1, W1), (hop2, last2, W2)):
-            last[d] = second_hop(full, z ^ d, hop[d])
-        if d == 0:
-            token_one.wait_recv()
-            token_two.wait_recv()
-            cores.append(s.go(X.at[bd], X.at[bd], to_core, X.at[bd ^ 1]))
-    for d in range(4):
-        for last, full in ((last1, W1), (last2, W2)):
-            for copy in last[d]:
-                copy.wait_recv()
-            core(full.at[bd, z ^ d], full, bd, z ^ d)
-    for copy in cores + columns:
+    token_yc = token_core(X.at[by], by)
+    token_yc.go()
+    token_dc = token_core(X.at[bd], bd)
+    both(first, 1)
+    for copy in columns:
         copy.wait_recv()
+    raw_copy = pltpu.make_async_copy(W, raw, lsem.at[4])
+    raw_copy.start()
+    for i in range(8):
+        for j in range(4):
+            at = (i * 4 + j) * 32
+            wfull[at : at + 32] = W[j, i, 0:32]
+    bias = [
+        jnp.concatenate([W[j, b, 32:33, at : at + 32] for j in range(4)], axis=1).astype(HIGH)
+        for at in (64, 96)
+    ]
+
+    def mix(i):
+        pltpu.make_async_copy(X.at[i], X_out.at[i], osem.at[i]).start()
+        mixed = product(X[i, 0:count], wfull[...])
+        codes = jnp.broadcast_to(X[i, count : count + 1, 0:count].astype(HIGH), (128, count)).T
+        queries, keys, values = split_heads(mixed, bias, codes.astype(jnp.int32))
+        for head in (0, 1):
+            qh[head, i] = queries[head].reshape(slots, rows, 128)
+            kh[head, i] = keys[head].reshape(slots, rows, 128)
+        v[i] = values.reshape(slots, rows, 128)
+
+    locs[1].wait()
+    mix(b)
+    token_c.wait_recv()
+    mix(bc)
+    mix(bx)
+    token_xc.wait_recv()
+    mix(bx ^ 1)
+    both(first, 2)
+    mix(by)
+    token_yc.wait_recv()
+    mix(by ^ 1)
+    token_one.wait_recv()
+    token_two.wait_recv()
+    token_dc.go()
+    mix(bd)
+    both(first, 3)
+    token_dc.wait_recv()
+    mix(bd ^ 1)
+    both(second, 0)
+
+    def piece_of(slot):
+        return pl.ds(pl.multiple_of(slot * rows, rows), rows)
+
+    def send_att(slot, d):
+        return pltpu.make_async_remote_copy(
+            src_ref=att.at[b ^ d, slot],
+            dst_ref=rows_att.at[b, piece_of(slot)],
+            send_sem=asend.at[slot * 8 + d],
+            recv_sem=arecv.at[slot * 8 + d],
+            device_id=(b ^ d, z),
+            device_id_type=MESH,
+        )
+
+    def keep_att(slot):
+        return pltpu.make_async_copy(
+            att.at[b, slot], rows_att.at[b, piece_of(slot)], osem.at[8 + slot]
+        )
+
+    events = {4: (second, 1, 0), 6: (second, 1, 1), 10: (second, 2, 0), 12: (second, 2, 1)}
+
+    @pl.loop(0, 8 * slots)
+    def _(step):
+        slot, d = step // 8, (step + 1) % 8
+        i = b ^ d
+        keys = [rows_of(kh[head, :, slot]) for head in (0, 1)]
+        out, logs = attend_tile([qh[head, i, slot] for head in (0, 1)], keys, rows_of(v[:, slot]))
+        att[i, slot] = out
+        lse[slot, :, pl.ds(pl.multiple_of(i * rows, rows), rows)] = logs
+
+        @pl.when(d != 0)
+        def _():
+            send_att(slot, d).start()
+
+        @pl.when(d == 0)
+        def _():
+            keep_att(slot).start()
+
+        for at, (event, *what) in events.items():
+            pl.when(step == at)(functools.partial(event, *what))
+
+    both(third, 0)
+    both(second, 3)
+    for d in (1, 2, 3):
+        both(third, d)
+    for way in ways.values():
+        for copy in way["core"]:
+            copy.wait_recv()
+    for slot in range(slots):
+        keep_att(slot).wait()
+        for d in range(1, 8):
+            copy = send_att(slot, d)
+            copy.wait_send()
+            pltpu.make_async_remote_copy(
+                src_ref=rows_att.at[b ^ d, piece_of(slot)],
+                dst_ref=rows_att.at[b ^ d, piece_of(slot)],
+                send_sem=asend.at[slot * 8 + d],
+                recv_sem=arecv.at[slot * 8 + d],
+                device_id=(b ^ d, z),
+                device_id_type=MESH,
+            ).wait_recv()
     s.drain()
-    for copy in locs[1:]:
+    for copy in locs[2:]:
         copy.wait()
+    raw_copy.wait()
+    for i in range(8):
+        pltpu.make_async_copy(X.at[i], X_out.at[i], osem.at[i]).wait()
 
 
 def in_hbm(count):
@@ -170,21 +366,36 @@
     return [pltpu.SemaphoreType.DMA((count,)), pltpu.SemaphoreType.DMA((count,))]
 
 
-def gather(x, win, w1, w2):
+def front(x, win, w1, w2, slots):
+    count, width = x.shape[0] - 16, x.shape[1]
+    rows = count // slots
     shape = lambda *s: jax.ShapeDtypeStruct(s, LOW)
+    vmem = pl.BlockSpec(memory_space=pltpu.VMEM)
     return pl.pallas_call(
-        gather_kernel,
+        front_kernel,
         out_shape=(
             shape(8, *x.shape),
             shape(4, *win.shape),
             shape(8, 4, *w1.shape),
             shape(8, 4, *w2.shape),
+            shape(8, count, 128),
+            shape(width, win.shape[2]),
+            shape(2, 8, slots, rows, 128),
+            shape(2, 8, slots, rows, 128),
+            shape(8, slots, rows, 128),
+            shape(8, slots, rows, 128),
+            jax.ShapeDtypeStruct((slots, 8, 8 * rows), HIGH),
         ),
         in_specs=in_hbm(4),
-        out_specs=tuple(in_hbm(4)),
-        scratch_shapes=pair_of_semaphores(100) + [pltpu.SemaphoreType.DMA((4,))],
-        compiler_params=pltpu.CompilerParams(collective_id=1, has_side_effects=True),
-        name="gather",
+        out_specs=tuple(in_hbm(5)) + (vmem,) * 6,
+        scratch_shapes=[pltpu.VMEM((8, *x.shape), LOW), pltpu.VMEM((4, *win.shape), LOW)]
+        + pair_of_semaphores(100)
+        + pair_of_semaphores(8 * slots)
+        + [pltpu.SemaphoreType.DMA((5,)), pltpu.SemaphoreType.DMA((8 + slots,))],
+        compiler_params=pltpu.CompilerParams(
+            collective_id=1, has_side_effects=True, vmem_limit_bytes=VMEM_LIMIT
+        ),
+        name="front",
     )(x, win, w1, w2)
 
 
@@ -296,118 +507,105 @@
     )(g1, g2)
 
 
-def first_lanes(shape):
-    return lax.broadcasted_iota(jnp.int32, shape, len(shape) - 1) < 64
-
-
-def marked(block, marks, head):
-    mine = first_lanes(block.shape)
-    return jnp.where(mine if head == 0 else jnp.logical_not(mine), block, marks)
-
-
-def rows_of(ref, slot=0):
-    block = ref[:, slot]
-    return block.reshape(-1, block.shape[-1])
-
-
-def attend_kernel(q_ref, qm_ref, k_ref, km_ref, v_ref, out_ref, lse_ref):
-    queries, q_marks = q_ref[0, 0], qm_ref[0, 0]
-    keys, k_marks, values = rows_of(k_ref), rows_of(km_ref), rows_of(v_ref)
-    ones = jnp.ones_like(values)
-    rows = queries.shape[0]
-    outs, logs = [], []
-    for head in (0, 1):
-        scores = product_nt(marked(queries, q_marks, head), marked(keys, k_marks, head))
-        top = jnp.max(scores, axis=-1, keepdims=True)
-        weights = jnp.exp(scores - top).astype(LOW)
-        total = product(weights, marked(values, ones, head))
-        mass = pltpu.roll(total, 64, 1)
-        outs.append(total / mass)
-        logs.append(top + jnp.log(mass))
-    out_ref[0, 0] = jnp.where(first_lanes((rows, 128)), outs[0], outs[1]).astype(LOW)
-    both = jnp.where(first_lanes((rows, 128)), logs[0], logs[1])
-    flipped = both.T
-    lse_ref[0] = jnp.concatenate(
-        [flipped[0:1], flipped[64:65], jnp.zeros((6, rows), HIGH)], axis=0
+def attend_kernel(qh_ref, kh_ref, v_ref, out_ref, lse_ref):
+    keys = [rows_of(kh_ref[head, :, 0]) for head in (0, 1)]
+    out_ref[0, 0], lse_ref[0] = attend_tile(
+        [qh_ref[head, 0, 0] for head in (0, 1)], keys, rows_of(v_ref[:, 0])
     )
 
 
-def attend(q, qm, k, km, v):
-    blocks, slots, rows, lanes = q.shape
+def attend(qh, kh, v):
+    blocks, slots, rows, lanes = v.shape
     tile = pl.BlockSpec((1, 1, rows, lanes), lambda s, i: (i, s, 0, 0))
+    tiles = pl.BlockSpec((2, 1, 1, rows, lanes), lambda s, i: (0, i, s, 0, 0))
     whole = pl.BlockSpec((blocks, 1, rows, lanes), lambda s, i: (0, s, 0, 0))
+    wholes = pl.BlockSpec((2, blocks, 1, rows, lanes), lambda s, i: (0, 0, s, 0, 0))
     return pl.pallas_call(
         attend_kernel,
         grid=(slots, blocks),
         out_shape=(
-            jax.ShapeDtypeStruct(q.shape, LOW),
+            jax.ShapeDtypeStruct(v.shape, LOW),
             jax.ShapeDtypeStruct((slots, 8, blocks * rows), HIGH),
         ),
-        in_specs=[tile, tile, whole, whole, whole],
+        in_specs=[tiles, wholes, whole],
         out_specs=(tile, pl.BlockSpec((1, 8, rows), lambda s, i: (s, 0, i))),
         compiler_params=pltpu.CompilerParams(vmem_limit_bytes=VMEM_LIMIT),
         name="attend",
-    )(q, qm, k, km, v)
+    )(qh, kh, v)
+
+
+def row_products(out, grad):
+    pick = (lax.broadcasted_iota(jnp.int32, (8, 128), 0) == 0) == first_lanes((8, 128))
+    return lax.dot_general(
+        pick.astype(HIGH),
+        out.astype(HIGH) * grad.astype(HIGH),
+        (((1,), (1,)), ((), ())),
+        precision=lax.Precision.HIGHEST,
+        preferred_element_type=HIGH,
+    )
+
+
+def attend_back_tile(queries, keys, values, grads, logs, delta, acc):
+    zeros = jnp.zeros_like(grads)
+    mine = first_lanes(grads.shape)
+    dk, dv = [], 0.0
+    for head in (0, 1):
+        grad = jnp.where(mine == (head == 0), grads, zeros)
+        probs = jnp.exp(product_nt(keys[head], queries[head]) - logs[head : head + 1])
+        pushed = product_nt(values, grad)
+        d_scores = (probs * (pushed - delta[head : head + 1])).astype(LOW)
+        dv = dv + product(probs.astype(LOW), grad)
+        dk.append(product(d_scores, queries[head]))
+        keys_t = keys[head].T[head * 64 : head * 64 + 64]
+        acc[head * 64 : head * 64 + 64, :] += product(keys_t, d_scores)
+    return jnp.where(first_lanes(dk[0].shape), dk[0], dk[1]).astype(LOW), dv.astype(LOW)
 
 
 def attend_back_kernel(
-    q_ref, qm_ref, o_ref, g_ref, lse_ref, k_ref, km_ref, v_ref, dq_ref, dk_ref, dv_ref, acc, delta
+    qh_ref, o_ref, g_ref, lse_ref, kh_ref, v_ref, dq_ref, dk_ref, dv_ref, acc, delta
 ):
     tile = pl.program_id(1)
-    blocks, _, rows, _ = q_ref.shape
-    count = blocks * rows
-    queries, q_marks, grads = rows_of(q_ref), rows_of(qm_ref), rows_of(g_ref)
-    keys, k_marks, values = k_ref[0, 0], km_ref[0, 0], v_ref[0, 0]
+    blocks, _, rows, _ = g_ref.shape
+    grads = rows_of(g_ref[:, 0])
 
     @pl.when(tile == 0)
     def _():
         acc[...] = jnp.zeros_like(acc)
-        pick = (lax.broadcasted_iota(jnp.int32, (8, 128), 0) == 0) == first_lanes((8, 128))
-        inner = rows_of(o_ref).astype(HIGH) * grads.astype(HIGH)
-        delta[...] = lax.dot_general(
-            pick.astype(HIGH),
-            inner,
-            (((1,), (1,)), ((), ())),
-            precision=lax.Precision.HIGHEST,
-            preferred_element_type=HIGH,
-        )
-
-    zeros = jnp.zeros((count, 128), LOW)
-    keys_t = keys.T
-    dk, dv = [], 0.0
-    for head in (0, 1):
-        query, grad = marked(queries, q_marks, head), marked(grads, zeros, head)
-        probs = jnp.exp(product_nt(marked(keys, k_marks, head), query) - lse_ref[0, head : head + 1])
-        pushed = product_nt(values, grad)
-        d_scores = (probs * (pushed - delta[head : head + 1])).astype(LOW)
-        dv = dv + product(probs.astype(LOW), grad)
-        dk.append(product(d_scores, query))
-        lanes = pl.ds(head * 64, 64)
-        acc[lanes, :] += product(keys_t[head * 64 : head * 64 + 64], d_scores)
-    dk_ref[0, 0] = jnp.where(first_lanes((rows, 128)), dk[0], dk[1]).astype(LOW)
-    dv_ref[0, 0] = dv.astype(LOW)
+        delta[...] = row_products(rows_of(o_ref[:, 0]), grads)
+
+    dk_ref[0, 0], dv_ref[0, 0] = attend_back_tile(
+        [rows_of(qh_ref[head, :, 0]) for head in (0, 1)],
+        [kh_ref[head, 0, 0] for head in (0, 1)],
+        v_ref[0, 0],
+        grads,
+        lse_ref[0],
+        delta[...],
+        acc,
+    )
 
     @pl.when(tile == blocks - 1)
     def _():
         dq_ref[:, 0] = (acc[...].T * 0.125).astype(LOW).reshape(blocks, rows, 128)
 
 
-def attend_back(q, qm, o, g, lse, k, km, v):
-    blocks, slots, rows, lanes = q.shape
+def attend_back(qh, o, g, lse, kh, v):
+    blocks, slots, rows, lanes = v.shape
     tile = pl.BlockSpec((1, 1, rows, lanes), lambda s, i: (i, s, 0, 0))
+    tiles = pl.BlockSpec((2, 1, 1, rows, lanes), lambda s, i: (0, i, s, 0, 0))
     whole = pl.BlockSpec((blocks, 1, rows, lanes), lambda s, i: (0, s, 0, 0))
+    wholes = pl.BlockSpec((2, blocks, 1, rows, lanes), lambda s, i: (0, 0, s, 0, 0))
     logs = pl.BlockSpec((1, 8, blocks * rows), lambda s, i: (s, 0, 0))
-    shape = jax.ShapeDtypeStruct(q.shape, LOW)
+    shape = jax.ShapeDtypeStruct(v.shape, LOW)
     return pl.pallas_call(
         attend_back_kernel,
         grid=(slots, blocks),
         out_shape=(shape,) * 3,
-        in_specs=[whole, whole, whole, whole, logs, tile, tile, tile],
+        in_specs=[wholes, whole, whole, logs, tiles, tile],
         out_specs=(whole, tile, tile),
         scratch_shapes=[pltpu.VMEM((lanes, blocks * rows), HIGH), pltpu.VMEM((8, blocks * rows), HIGH)],
         compiler_params=pltpu.CompilerParams(vmem_limit_bytes=VMEM_LIMIT),
         name="attend_back",
-    )(q, qm, o, g, lse, k, km, v)
+    )(qh, o, g, lse, kh, v)
 
 
 def normalize(values):
@@ -765,6 +963,32 @@
     return lax.all_to_all(pieces, "blk", 0, 0)
 
 
+def by_slot(block, slots):
+    blocks, count, held = block.shape
+    block = block.reshape(blocks, slots, count // slots, held)
+    return jnp.pad(block, ((0, 0),) * 3 + ((0, 128 - held),))
+
+
+def front_apart(X, W, bias, slots):
+    n_blk, count = X.shape[0], X.shape[1] - 16
+    held = W.shape[1] // 3
+    mixed = jnp.einsum("brd,dc->brc", X[:, :count], W, preferred_element_type=HIGH)
+    parts = [mixed[..., i * held : (i + 1) * held] for i in range(3)]
+    parts = [jnp.pad(p, ((0, 0), (0, 0), (0, 128 - held))).reshape(-1, 128) for p in parts]
+    own = lax.dynamic_slice(bias[:2], (0, lax.axis_index("blk") * held), (2, held))
+    own = jnp.pad(own, ((0, 0), (0, 128 - held)))
+    codes = X[:, count, :count].reshape(-1, 1).astype(jnp.int32)
+    codes = jnp.broadcast_to(codes, (n_blk * count, 128))
+    queries, keys, values = split_heads(jnp.concatenate(parts, axis=1), (own[0], own[1]), codes)
+    shape = (n_blk, slots, count // slots, 128)
+    qh = jnp.stack(queries).reshape(2, *shape)
+    kh = jnp.stack(keys).reshape(2, *shape)
+    v = values.reshape(shape)
+    att, lse = attend(qh, kh, v)
+    rows_att = swap(att[..., :held].reshape(n_blk, count, held))
+    return qh, kh, v, att, lse, rows_att
+
+
 def on_device(
     tokens,
     input_weight,
@@ -798,12 +1022,11 @@
     if fast:
         small = jnp.concatenate([small[None], jnp.zeros((15, small.shape[0]), LOW)], axis=0)
         small = jnp.broadcast_to(small, (n_blk, *small.shape))
-        X, W, W1, W2 = gather(
-            sent_tokens, jnp.concatenate([columns, small], axis=1), both, reduce_weight
+        win = jnp.concatenate([columns, small], axis=1)
+        X, raw, W1, W2, rows_att, W, qh, kh, v, att, lse = front(
+            sent_tokens, win, both, reduce_weight, slots
         )
-        W = W.transpose(1, 0, 2, 3).reshape(shards, -1, 3 * held)
-        small = W[:, shard]
-        W = W[:, :shard].reshape(width, 3 * held)
+        small = raw[:, :, shard].transpose(1, 0, 2).reshape(shards, 3 * held)
         W1, W2 = W1.reshape(width, -1), W2.reshape(hidden, width)
     else:
         X = lax.all_gather(sent_tokens, "blk")
@@ -817,26 +1040,9 @@
     gain, bias = cuts[:2], cuts[2:]
     hidden_full = small[:, 8 * part :].reshape(hidden).astype(HIGH)
 
-    codes = X[:, count, :count].reshape(n_blk, slots, rows, 1).astype(jnp.int32)
-    lanes = lax.broadcasted_iota(jnp.int32, (1, 1, 1, 128), 3) % 64
-    q_marks = jnp.where((lanes < 5) & (lanes != codes % 4), -FAR, 0.0).astype(LOW)
-    k_marks = jnp.where(lanes == jnp.minimum(codes, 4), 1.0, 0.0).astype(LOW)
-
     all_tokens = X[:, :count]
-    me = lax.axis_index("blk")
-    mixed = jnp.einsum("brd,dc->brc", all_tokens, W, preferred_element_type=HIGH)
-    own_bias = lax.dynamic_slice(bias[:2], (0, me * held), (2, held))
-    q = (mixed[..., :held] + own_bias[0]).astype(LOW) * LOW(0.125)
-    k = mixed[..., held : 2 * held].astype(LOW)
-    v = (mixed[..., 2 * held :] + own_bias[1]).astype(LOW)
-
-    def heads(block):
-        block = block.reshape(n_blk, slots, rows, held)
-        return jnp.pad(block, ((0, 0),) * 3 + ((0, 128 - held),))
-
-    q, k, v = heads(q), heads(k), heads(v)
-    att, lse = attend(q, q_marks, k, k_marks, v)
-    rows_att = swap(att[..., :held].reshape(n_blk, count, held))
+    if not fast:
+        qh, kh, v, att, lse, rows_att = front_apart(X, W, bias, slots)
     middle_out = middle(
         flat,
         rows_att,
@@ -858,7 +1064,8 @@
         sum_reduce = lax.psum_scatter(grad_reduce, BOTH, scatter_dimension=0, tiled=True)
         sum_reduce = sum_reduce.astype(HIGH)
 
-    dq, dk, dv = attend_back(q, q_marks, att, heads(g), lse, k, k_marks, v)
+    g = by_slot(g, slots)
+    dq, dk, dv = attend_back(qh, att, g, lse, kh, v)
     small_rows = sums[:6].reshape(6, shards, part).transpose(1, 0, 2).reshape(shards, 6 * part)
     small_rows = jnp.concatenate([small_rows, d_hidden.reshape(shards, -1)], axis=1)
     if fast:

time: 494 us -> 454 us (0.919)
  waiting for transfers between devices: 13.8 us -> 0.01 us
  Pallas kernels: 430 us -> 423 us
  matrix products: 6.95 us -> 0 us
  other arithmetic: 13.7 us -> 7.19 us
    all_to_all x2 -> x1, waiting for transfers between devices: 13.8 us -> 0.01 us  [swap(): return lax.all_to_all(pieces, 'blk', 0, 0)]
    dot_general x1 -> x0, matrix products: 6.95 us -> none  [on_device(): jnp.einsum('brd,dc->brc', all_tokens, W, preferred_element_type=HIGH)]
    pallas_call x2 -> x1, Pallas kernels: 156 us -> 150 us  [front(): pl.pallas_call(front_kernel, out_shape=(shape(8, *x.shape), shape(4, *win...]
  transfers between devices with their start and end apart: 2 -> 1, of which waited for: 1 -> 0; matrix products, arithmetic and copies ran while one was open for 1% -> 1% of each run, Pallas kernels for 20% -> 21%
where the time goes in v3:
time: 454 us; the launch traced here: 452 us
  Pallas kernels  423 us (93%)
  local copies, waits for them, and re-layouts  17.4 us (4%)
  other arithmetic  7.19 us (2%)
    pallas_call x1, Pallas kernels, front(): pl.pallas_call(front_kernel, out_shape=(shape(8, *x.shape), shape(4, *win...  150 us
    pallas_call x1, Pallas kernels, reduce(): pl.pallas_call(reduce_kernel, out_shape=tuple((jax.ShapeDtypeStruct(s, HI...  97.1 us
    pallas_call x1, Pallas kernels, finish(): pl.pallas_call(finish_kernel, out_shape=(shape((count, width), HIGH), sha...  71.6 us
    pallas_call x1, Pallas kernels, attend_back(): pl.pallas_call(attend_back_kernel, grid=(slots, blocks), out_shape=(shape...  52.3 us
    pallas_call x1, Pallas kernels, middle(): pl.pallas_call(functools.partial(middle_kernel, chunk), out_shape=(shape(...  51.9 us
  transfers between devices with their start and end apart: 1, of which 0 were waited for; matrix products, arithmetic and copies ran while one was open for 1% of the time, Pallas kernels for 21%

profile of v3, /device:TPU:0, one launch (start us, length us, event | category | flops | bytes accessed | tf_op | source)
XLA Modules:
  0.0 451.9 jit_solution(4362625276918053500)
XLA Ops:
  0.7 0.8 fusion.2
  1.4 1.0 copy.35
  2.5 0.2 reshape.140
  2.7 0.7 reshape.141
  3.4 0.8 reshape.142
  4.2 0.7 pad_maximum_fusion.3
  4.9 2.3 fusion.1.x
  7.2 0.7 pad_maximum_fusion.1.win
  8.0 0.7 pad_maximum_fusion.w1
  8.7 150.0 %front.1 = (bf16[8,528,1024]{2,1,0:T(8,128)(2,1)}, bf16[4,8,48,384]{3,2,1,0:T(8,128)(2,1)}, bf16[8,4,32,5120]{3,2,1,0:T(8,128)(2,1)}, bf16[8,4,128,1024]{3,2,1,0...) custom-call(bf16[528,1024]{1,0:T(8,128)(2,1)} %fusion.1.x, ...), custom_call_target="tpu_custom_call" | custom-call | tf_op jit(solution)/shard_map/front/pallas_call | solution.py:374
  158.7 1.0 slice.56
  159.7 0.6 slice_convert_fusion.1
  160.4 0.7 reshape.155.par_ref
  161.2 51.9 %middle.1 = (bf16[512,1024]{1,0:T(8,128)(2,1)}, f32[512,1024]{1,0:T(8,128)}, bf16[8,512,128]{2,1,0:T(8,128)(2,1)}, f32[8,1024]{1,0:T(8,128)}, f32[1,4096]{1,0:T(...) custom-call(bf16[512,1024]{1,0:T(8,128)(2,1)} %bitcast.46, ...), custom_call_target="tpu_custom_call" | custom-call | tf_op jit(solution)/shard_map/middle/pallas_call | solution.py:768
  213.1 3.6 all-to-all-start
  216.7 97.1 %reduce.11 = (f32[32,5120]{1,0:T(8,128)}, f32[128,1024]{1,0:T(8,128)}) custom-call(bf16[8,4,32,5120]{3,2,1,0:T(8,128)(2,1)} %bitcast.42, bf16[8,4,128,1024]{3,2,1,0:T(8,128)(2,1)} %bitcast.44), custom_call_target="tpu_custom_call" | custom-call | tf_op jit(solution)/shard_map/reduce/pallas_call | solution.py:497
  313.8 1.9 slice.61
  315.7 1.6 slice.60
  317.5 0.7 select_maximum_fusion.small
  318.3 1.0 copy-done
  319.3 52.3 %attend_back.1 = (bf16[8,2,256,128]{3,2,1,0:T(8,128)(2,1)}, bf16[8,2,256,128]{3,2,1,0:T(8,128)(2,1)}, bf16[8,2,256,128]{3,2,1,0:T(8,128)(2,1)}) custom-call(bf16[2,8,2,256,128]{4,3,2,1,0:T(8,128)(2,1)} %get-tuple-element.52.qh_ref, bf16[8,2,256,128]{3,2,1,0:T(8,128)(2,1)} %get-tuple-element.53.o_ref, bf16[8,2,256,128]{3,2,1,0:T(8,128)(2,1)} %bitcast.47, ...), custom_call_target="tpu_custom_call" | custom-call | tf_op jit(solution)/shard_map/attend_back/pallas_call | solution.py:599
  371.6 71.6 %finish.1 = (f32[512,1024]{1,0:T(8,128)}, f32[8,32,384]{2,1,0:T(8,128)}, f32[8,384]{1,0:T(8,128)}) custom-call(bf16[8,2,256,128]{3,2,1,0:T(8,128)(2,1)} %get-tuple-element.58.dq, bf16[8,2,256,128]{3,2,1,0:T(8,128)(2,1)} %get-tuple-element.59.dk, bf16[8,2,256,128]{3,2,1,0:T(8,128)(2,1)} %get-tuple-element.60.dv, bf16[1024,384]{1,0:T(8,128)(2,1)} %get-tuple-element.61.w, ...), custom_call_target="tpu_custom_call" | custom-call | tf_op jit(solution)/shard_map/finish/pallas_call | solution.py:929
  443.2 0.9 dynamic-slice_reduce_fusion.1
  444.0 1.4 dynamic-slice_bitcast_fusion
  445.5 0.8 constant_dynamic-slice_fusion
  446.2 1.1 reshape.151
  447.4 0.2 copy.32
  447.6 0.8 copy.42
  448.4 0.6 slice.63
  449.1 0.6 pad_maximum_fusion.2
  449.7 1.3 copy.49
  451.1 0.8 copy.50
  (29 shorter events, 0.7 us)
Async XLA Ops:
  0.6 7.3 %copy-start.4 = (bf16[32,1024]{1,0:T(8,128)(2,1)S(1)}, bf16[32,1024]{1,0:T(8,128)(2,1)}, u32[]{:S(2)}) copy-start(bf16[32,1024]{1,0:T(8,128)(2,1)} %param.15) | copy-start | bytes 196612
  0.7 7.3 %copy-start.3 = (bf16[32,4096]{1,0:T(8,128)(2,1)S(1)}, bf16[32,4096]{1,0:T(8,128)(2,1)}, u32[]{:S(2)}) copy-start(bf16[32,4096]{1,0:T(8,128)(2,1)} %param.16) | copy-start | bytes 786436
  213.1 105.2 %all-to-all-start = ((bf16[8,512,128]{2,1,0:T(8,128)(2,1)}), bf16[8,512,128]{2,1,0:T(8,128)(2,1)S(1)}, u32[]{:S(2)}, u32[]{:S(2)}) async-start(bf16[8,512,128]{2,1,0:T(8,128)(2,1)} %get-tuple-element.54), calls=%async_computation | async-start | bytes 2097152 | tf_op jit(solution)/shard_map/all_to_all | solution.py:963
  216.7 100.6 %copy-start.5 = (f32[8,1024]{1,0:T(8,128)S(1)}, f32[8,1024]{1,0:T(8,128)}, u32[]{:S(2)}) copy-start(f32[8,1024]{1,0:T(8,128)} %get-tuple-element.63) | copy-start | bytes 98308
  216.7 100.8 %copy-start.6 = (f32[1,4096]{1,0:T(1,128)S(1)}, f32[1,4096]{1,0:T(1,128)}, u32[]{:S(2)}) copy-start(f32[1,4096]{1,0:T(1,128)} %get-tuple-element.64) | copy-start | bytes 49156
  318.3 1.0 copy-start
  443.2 6.5 %copy-start.1 = (f32[512,1024]{1,0:T(8,128)S(1)}, f32[512,1024]{1,0:T(8,128)}, u32[]{:S(2)}) copy-start(f32[512,1024]{1,0:T(8,128)} %get-tuple-element.66) | copy-start | bytes 6291460
  449.7 1.4 copy-start.2

commit v4 on v3

--- a/solution.py
+++ b/solution.py
@@ -406,105 +406,87 @@
         out[rows, :] = one[rows, :] + two[rows, :]
 
 
-def reduce_kernel(g1, g2, o1, o2, *scratch):
-    C, S, H, Q, Z = [scratch[2 * i : 2 * i + 2] for i in range(5)]
-    send, recv, lsem = scratch[10:]
-    G, O = (g1, g2), (o1, o2)
-    b, z = position()
-    greet([(b ^ d, z) for d in (1, 2, 4)] + [(b, z ^ d) for d in (1, 2, 3)])
-    to_x, to_y, to_core = (b ^ 2, z), (b ^ 4, z), (b ^ 1, z)
-    s = Sender(send, recv)
-    own, other = {}, {}
-    order = (1, 2, 3, 0)
-    for d in order:
+class Reducer:
+    ORDER = (1, 2, 3, 0)
+
+    def __init__(self, s, g, out, C, S, H, Q, Z, lsem):
+        b, z = position()
+        to_x, to_y, to_core = (b ^ 2, z), (b ^ 4, z), (b ^ 1, z)
+        self.out, self.C, self.S, self.H, self.Q, self.Z = out, C, S, H, Q, Z
+        self.mine, self.other, self.halves, self.ahead, self.rest, self.last = ({} for _ in range(6))
+        for d in self.ORDER:
+            for e in (3, 1, 2, 0):
+                self.mine[d, e] = pltpu.make_async_copy(
+                    g.at[b ^ (2 * e), z ^ d], S.at[e, d], lsem.at[d * 4 + e]
+                )
+                self.other[d, e] = s.plan(
+                    g.at[b ^ 1 ^ (2 * e), z ^ d], C.at[e, d], to_core, C.at[e, d]
+                )
+
+            def send(e, part, to, where):
+                return s.plan(half(S.at[e, d], part), where, to, where)
+
+            self.halves[d] = [send(3, 0, to_x, H.at[d, 0]), send(3, 1, to_y, H.at[d, 1])]
+            self.ahead[d] = [
+                send(2, 1, to_y, half(Q.at[d, 1], 1)),
+                send(1, 0, to_x, half(Q.at[d, 0], 0)),
+            ]
+            self.rest[d] = [
+                send(2, 0, to_y, half(Q.at[d, 1], 0)),
+                send(1, 1, to_x, half(Q.at[d, 0], 1)),
+            ]
+            if d:
+                self.last[d] = s.plan(S.at[0, d], Z.at[d - 1], (b, z ^ d), Z.at[d - 1])
+
+    def start(self):
+        for d in self.ORDER:
+            for e in (3, 1, 2, 0):
+                self.mine[d, e].start()
+                self.other[d, e].go()
+
+    def fold(self, d):
         for e in (3, 1, 2, 0):
-            for a in (0, 1):
-                at = (d * 4 + e) * 2 + a
-                copy = pltpu.make_async_copy(G[a].at[b ^ (2 * e), z ^ d], S[a].at[e, d], lsem.at[at])
-                copy.start()
-                own[a, d, e] = copy
-                other[a, d, e] = s.go(
-                    G[a].at[b ^ 1 ^ (2 * e), z ^ d], C[a].at[e, d], to_core, C[a].at[e, d]
-                )
-    halves, pieces, last = {}, {}, {}
-
-    def fold(d):
-        for e in (3, 1, 2, 0):
-            for a in (0, 1):
-                own[a, d, e].wait()
-                other[a, d, e].wait_recv()
-                add_rows(S[a].at[e, d], S[a].at[e, d], C[a].at[e, d])
-                if e == 3:
-                    halves[a, d] = [
-                        s.go(half(S[a].at[3, d], 0), H[a].at[d, 0], to_x, H[a].at[d, 0]),
-                        s.go(half(S[a].at[3, d], 1), H[a].at[d, 1], to_y, H[a].at[d, 1]),
-                    ]
-
-    def relay(d):
-        for a in (0, 1):
-            halves[a, d][0].wait_recv()
-            part = half(S[a].at[2, d], 0)
-            add_rows(part, part, H[a].at[d, 0])
-            one = s.go(S[a].at[2, d], Q[a].at[d, 1], to_y, Q[a].at[d, 1])
-            halves[a, d][1].wait_recv()
-            part = half(S[a].at[1, d], 1)
-            add_rows(part, part, H[a].at[d, 1])
-            two = s.go(S[a].at[1, d], Q[a].at[d, 0], to_x, Q[a].at[d, 0])
-            pieces[a, d] = [one, two]
-
-    def collect(d):
-        for a in (0, 1):
-            for copy in pieces[a, d]:
-                copy.wait_recv()
-            add_rows(S[a].at[0, d], S[a].at[0, d], Q[a].at[d, 0])
-            add_rows(S[a].at[0, d], S[a].at[0, d], Q[a].at[d, 1])
-            if d:
-                last[a, d] = s.go(S[a].at[0, d], Z[a].at[d - 1], (b, z ^ d), Z[a].at[d - 1])
-
-    fold(1)
-    fold(2)
-    relay(1)
-    fold(3)
-    relay(2)
-    collect(1)
-    fold(0)
-    relay(3)
-    collect(2)
-    relay(0)
-    collect(3)
-    collect(0)
-    for a in (0, 1):
+            self.mine[d, e].wait()
+            self.other[d, e].wait_recv()
+            add_rows(self.S.at[e, d], self.S.at[e, d], self.C.at[e, d])
+            for copy in {3: self.halves[d], 1: self.ahead[d][1:], 2: self.ahead[d][:1], 0: []}[e]:
+                copy.go()
+
+    def relay(self, d):
+        for i, e in ((0, 2), (1, 1)):
+            self.halves[d][i].wait_recv()
+            part = half(self.S.at[e, d], i)
+            add_rows(part, part, self.H.at[d, i])
+            self.rest[d][i].go()
+
+    def collect(self, d):
+        for copy in self.ahead[d] + self.rest[d]:
+            copy.wait_recv()
+        for i in (0, 1):
+            add_rows(self.S.at[0, d], self.S.at[0, d], self.Q.at[d, i])
+        if d:
+            self.last[d].go()
+
+    def total(self):
         for d in (1, 2, 3):
-            last[a, d].wait_recv()
-
-        @pl.loop(0, O[a].shape[0] // 16)
-        def _(i, a=a):
+            self.last[d].wait_recv()
+        S, Z, out = self.S, self.Z, self.out
+
+        @pl.loop(0, out.shape[0] // 16)
+        def _(i):
             rows = pl.ds(pl.multiple_of(i * 16, 16), 16)
-            total = S[a][0, 0, rows, :].astype(HIGH)
+            total = S[0, 0, rows, :].astype(HIGH)
             for d in range(3):
-                total = total + Z[a][d, rows, :].astype(HIGH)
-            O[a][rows, :] = total
-
-    s.drain()
-
-
-def reduce(g1, g2):
-    shapes = [g1.shape[2:], g2.shape[2:]]
-    scratch = []
-    for lead, cut in (((4, 4), 1), ((4, 4), 1), ((4, 2), 2), ((4, 2), 1), ((3,), 1)):
-        for rows, columns in shapes:
-            scratch.append(pltpu.VMEM((*lead, rows // cut, columns), LOW))
-    return pl.pallas_call(
-        reduce_kernel,
-        out_shape=tuple(jax.ShapeDtypeStruct(s, HIGH) for s in shapes),
-        in_specs=in_hbm(2),
-        out_specs=(pl.BlockSpec(memory_space=pltpu.VMEM),) * 2,
-        scratch_shapes=scratch + pair_of_semaphores(80) + [pltpu.SemaphoreType.DMA((32,))],
-        compiler_params=pltpu.CompilerParams(
-            collective_id=2, has_side_effects=True, vmem_limit_bytes=VMEM_LIMIT
-        ),
-        name="reduce",
-    )(g1, g2)
+                total = total + Z[d, rows, :].astype(HIGH)
+            out[rows, :] = total
+
+    @staticmethod
+    def scratch(rows, columns):
+        lead = (((4, 4), 1), ((4, 4), 1), ((4, 2), 2), ((4, 2), 1), ((3,), 1))
+        shapes = [pltpu.VMEM((*n, rows // cut, columns), LOW) for n, cut in lead]
+        return shapes + [pltpu.SemaphoreType.DMA((16,))]
+
+    COPIES = 16 + 4 * 6 + 3
 
 
 def attend_kernel(qh_ref, kh_ref, v_ref, out_ref, lse_ref):
@@ -606,6 +588,96 @@
         compiler_params=pltpu.CompilerParams(vmem_limit_bytes=VMEM_LIMIT),
         name="attend_back",
     )(qh, o, g, lse, kh, v)
+
+
+def back_kernel(
+    d_att, qh, kh, v, att, lse, g1, dq, dk, dv, o1, grads, acc, delta, C, S, H, Q, Z, lsem, send, recv
+):
+    b, z = position()
+    blocks, slots, rows, _ = v.shape
+    count = slots * rows
+    greet([(b ^ d, z) for d in range(1, 8)] + [(b, z ^ d) for d in (1, 2, 3)])
+    s = Sender(send, recv)
+    arriving = [
+        s.go(d_att.at[b ^ d], grads.at[b], (b ^ d, z), grads.at[b ^ d]) for d in range(1, 8)
+    ]
+    sums = Reducer(s, g1, o1, C, S, H, Q, Z, lsem)
+    sums.start()
+    grads[b] = d_att[b]
+    sums.fold(1)
+    sums.fold(2)
+    for copy in arriving:
+        copy.wait_recv()
+
+    def grad_rows(slot):
+        part = pl.ds(pl.multiple_of(slot * rows, rows), rows)
+        return rows_of(grads[:, part])
+
+    events = {
+        1: (sums.relay, 1),
+        3: (sums.fold, 3),
+        4: (sums.relay, 2),
+        5: (sums.collect, 1),
+        6: (sums.fold, 0),
+        8: (sums.relay, 3),
+        9: (sums.collect, 2),
+        11: (sums.relay, 0),
+        13: (sums.collect, 3),
+    }
+
+    @pl.loop(0, blocks * slots)
+    def _(step):
+        slot, tile = step // blocks, step % blocks
+        slot_grads = grad_rows(slot)
+
+        @pl.when(tile == 0)
+        def _():
+            acc[...] = jnp.zeros_like(acc)
+            delta[...] = row_products(rows_of(att[:, slot]), slot_grads)
+
+        dk[tile, slot], dv[tile, slot] = attend_back_tile(
+            [rows_of(qh[head, :, slot]) for head in (0, 1)],
+            [kh[head, tile, slot] for head in (0, 1)],
+            v[tile, slot],
+            slot_grads,
+            lse[slot],
+            delta[...],
+            acc,
+        )
+
+        @pl.when(tile == blocks - 1)
+        def _():
+            dq[:, slot] = (acc[...].T * 0.125).astype(LOW).reshape(blocks, rows, 128)
+
+        for at, (event, what) in events.items():
+            pl.when(step == at)(functools.partial(event, what))
+
+    sums.collect(0)
+    sums.total()
+    s.drain()
+
+
+def back(d_att, qh, kh, v, att, lse, g1):
+    blocks, slots, rows, lanes = v.shape
+    shape = jax.ShapeDtypeStruct
+    vmem = pl.BlockSpec(memory_space=pltpu.VMEM)
+    return pl.pallas_call(
+        back_kernel,
+        out_shape=(shape(v.shape, LOW),) * 3 + (shape(g1.shape[2:], HIGH),),
+        in_specs=[vmem] * 6 + in_hbm(1),
+        out_specs=(vmem,) * 4,
+        scratch_shapes=[
+            pltpu.VMEM(d_att.shape, LOW),
+            pltpu.VMEM((lanes, blocks * rows), HIGH),
+            pltpu.VMEM((8, blocks * rows), HIGH),
+        ]
+        + Reducer.scratch(*g1.shape[2:])
+        + pair_of_semaphores(7 + Reducer.COPIES),
+        compiler_params=pltpu.CompilerParams(
+            collective_id=2, has_side_effects=True, vmem_limit_bytes=VMEM_LIMIT
+        ),
+        name="back",
+    )(d_att, qh, kh, v, att, lse, g1)
 
 
 def normalize(values):
@@ -805,9 +877,11 @@
     d_first,
     small,
     x_hbm,
+    g2,
     tok_out,
     in_out,
     small_out,
+    o2,
     x,
     sent,
     C,
@@ -821,6 +895,12 @@
     M,
     N,
     T,
+    C2,
+    S2,
+    H2,
+    Q2,
+    Z2,
+    lsem2,
     send,
     recv,
     lsem,
@@ -836,6 +916,7 @@
         loads.append(load)
     greet([(b ^ d, z) for d in range(1, 8)] + [(b, z ^ d) for d in (1, 2, 3)])
     s = Sender(send, recv)
+    sums = Reducer(s, g2, o2, C2, S2, H2, Q2, Z2, lsem2)
     small_in = [
         s.go(small.at[b ^ d], M.at[d - 1], (b ^ d, z), M.at[d - 1]) for d in range(1, 8)
     ]
@@ -850,6 +931,9 @@
     for e in (3, 1, 2, 0):
         sent[e] = piece(b ^ 1 ^ (2 * e)).astype(LOW)
         other[e] = s.go(sent.at[e], C.at[e], to_core, C.at[e])
+        if e == 3:
+            sums.start()
+    sums.fold(1)
 
     def own(e):
         mine = piece(b ^ (2 * e))
@@ -861,11 +945,15 @@
         s.go(half(S.at[3], 0), H.at[0], to_x, H.at[0]),
         s.go(half(S.at[3], 1), H.at[1], to_y, H.at[1]),
     ]
+    sums.fold(2)
     S[2] = own(2).astype(LOW)
     pieces = [s.go(half(S.at[2], 1), half(Q.at[1], 1), to_y, half(Q.at[1], 1))]
+    sums.relay(1)
     S[1] = own(1).astype(LOW)
     pieces.append(s.go(half(S.at[1], 0), half(Q.at[0], 0), to_x, half(Q.at[0], 0)))
     A[...] = own(0) + d_first[...]
+    sums.fold(3)
+    sums.relay(2)
 
     total = jnp.zeros((width, w.shape[1]), HIGH)
     for i in range(blocks):
@@ -876,6 +964,8 @@
         s.go(D.at[b ^ d], R.at[b], (b ^ d, z), R.at[b ^ d]) for d in range(1, 8)
     ]
     R[b] = D[b]
+    sums.collect(1)
+    sums.fold(0)
 
     halves[0].wait_recv()
     part = half(S.at[2], 0)
@@ -886,17 +976,21 @@
     part[...] = part[...] + H[1]
     pieces.append(s.go(part, half(Q.at[0], 1), to_x, half(Q.at[0], 1)))
 
+    sums.relay(3)
+    sums.collect(2)
+
     N[...] = small[b]
     for i in range(7):
         small_in[i].wait_recv()
         N[...] += M[i]
     for row, ref in ((4, dq), (5, dv)):
-        sums = jnp.zeros((1, 128), HIGH)
+        whole = jnp.zeros((1, 128), HIGH)
         for i in range(blocks):
-            sums = sums + column_sum(ref[i].reshape(count, -1))
-        N[row : row + 1, 0:128] = sums
+            whole = whole + column_sum(ref[i].reshape(count, -1))
+        N[row : row + 1, 0:128] = whole
     small_z = [s.go(N, T.at[d - 1], (b, z ^ d), T.at[d - 1]) for d in (1, 2, 3)]
 
+    sums.relay(0)
     for copy in grads_in:
         copy.wait_recv()
     rows = R.shape[1] // 4
@@ -905,6 +999,7 @@
         return R.at[:, pl.ds(pl.multiple_of((z ^ d) * rows, rows), rows)]
 
     in_z = [s.go(share(d), Z.at[d - 1], (b, z ^ d), Z.at[d - 1]) for d in (1, 2, 3)]
+    sums.collect(3)
     for copy in small_z:
         copy.wait_recv()
     small_out[...] = ((N[...] + T[0]) + T[1]) + T[2]
@@ -916,10 +1011,12 @@
     for copy in pieces:
         copy.wait_recv()
     tok_out[...] = A[...] + Q[0].astype(HIGH) + Q[1].astype(HIGH)
+    sums.collect(0)
+    sums.total()
     s.drain()
 
 
-def finish(dq, dk, dv, w, d_first, small, x):
+def finish(dq, dk, dv, w, d_first, small, x, g2):
     count, width = d_first.shape
     blocks, columns = dq.shape[0], w.shape[1]
     share = width // (4 * blocks)
@@ -932,9 +1029,10 @@
             shape((count, width), HIGH),
             shape((blocks, share, columns), HIGH),
             shape(small.shape[1:], HIGH),
+            shape(g2.shape[2:], HIGH),
         ),
-        in_specs=[vmem] * 6 + in_hbm(1),
-        out_specs=(vmem,) * 3,
+        in_specs=[vmem] * 6 + in_hbm(2),
+        out_specs=(vmem,) * 4,
         scratch_shapes=[
             low(blocks, count, width),
             low(4, count, width),
@@ -950,13 +1048,14 @@
             pltpu.VMEM(small.shape[1:], HIGH),
             pltpu.VMEM((3, *small.shape[1:]), HIGH),
         ]
-        + pair_of_semaphores(32)
+        + Reducer.scratch(*g2.shape[2:])
+        + pair_of_semaphores(32 + Reducer.COPIES)
         + [pltpu.SemaphoreType.DMA((blocks,))],
         compiler_params=pltpu.CompilerParams(
             collective_id=3, has_side_effects=True, vmem_limit_bytes=VMEM_LIMIT
         ),
         name="finish",
-    )(dq, dk, dv, w, d_first, small, x)
+    )(dq, dk, dv, w, d_first, small, x, g2)
 
 
 def swap(pieces):
@@ -1054,25 +1153,25 @@
     )
     output, d_first, d_att, sums, d_hidden, grad_both, grad_reduce = middle_out
     output = output.reshape(slots, rows, width)
-    g = swap(d_att)
     if fast:
-        sum_both, sum_reduce = reduce(
-            grad_both.reshape(n_blk, n_dp, shard, -1), grad_reduce.reshape(n_blk, n_dp, -1, width)
+        dq, dk, dv, sum_both = back(
+            d_att, qh, kh, v, att, lse, grad_both.reshape(n_blk, n_dp, shard, -1)
         )
+        grad_reduce = grad_reduce.reshape(n_blk, n_dp, -1, width)
     else:
         sum_both = lax.psum_scatter(grad_both, BOTH, scatter_dimension=0, tiled=True).astype(HIGH)
         sum_reduce = lax.psum_scatter(grad_reduce, BOTH, scatter_dimension=0, tiled=True)
         sum_reduce = sum_reduce.astype(HIGH)
-
-    g = by_slot(g, slots)
-    dq, dk, dv = attend_back(qh, att, g, lse, kh, v)
+        dq, dk, dv = attend_back(qh, att, by_slot(swap(d_att), slots), lse, kh, v)
     small_rows = sums[:6].reshape(6, shards, part).transpose(1, 0, 2).reshape(shards, 6 * part)
     small_rows = jnp.concatenate([small_rows, d_hidden.reshape(shards, -1)], axis=1)
     if fast:
         lanes = small_rows.shape[1]
         small_rows = small_rows.reshape(n_blk, n_dp, lanes)
         small_rows = jnp.pad(small_rows, ((0, 0), (0, 4), (0, 3 * held - lanes)))
-        grad_tokens, d_input, small_sum = finish(dq, dk, dv, W, d_first, small_rows, X)
+        grad_tokens, d_input, small_sum, sum_reduce = finish(
+            dq, dk, dv, W, d_first, small_rows, X, grad_reduce
+        )
         grad_input = d_input.reshape(n_blk, shard, 3, held).transpose(1, 2, 0, 3)
         grad_input = grad_input.reshape(shard, 3 * width)
         me_dp = lax.axis_index("dp")

time: 454 us -> 411 us (0.905)
  Pallas kernels: 423 us -> 385 us
    pallas_call x2 -> x1, Pallas kernels: 149 us -> 82.9 us  [back(): pl.pallas_call(back_kernel, out_shape=(shape(v.shape, LOW),) * 3 + (shape...]
    pallas_call x1, Pallas kernels: 71.6 us -> 100 us  [finish(): pl.pallas_call(finish_kernel, out_shape=(shape((count, width), HIGH), sha...]
  transfers between devices with their start and end apart: 1 -> 0, of which waited for: 0 -> 0; matrix products, arithmetic and copies ran while one was open for 1% -> 0% of each run, Pallas kernels for 21% -> 0%
where the time goes in v4:
time: 411 us; the launch traced here: 406 us
  Pallas kernels  385 us (94%)
  local copies, waits for them, and re-layouts  12.9 us (3%)
  other arithmetic  7.34 us (2%)
    pallas_call x1, Pallas kernels, front(): pl.pallas_call(front_kernel, out_shape=(shape(8, *x.shape), shape(4, *win...  150 us
    pallas_call x1, Pallas kernels, finish(): pl.pallas_call(finish_kernel, out_shape=(shape((count, width), HIGH), sha...  100 us
    pallas_call x1, Pallas kernels, back(): pl.pallas_call(back_kernel, out_shape=(shape(v.shape, LOW),) * 3 + (shape...  82.9 us
    pallas_call x1, Pallas kernels, middle(): pl.pallas_call(functools.partial(middle_kernel, chunk), out_shape=(shape(...  51.9 us

profile of v4, /device:TPU:0, one launch (start us, length us, event | category | flops | bytes accessed | tf_op | source)
XLA Modules:
  0.0 406.3 jit_solution(302421651415188749)
XLA Ops:
  0.7 0.8 fusion.2
  1.5 2.3 fusion.1.x
  3.9 0.1 copy.43
  4.0 0.2 reshape.137
  4.1 0.1 reshape.138
  4.2 0.1 reshape.139
  4.4 0.7 pad_maximum_fusion.1.win
  5.2 0.7 pad_maximum_fusion.w1
  5.9 150.0 %front.1 = (bf16[8,528,1024]{2,1,0:T(8,128)(2,1)}, bf16[4,8,48,384]{3,2,1,0:T(8,128)(2,1)}, bf16[8,4,32,5120]{3,2,1,0:T(8,128)(2,1)}, bf16[8,4,128,1024]{3,2,1,0...) custom-call(bf16[528,1024]{1,0:T(8,128)(2,1)} %fusion.1.x, ...), custom_call_target="tpu_custom_call" | custom-call | tf_op jit(solution)/shard_map/front/pallas_call | solution.py:374
  155.9 1.0 slice.56
  156.9 0.1 reshape.153
  157.1 0.7 reshape.151.par_ref
  157.8 0.6 slice_convert_fusion.1
  158.4 51.9 %middle.1 = (bf16[512,1024]{1,0:T(8,128)(2,1)}, f32[512,1024]{1,0:T(8,128)}, bf16[8,512,128]{2,1,0:T(8,128)(2,1)}, f32[8,1024]{1,0:T(8,128)}, f32[1,4096]{1,0:T(...) custom-call(bf16[512,1024]{1,0:T(8,128)(2,1)} %bitcast.45, ...), custom_call_target="tpu_custom_call" | custom-call | tf_op jit(solution)/shard_map/middle/pallas_call | solution.py:840
  210.3 0.8 reshape.146
  211.2 0.1 concatenate.33
  211.3 1.4 select_maximum_fusion.small
  212.8 82.9 %back.1 = (bf16[8,2,256,128]{3,2,1,0:T(8,128)(2,1)}, bf16[8,2,256,128]{3,2,1,0:T(8,128)(2,1)}, bf16[8,2,256,128]{3,2,1,0:T(8,128)(2,1)}, f32[32,5120]{1,0:T(8,128)}) custom-call(bf16[8,512,128]{2,1,0:T(8,128)(2,1)} %get-tuple-element.52.d_att, bf16[2,8,2,256,128]{4,3,2,1,0:T(8,128)(2,1)} %get-tuple-element.53.qh, ...), custom_call_target="tpu_custom_call" | custom-call | tf_op jit(solution)/shard_map/back/pallas_call | solution.py:664
  295.7 100.5 %finish.1 = (f32[512,1024]{1,0:T(8,128)}, f32[8,32,384]{2,1,0:T(8,128)}, f32[8,384]{1,0:T(8,128)}, f32[128,1024]{1,0:T(8,128)}) custom-call(bf16[8,2,256,128]{3,2,1,0:T(8,128)(2,1)} %get-tuple-element.59.dq, bf16[8,2,256,128]{3,2,1,0:T(8,128)(2,1)} %get-tuple-element.60.dk, bf16[8,2,256,128]{3,2,1,0:T(8,128)(2,1)} %get-tuple-element.61.dv, ...), custom_call_target="tpu_custom_call" | custom-call | tf_op jit(solution)/shard_map/finish/pallas_call | solution.py:1026
  396.2 1.5 dynamic-slice_bitcast_fusion
  397.6 0.1 slice.65
  397.7 0.8 constant_dynamic-slice_fusion
  398.5 0.6 pad_maximum_fusion.2
  399.1 1.1 reshape.149
  400.2 0.2 copy.32
  400.5 0.8 copy.42
  401.3 0.7 dynamic-slice_reduce_fusion.1
  402.0 0.6 slice.63
  402.6 0.8 slice.61
  403.5 0.7 slice.60
  404.1 1.3 copy.49
  405.5 0.8 copy.50
  (30 shorter events, 0.4 us)
Async XLA Ops:
  0.6 3.2 copy-start.4
  0.7 3.5 copy-start.8
  0.7 3.6 copy-start.6
  0.7 3.6 copy-start.7
  0.7 4.5 %copy-start.5 = (bf16[32,1024]{1,0:T(8,128)(2,1)S(1)}, bf16[32,1024]{1,0:T(8,128)(2,1)}, u32[]{:S(2)}) copy-start(bf16[32,1024]{1,0:T(8,128)(2,1)} %param.15) | copy-start | bytes 196612
  0.7 4.5 %copy-start.3 = (bf16[32,4096]{1,0:T(8,128)(2,1)S(1)}, bf16[32,4096]{1,0:T(8,128)(2,1)}, u32[]{:S(2)}) copy-start(bf16[32,4096]{1,0:T(8,128)(2,1)} %param.16) | copy-start | bytes 786436
  295.7 107.0 %copy-start.1 = (f32[32,5120]{1,0:T(8,128)S(1)}, f32[32,5120]{1,0:T(8,128)}, u32[]{:S(2)}) copy-start(f32[32,5120]{1,0:T(8,128)} %get-tuple-element.70) | copy-start | bytes 1966084
  396.2 8.0 %copy-start = (f32[512,1024]{1,0:T(8,128)S(1)}, f32[512,1024]{1,0:T(8,128)}, u32[]{:S(2)}) copy-start(f32[512,1024]{1,0:T(8,128)} %get-tuple-element.68) | copy-start | bytes 6291460
  404.1 1.4 copy-start.2

commit v5 on v4

--- a/solution.py
+++ b/solution.py
@@ -129,11 +129,11 @@
     w1,
     w2,
     X_out,
-    raw,
     W1,
     W2,
     rows_att,
     wfull,
+    small,
     qh,
     kh,
     v,
@@ -170,71 +170,114 @@
     def token_core(src, bb):
         return s.plan(src, X.at[bb], to_core, X.at[bb ^ 1])
 
+    def to_z(d):
+        return b, z ^ d
+
+    def hops(F, src, zz):
+        near = [
+            s.plan(src, F.at[b, zz], to_x, F.at[bx, zz]),
+            s.plan(src, F.at[b, zz], to_y, F.at[by, zz]),
+        ]
+        one, two = half(F.at[bx, zz], 0), half(F.at[by, zz], 1)
+        far = [
+            s.plan(one, one, to_y, half(F.at[bd, zz], 0)),
+            s.plan(two, two, to_x, half(F.at[bd, zz], 1)),
+        ]
+        return near, far
+
+    def planes(F, src, bb):
+        pair = [s.plan(src, F.at[bb, z], to_z(d), F.at[bb, z ^ d]) for d in (1, 2)]
+        on = F.at[bb, z ^ 2]
+        return pair + [s.plan(on, on, to_z(1), F.at[bb, z ^ 3])]
+
+    def to_sibling(F, src, bb, zz):
+        return s.plan(src, F.at[bb, zz], to_core, F.at[bb ^ 1, zz])
+
+    places = (b, bx, by, bd)
+    z1 = planes(W1, w1, b)
+    hop1 = [hops(W1, W1.at[b, z ^ d] if d else w1, z ^ d) for d in range(4)]
+    hop2 = hops(W2, w2, z)
+    z2 = [planes(W2, W2.at[bb, z] if i else w2, bb) for i, bb in enumerate(places)]
+    core1, core2 = (
+        {
+            (i, d): to_sibling(F, F.at[bb, z ^ d] if i or d else own, bb, z ^ d)
+            for i, bb in enumerate(places)
+            for d in range(4)
+        }
+        for F, own in ((W1, w1), (W2, w2))
+    )
+
+    def start(*copies):
+        for copy in copies:
+            copy.go()
+
+    def first(d):
+        if d:
+            z1[d - 1].wait_recv()
+        if d == 2:
+            z1[2].go()
+        start(*hop1[d][0], core1[0, d])
+
+    def second(d):
+        near, far = hop1[d]
+        for i in (0, 1):
+            near[i].wait_recv()
+            start(far[i], core1[1 + i, d])
+
+    def third(d):
+        for copy in hop1[d][1]:
+            copy.wait_recv()
+        core1[3, d].go()
+
+    def spread(i):
+        start(z2[i][0], z2[i][1], core2[i, 0])
+
+    def second2():
+        near, far = hop2
+        for i in (0, 1):
+            near[i].wait_recv()
+            far[i].go()
+            spread(1 + i)
+
+    def third2():
+        for copy in hop2[1]:
+            copy.wait_recv()
+        spread(3)
+
+    def arrive2(i):
+        z2[i][1].wait_recv()
+        start(z2[i][2], core2[i, 2])
+        z2[i][0].wait_recv()
+        core2[i, 1].go()
+
+    def last2(i):
+        z2[i][2].wait_recv()
+        core2[i, 3].go()
+
     columns = [
         s.go(win.at[b ^ d], W.at[z, b], (b ^ d, z), W.at[z, b ^ d]) for d in range(1, 8)
     ]
+    start(*hop2[0])
     token_x = s.go(x, X.at[b], to_x, X.at[bx])
     token_y = s.go(x, X.at[b], to_y, X.at[by])
     token_c = token_core(x, b)
     token_c.go()
-
-    own, full = (w1, w2), (W1, W2)
-    ways = {}
-    for a in (0, 1):
-        F = full[a]
-        for d in range(4):
-            zz = z ^ d
-            src = F.at[b, zz] if d else own[a]
-            way = {}
-            if d:
-                way["z"] = s.plan(own[a], F.at[b, z], (b, zz), F.at[b, zz])
-            way["x"] = s.plan(src, F.at[b, zz], to_x, F.at[bx, zz])
-            way["y"] = s.plan(src, F.at[b, zz], to_y, F.at[by, zz])
-            piece = half(F.at[bx, zz], 0)
-            way["xy"] = s.plan(piece, piece, to_y, half(F.at[bd, zz], 0))
-            piece = half(F.at[by, zz], 1)
-            way["yx"] = s.plan(piece, piece, to_x, half(F.at[bd, zz], 1))
-            way["core"] = [
-                s.plan(src if bb is b else F.at[bb, zz], F.at[bb, zz], to_core, F.at[bb ^ 1, zz])
-                for bb in (b, bx, by, bd)
-            ]
-            ways[a, d] = way
-    for a in (0, 1):
-        for d in (1, 2, 3):
-            ways[a, d]["z"].go()
-
-    def first(d, a):
-        way = ways[a, d]
-        if d:
-            way["z"].wait_recv()
-        way["x"].go()
-        way["y"].go()
-        way["core"][0].go()
-
-    def second(d, a):
-        way = ways[a, d]
-        way["x"].wait_recv()
-        way["xy"].go()
-        way["core"][1].go()
-        way["y"].wait_recv()
-        way["yx"].go()
-        way["core"][2].go()
-
-    def third(d, a):
-        way = ways[a, d]
-        way["xy"].wait_recv()
-        way["yx"].wait_recv()
-        way["core"][3].go()
-
-    def both(stage, d):
-        stage(d, 0)
-        stage(d, 1)
-
-    both(first, 0)
+    start(z1[0], z1[1])
+    spread(0)
+    first(0)
     for copy in columns:
         copy.wait_recv()
     locs[0].wait()
-    columns = [s.go(W.at[z], W.at[z], (b, z ^ d), W.at[z ^ d]) for d in (1, 2, 3)]
+    for i in range(8):
+        small[z, i : i + 1] = W[z, i, 32:33]
+    trimmed = lambda zz: W.at[zz, :, pl.ds(0, 32)]
+    columns, vectors = (
+        [s.plan(at(z), at(z), to_z(d), at(z ^ d)) for d in (1, 2)]
+        + [s.plan(at(z ^ 2), at(z ^ 2), to_z(1), at(z ^ 3))]
+        for at in (trimmed, lambda zz: small.at[zz])
+    )
+    start(*columns[:2], *vectors[:2])
+    second2()
     token_x.wait_recv()
     piece = half(X.at[bx], 0)
     token_one = s.go(piece, piece, to_y, half(X.at[bd], 0))
@@ -246,19 +289,27 @@
     token_yc = token_core(X.at[by], by)
     token_yc.go()
     token_dc = token_core(X.at[bd], bd)
-    both(first, 1)
-    for copy in columns:
+    first(2)
+    first(1)
+    columns[1].wait_recv()
+    columns[2].go()
+    vectors[1].wait_recv()
+    vectors[2].go()
+    third2()
+    for copy in (columns[0], columns[2], vectors[0], vectors[2]):
         copy.wait_recv()
-    raw_copy = pltpu.make_async_copy(W, raw, lsem.at[4])
-    raw_copy.start()
     for i in range(8):
         for j in range(4):
             at = (i * 4 + j) * 32
             wfull[at : at + 32] = W[j, i, 0:32]
-    bias = [
-        jnp.concatenate([W[j, b, 32:33, at : at + 32] for j in range(4)], axis=1).astype(HIGH)
-        for at in (64, 96)
-    ]
+    chosen = lax.broadcasted_iota(jnp.int32, (16, 128), 0) == b
+    bias = [[], []]
+    for j in range(4):
+        row = jnp.where(chosen, small[j, :, 0:128].astype(HIGH), 0.0)
+        row = jnp.sum(row, axis=0, keepdims=True)
+        bias[0].append(row[:, 64:96])
+        bias[1].append(row[:, 96:128])
+    bias = [jnp.concatenate(parts, axis=1) for parts in bias]
 
     def mix(i):
         pltpu.make_async_copy(X.at[i], X_out.at[i], osem.at[i]).start()
@@ -277,18 +328,18 @@
     mix(bx)
     token_xc.wait_recv()
     mix(bx ^ 1)
-    both(first, 2)
+    first(3)
     mix(by)
     token_yc.wait_recv()
     mix(by ^ 1)
     token_one.wait_recv()
     token_two.wait_recv()
     token_dc.go()
+    arrive2(0)
     mix(bd)
-    both(first, 3)
     token_dc.wait_recv()
     mix(bd ^ 1)
-    both(second, 0)
+    second(0)
 
     def piece_of(slot):
         return pl.ds(pl.multiple_of(slot * rows, rows), rows)
@@ -308,7 +359,22 @@
             att.at[b, slot], rows_att.at[b, piece_of(slot)], osem.at[8 + slot]
         )
 
-    events = {4: (second, 1, 0), 6: (second, 1, 1), 10: (second, 2, 0), 12: (second, 2, 1)}
+    events = {
+        0: (second, 1),
+        1: (arrive2, 1),
+        2: (arrive2, 2),
+        3: (second, 2),
+        4: (third, 0),
+        5: (second, 3),
+        6: (arrive2, 3),
+        8: (third, 1),
+        9: (last2, 0),
+        10: (third, 2),
+        12: (last2, 1),
+        13: (last2, 2),
+        14: (last2, 3),
+        15: (third, 3),
+    }
 
     @pl.loop(0, 8 * slots)
     def _(step):
@@ -330,13 +396,8 @@
         for at, (event, *what) in events.items():
             pl.when(step == at)(functools.partial(event, *what))
 
-    both(third, 0)
-    both(second, 3)
-    for d in (1, 2, 3):
-        both(third, d)
-    for way in ways.values():
-        for copy in way["core"]:
-            copy.wait_recv()
+    for copy in [*core1.values(), *core2.values()]:
+        copy.wait_recv()
     for slot in range(slots):
         keep_att(slot).wait()
         for d in range(1, 8):
@@ -353,7 +414,6 @@
     s.drain()
     for copy in locs[2:]:
         copy.wait()
-    raw_copy.wait()
     for i in range(8):
         pltpu.make_async_copy(X.at[i], X_out.at[i], osem.at[i]).wait()
 
@@ -375,11 +435,11 @@
         front_kernel,
         out_shape=(
             shape(8, *x.shape),
-            shape(4, *win.shape),
             shape(8, 4, *w1.shape),
             shape(8, 4, *w2.shape),
             shape(8, count, 128),
             shape(width, win.shape[2]),
+            shape(4, 16, win.shape[2]),
             shape(2, 8, slots, rows, 128),
             shape(2, 8, slots, rows, 128),
             shape(8, slots, rows, 128),
@@ -387,11 +447,11 @@
             jax.ShapeDtypeStruct((slots, 8, 8 * rows), HIGH),
         ),
         in_specs=in_hbm(4),
-        out_specs=tuple(in_hbm(5)) + (vmem,) * 6,
+        out_specs=tuple(in_hbm(4)) + (vmem,) * 7,
         scratch_shapes=[pltpu.VMEM((8, *x.shape), LOW), pltpu.VMEM((4, *win.shape), LOW)]
-        + pair_of_semaphores(100)
+        + pair_of_semaphores(116)
         + pair_of_semaphores(8 * slots)
-        + [pltpu.SemaphoreType.DMA((5,)), pltpu.SemaphoreType.DMA((8 + slots,))],
+        + [pltpu.SemaphoreType.DMA((4,)), pltpu.SemaphoreType.DMA((8 + slots,))],
         compiler_params=pltpu.CompilerParams(
             collective_id=1, has_side_effects=True, vmem_limit_bytes=VMEM_LIMIT
         ),
@@ -406,10 +466,21 @@
         out[rows, :] = one[rows, :] + two[rows, :]
 
 
+def sum_rows(out, *terms):
+    @pl.loop(0, out.shape[0] // 16)
+    def _(i):
+        rows = pl.ds(pl.multiple_of(i * 16, 16), 16)
+        total = terms[0][rows, :].astype(HIGH)
+        for term in terms[1:]:
+            total = total + term[rows, :].astype(HIGH)
+        out[rows, :] = total
+
+
 class Reducer:
-    ORDER = (1, 2, 3, 0)
-
-    def __init__(self, s, g, out, C, S, H, Q, Z, lsem):
+    ORDER = (3, 2, 1, 0)
+    COPIES = 16 + 4 * 6 + 3
+
+    def __init__(self, s, share, out, C, S, H, Q, Z, lsem):
         b, z = position()
         to_x, to_y, to_core = (b ^ 2, z), (b ^ 4, z), (b ^ 1, z)
         self.out, self.C, self.S, self.H, self.Q, self.Z = out, C, S, H, Q, Z
@@ -417,10 +488,10 @@
         for d in self.ORDER:
             for e in (3, 1, 2, 0):
                 self.mine[d, e] = pltpu.make_async_copy(
-                    g.at[b ^ (2 * e), z ^ d], S.at[e, d], lsem.at[d * 4 + e]
+                    share(b ^ (2 * e), z ^ d), S.at[e, d], lsem.at[d * 4 + e]
                 )
                 self.other[d, e] = s.plan(
-                    g.at[b ^ 1 ^ (2 * e), z ^ d], C.at[e, d], to_core, C.at[e, d]
+                    share(b ^ 1 ^ (2 * e), z ^ d), C.at[e, d], to_core, C.at[e, d]
                 )
 
             def send(e, part, to, where):
@@ -436,7 +507,8 @@
                 send(1, 1, to_x, half(Q.at[d, 0], 1)),
             ]
             if d:
-                self.last[d] = s.plan(S.at[0, d], Z.at[d - 1], (b, z ^ d), Z.at[d - 1])
+                to = (b, z ^ (2 if d == 2 else 1))
+                self.last[d] = s.plan(S.at[0, d], Z.at[d - 1], to, Z.at[d - 1])
 
     def start(self):
         for d in self.ORDER:
@@ -462,23 +534,19 @@
     def collect(self, d):
         for copy in self.ahead[d] + self.rest[d]:
             copy.wait_recv()
+        total = self.S.at[0, d]
         for i in (0, 1):
-            add_rows(self.S.at[0, d], self.S.at[0, d], self.Q.at[d, i])
+            add_rows(total, total, self.Q.at[d, i])
+        if d == 2:
+            self.last[3].wait_recv()
+            add_rows(total, total, self.Z.at[2])
         if d:
             self.last[d].go()
 
     def total(self):
-        for d in (1, 2, 3):
+        for d in (1, 2):
             self.last[d].wait_recv()
-        S, Z, out = self.S, self.Z, self.out
-
-        @pl.loop(0, out.shape[0] // 16)
-        def _(i):
-            rows = pl.ds(pl.multiple_of(i * 16, 16), 16)
-            total = S[0, 0, rows, :].astype(HIGH)
-            for d in range(3):
-                total = total + Z[d, rows, :].astype(HIGH)
-            out[rows, :] = total
+        sum_rows(self.out, self.S.at[0, 0], self.Z.at[0], self.Z.at[1])
 
     @staticmethod
     def scratch(rows, columns):
@@ -486,7 +554,83 @@
         shapes = [pltpu.VMEM((*n, rows // cut, columns), LOW) for n, cut in lead]
         return shapes + [pltpu.SemaphoreType.DMA((16,))]
 
-    COPIES = 16 + 4 * 6 + 3
+
+class ReducerAlongZ:
+    COPIES = 16 + 4 * 3 + 6
+
+    def __init__(self, s, share, out, C, S, H, Q, Z, lsem):
+        b, z = position()
+        to_x, to_y, to_core = (b ^ 2, z), (b ^ 4, z), (b ^ 1, z)
+        self.out, self.C, self.S, self.H, self.Q, self.Z = out, C, S, H, Q, Z
+        self.mine, self.other, self.along = {}, {}, {}
+        for e in (3, 1, 2, 0):
+            for d in (3, 2, 1, 0):
+                self.mine[e, d] = pltpu.make_async_copy(
+                    share(b ^ (2 * e), z ^ d), S.at[e, d], lsem.at[d * 4 + e]
+                )
+                self.other[e, d] = s.plan(
+                    share(b ^ 1 ^ (2 * e), z ^ d), C.at[e, d], to_core, C.at[e, d]
+                )
+                if d:
+                    to = (b, z ^ (2 if d == 2 else 1))
+                    self.along[e, d] = s.plan(S.at[e, d], Z.at[e, d - 1], to, Z.at[e, d - 1])
+
+        def send(e, part, to, where):
+            return s.plan(half(S.at[e, 0], part), where, to, where)
+
+        self.halves = [send(3, 0, to_x, H.at[0]), send(3, 1, to_y, H.at[1])]
+        self.ahead = [
+            send(2, 1, to_y, half(Q.at[1], 1)),
+            send(1, 0, to_x, half(Q.at[0], 0)),
+        ]
+        self.rest = [
+            send(2, 0, to_y, half(Q.at[1], 0)),
+            send(1, 1, to_x, half(Q.at[0], 1)),
+        ]
+
+    def start(self):
+        for at in self.mine:
+            self.mine[at].start()
+            self.other[at].go()
+
+    def fold(self, e):
+        for d in (3, 1, 2, 0):
+            self.mine[e, d].wait()
+            self.other[e, d].wait_recv()
+            add_rows(self.S.at[e, d], self.S.at[e, d], self.C.at[e, d])
+            if d in (1, 3):
+                self.along[e, d].go()
+
+    def relay(self, e):
+        self.along[e, 3].wait_recv()
+        add_rows(self.S.at[e, 2], self.S.at[e, 2], self.Z.at[e, 2])
+        self.along[e, 2].go()
+
+    def collect(self, e):
+        total = self.S.at[e, 0]
+        for d in (1, 2):
+            self.along[e, d].wait_recv()
+            add_rows(total, total, self.Z.at[e, d - 1])
+        for copy in {3: self.halves, 1: self.ahead[1:], 2: self.ahead[:1], 0: []}[e]:
+            copy.go()
+
+    def cross(self):
+        for i, e in ((0, 2), (1, 1)):
+            self.halves[i].wait_recv()
+            part = half(self.S.at[e, 0], i)
+            add_rows(part, part, self.H.at[i])
+            self.rest[i].go()
+
+    def total(self):
+        for copy in self.ahead + self.rest:
+            copy.wait_recv()
+        sum_rows(self.out, self.S.at[0, 0], self.Q.at[0], self.Q.at[1])
+
+    @staticmethod
+    def scratch(rows, columns):
+        lead = (((4, 4), 1), ((4, 4), 1), ((2,), 2), ((2,), 1), ((4, 3), 1))
+        shapes = [pltpu.VMEM((*n, rows // cut, columns), LOW) for n, cut in lead]
+        return shapes + [pltpu.SemaphoreType.DMA((16,))]
 
 
 def attend_kernel(qh_ref, kh_ref, v_ref, out_ref, lse_ref):
@@ -601,10 +745,10 @@
     arriving = [
         s.go(d_att.at[b ^ d], grads.at[b], (b ^ d, z), grads.at[b ^ d]) for d in range(1, 8)
     ]
-    sums = Reducer(s, g1, o1, C, S, H, Q, Z, lsem)
+    sums = Reducer(s, lambda bb, zz: g1.at[bb, zz], o1, C, S, H, Q, Z, lsem)
     sums.start()
     grads[b] = d_att[b]
-    sums.fold(1)
+    sums.fold(3)
     sums.fold(2)
     for copy in arriving:
         copy.wait_recv()
@@ -614,15 +758,15 @@
         return rows_of(grads[:, part])
 
     events = {
-        1: (sums.relay, 1),
-        3: (sums.fold, 3),
+        1: (sums.relay, 3),
+        3: (sums.fold, 1),
         4: (sums.relay, 2),
-        5: (sums.collect, 1),
+        5: (sums.collect, 3),
         6: (sums.fold, 0),
-        8: (sums.relay, 3),
+        8: (sums.relay, 1),
         9: (sums.collect, 2),
         11: (sums.relay, 0),
-        13: (sums.collect, 3),
+        13: (sums.collect, 1),
     }
 
     @pl.loop(0, blocks * slots)
@@ -895,15 +1039,10 @@
     M,
     N,
     T,
-    C2,
-    S2,
-    H2,
-    Q2,
-    Z2,
-    lsem2,
+    lsem,
     send,
     recv,
-    lsem,
+    *reducing,
 ):
     b, z = position()
     count, width = d_first.shape
@@ -916,7 +1055,10 @@
         loads.append(load)
     greet([(b ^ d, z) for d in range(1, 8)] + [(b, z ^ d) for d in (1, 2, 3)])
     s = Sender(send, recv)
-    sums = Reducer(s, g2, o2, C2, S2, H2, Q2, Z2, lsem2)
+    cut = o2.shape[0] // 2
+    lower, upper = pl.ds(0, cut), pl.ds(cut, cut)
+    sums = Reducer(s, lambda bb, zz: g2.at[bb, zz, lower], o2.at[lower], *reducing[:6])
+    late = ReducerAlongZ(s, lambda bb, zz: g2.at[bb, zz, upper], o2.at[upper], *reducing[6:])
     small_in = [
         s.go(small.at[b ^ d], M.at[d - 1], (b ^ d, z), M.at[d - 1]) for d in range(1, 8)
     ]
@@ -932,8 +1074,12 @@
         sent[e] = piece(b ^ 1 ^ (2 * e)).astype(LOW)
         other[e] = s.go(sent.at[e], C.at[e], to_core, C.at[e])
         if e == 3:
+            late.start()
+        if e == 1:
             sums.start()
-    sums.fold(1)
+    late.fold(3)
+    sums.fold(3)
+    late.fold(1)
 
     def own(e):
         mine = piece(b ^ (2 * e))
@@ -945,15 +1091,21 @@
         s.go(half(S.at[3], 0), H.at[0], to_x, H.at[0]),
         s.go(half(S.at[3], 1), H.at[1], to_y, H.at[1]),
     ]
+    late.relay(3)
+    late.fold(2)
     sums.fold(2)
     S[2] = own(2).astype(LOW)
     pieces = [s.go(half(S.at[2], 1), half(Q.at[1], 1), to_y, half(Q.at[1], 1))]
-    sums.relay(1)
+    sums.relay(3)
+    late.fold(0)
+    late.relay(1)
     S[1] = own(1).astype(LOW)
     pieces.append(s.go(half(S.at[1], 0), half(Q.at[0], 0), to_x, half(Q.at[0], 0)))
     A[...] = own(0) + d_first[...]
-    sums.fold(3)
+    sums.fold(1)
     sums.relay(2)
+    late.relay(2)
+    late.collect(3)
 
     total = jnp.zeros((width, w.shape[1]), HIGH)
     for i in range(blocks):
@@ -964,8 +1116,9 @@
         s.go(D.at[b ^ d], R.at[b], (b ^ d, z), R.at[b ^ d]) for d in range(1, 8)
     ]
     R[b] = D[b]
-    sums.collect(1)
+    sums.collect(3)
     sums.fold(0)
+    late.relay(0)
 
     halves[0].wait_recv()
     part = half(S.at[2], 0)
@@ -976,8 +1129,10 @@
     part[...] = part[...] + H[1]
     pieces.append(s.go(part, half(Q.at[0], 1), to_x, half(Q.at[0], 1)))
 
-    sums.relay(3)
+    sums.relay(1)
+    late.collect(1)
     sums.collect(2)
+    late.collect(2)
 
     N[...] = small[b]
     for i in range(7):
@@ -991,6 +1146,7 @@
     small_z = [s.go(N, T.at[d - 1], (b, z ^ d), T.at[d - 1]) for d in (1, 2, 3)]
 
     sums.relay(0)
+    late.cross()
     for copy in grads_in:
         copy.wait_recv()
     rows = R.shape[1] // 4
@@ -999,7 +1155,7 @@
         return R.at[:, pl.ds(pl.multiple_of((z ^ d) * rows, rows), rows)]
 
     in_z = [s.go(share(d), Z.at[d - 1], (b, z ^ d), Z.at[d - 1]) for d in (1, 2, 3)]
-    sums.collect(3)
+    sums.collect(1)
     for copy in small_z:
         copy.wait_recv()
     small_out[...] = ((N[...] + T[0]) + T[1]) + T[2]
@@ -1011,8 +1167,10 @@
     for copy in pieces:
         copy.wait_recv()
     tok_out[...] = A[...] + Q[0].astype(HIGH) + Q[1].astype(HIGH)
+    late.collect(0)
     sums.collect(0)
     sums.total()
+    late.total()
     s.drain()
 
 
@@ -1048,9 +1206,10 @@
             pltpu.VMEM(small.shape[1:], HIGH),
             pltpu.VMEM((3, *small.shape[1:]), HIGH),
         ]
-        + Reducer.scratch(*g2.shape[2:])
-        + pair_of_semaphores(32 + Reducer.COPIES)
-        + [pltpu.SemaphoreType.DMA((blocks,))],
+        + [pltpu.SemaphoreType.DMA((blocks,))]
+        + pair_of_semaphores(32 + Reducer.COPIES + ReducerAlongZ.COPIES)
+        + Reducer.scratch(g2.shape[2] // 2, width)
+        + ReducerAlongZ.scratch(g2.shape[2] // 2, width),
         compiler_params=pltpu.CompilerParams(
             collective_id=3, has_side_effects=True, vmem_limit_bytes=VMEM_LIMIT
         ),
@@ -1122,10 +1281,10 @@
         small = jnp.concatenate([small[None], jnp.zeros((15, small.shape[0]), LOW)], axis=0)
         small = jnp.broadcast_to(small, (n_blk, *small.shape))
         win = jnp.concatenate([columns, small], axis=1)
-        X, raw, W1, W2, rows_att, W, qh, kh, v, att, lse = front(
+        X, W1, W2, rows_att, W, small, qh, kh, v, att, lse = front(
             sent_tokens, win, both, reduce_weight, slots
         )
-        small = raw[:, :, shard].transpose(1, 0, 2).reshape(shards, 3 * held)
+        small = small[:, :n_blk].transpose(1, 0, 2).reshape(shards, 3 * held)
         W1, W2 = W1.reshape(width, -1), W2.reshape(hidden, width)
     else:
         X = lax.all_gather(sent_tokens, "blk")

time: 411 us -> 369 us (0.90)
  Pallas kernels: 385 us -> 342 us
    pallas_call x1, Pallas kernels: 150 us -> 131 us  [front(): pl.pallas_call(front_kernel, out_shape=(shape(8, *x.shape), shape(8, 4, *...]
    pallas_call x1, Pallas kernels: 100 us -> 83.3 us  [finish(): pl.pallas_call(finish_kernel, out_shape=(shape((count, width), HIGH), sha...]
    pallas_call x1, Pallas kernels: 82.9 us -> 76.6 us  [back(): pl.pallas_call(back_kernel, out_shape=(shape(v.shape, LOW),) * 3 + (shape...]
where the time goes in v5:
time: 369 us; the launch traced here: 364 us
  Pallas kernels  342 us (93%)
  local copies, waits for them, and re-layouts  12.7 us (3%)
  other arithmetic  7.34 us (2%)
    pallas_call x1, Pallas kernels, front(): pl.pallas_call(front_kernel, out_shape=(shape(8, *x.shape), shape(8, 4, *...  131 us
    pallas_call x1, Pallas kernels, finish(): pl.pallas_call(finish_kernel, out_shape=(shape((count, width), HIGH), sha...  83.3 us
    pallas_call x1, Pallas kernels, back(): pl.pallas_call(back_kernel, out_shape=(shape(v.shape, LOW),) * 3 + (shape...  76.6 us
    pallas_call x1, Pallas kernels, middle(): pl.pallas_call(functools.partial(middle_kernel, chunk), out_shape=(shape(...  51.9 us

profile of v5, /device:TPU:0, one launch (start us, length us, event | category | flops | bytes accessed | tf_op | source)
XLA Modules:
  0.0 363.6 jit_solution(15373389817111290240)
XLA Ops:
  0.7 0.8 fusion.2
  1.5 2.3 fusion.1.x
  3.9 0.1 copy.41
  4.0 0.2 reshape.137
  4.1 0.1 reshape.138
  4.2 0.1 reshape.139
  4.4 0.7 pad_maximum_fusion.1.win
  5.2 0.7 pad_maximum_fusion.w1
  5.9 130.6 %front.1 = (bf16[8,528,1024]{2,1,0:T(8,128)(2,1)}, bf16[8,4,32,5120]{3,2,1,0:T(8,128)(2,1)}, bf16[8,4,128,1024]{3,2,1,0:T(8,128)(2,1)}, bf16[8,512,128]{2,1,0:T(...) custom-call(bf16[528,1024]{1,0:T(8,128)(2,1)} %fusion.1.x, ...), custom_call_target="tpu_custom_call" | custom-call | tf_op jit(solution)/shard_map/front/pallas_call | solution.py:434
  136.5 0.7 slice_bitcast_fusion
  137.3 0.1 reshape.153
  137.4 0.7 reshape.151.par_ref
  138.2 0.6 slice_convert_fusion.1
  138.8 51.9 %middle.1 = (bf16[512,1024]{1,0:T(8,128)(2,1)}, f32[512,1024]{1,0:T(8,128)}, bf16[8,512,128]{2,1,0:T(8,128)(2,1)}, f32[8,1024]{1,0:T(8,128)}, f32[1,4096]{1,0:T(...) custom-call(bf16[512,1024]{1,0:T(8,128)(2,1)} %bitcast.42, ...), custom_call_target="tpu_custom_call" | custom-call | tf_op jit(solution)/shard_map/middle/pallas_call | solution.py:984
  190.7 0.8 reshape.146
  191.6 0.1 concatenate.33
  191.7 1.4 select_maximum_fusion.small
  193.1 76.6 %back.1 = (bf16[8,2,256,128]{3,2,1,0:T(8,128)(2,1)}, bf16[8,2,256,128]{3,2,1,0:T(8,128)(2,1)}, bf16[8,2,256,128]{3,2,1,0:T(8,128)(2,1)}, f32[32,5120]{1,0:T(8,128)}) custom-call(bf16[8,512,128]{2,1,0:T(8,128)(2,1)} %get-tuple-element.52.d_att, bf16[2,8,2,256,128]{4,3,2,1,0:T(8,128)(2,1)} %get-tuple-element.53.qh, ...), custom_call_target="tpu_custom_call" | custom-call | tf_op jit(solution)/shard_map/back/pallas_call | solution.py:808
  269.7 83.3 %finish.1 = (f32[512,1024]{1,0:T(8,128)}, f32[8,32,384]{2,1,0:T(8,128)}, f32[8,384]{1,0:T(8,128)}, f32[128,1024]{1,0:T(8,128)}) custom-call(bf16[8,2,256,128]{3,2,1,0:T(8,128)(2,1)} %get-tuple-element.59.dq, bf16[8,2,256,128]{3,2,1,0:T(8,128)(2,1)} %get-tuple-element.60.dk, bf16[8,2,256,128]{3,2,1,0:T(8,128)(2,1)} %get-tuple-element.61.dv, ...), custom_call_target="tpu_custom_call" | custom-call | tf_op jit(solution)/shard_map/finish/pallas_call | solution.py:1184
  353.0 1.5 dynamic-slice_bitcast_fusion
  354.5 0.1 slice.65
  354.6 0.8 constant_dynamic-slice_fusion
  355.3 0.6 pad_maximum_fusion.2
  355.9 1.1 reshape.149
  357.1 0.2 copy.32
  357.3 0.8 copy.40
  358.1 0.7 dynamic-slice_reduce_fusion.1
  358.8 0.6 slice.63
  359.5 0.8 slice.61
  360.3 0.7 slice.60
  361.0 1.3 copy.46
  362.4 0.8 copy.47
  (29 shorter events, 0.4 us)
Async XLA Ops:
  0.6 3.2 copy-start.4
  0.7 3.5 copy-start.8
  0.7 3.6 copy-start.6
  0.7 3.6 %copy-start.7 = (bf16[128]{0:T(256)(128)(2,1)S(1)}, bf16[128]{0:T(256)(128)(2,1)}, u32[]{:S(2)}) copy-start(bf16[128]{0:T(256)(128)(2,1)} %param.20) | copy-start | bytes 772
  0.7 4.5 %copy-start.5 = (bf16[32,1024]{1,0:T(8,128)(2,1)S(1)}, bf16[32,1024]{1,0:T(8,128)(2,1)}, u32[]{:S(2)}) copy-start(bf16[32,1024]{1,0:T(8,128)(2,1)} %param.15) | copy-start | bytes 196612
  0.7 4.5 %copy-start.3 = (bf16[32,4096]{1,0:T(8,128)(2,1)S(1)}, bf16[32,4096]{1,0:T(8,128)(2,1)}, u32[]{:S(2)}) copy-start(bf16[32,4096]{1,0:T(8,128)(2,1)} %param.16) | copy-start | bytes 786436
  269.7 89.8 %copy-start.1 = (f32[32,5120]{1,0:T(8,128)S(1)}, f32[32,5120]{1,0:T(8,128)}, u32[]{:S(2)}) copy-start(f32[32,5120]{1,0:T(8,128)} %get-tuple-element.70) | copy-start | bytes 1966084
  353.0 8.0 %copy-start = (f32[512,1024]{1,0:T(8,128)S(1)}, f32[512,1024]{1,0:T(8,128)}, u32[]{:S(2)}) copy-start(f32[512,1024]{1,0:T(8,128)} %get-tuple-element.68) | copy-start | bytes 6291460
  361.0 1.4 copy-start.2

commit v6 on v5

--- a/solution.py
+++ b/solution.py
@@ -27,6 +27,34 @@
 
 def product_tn(left, right):
     return lax.dot_general(left, right, (((0,), (0,)), ((), ())), preferred_element_type=HIGH)
+
+
+def normalize(values):
+    mean = jnp.mean(values, axis=-1, keepdims=True)
+    centred = values - mean
+    spread = jnp.mean(centred * centred, axis=-1, keepdims=True)
+    inverse = lax.rsqrt(spread + EPSILON)
+    return centred * inverse, inverse
+
+
+def normalize_back(grad, normal, inverse):
+    return inverse * (
+        grad
+        - jnp.mean(grad, axis=-1, keepdims=True)
+        - normal * jnp.mean(grad * normal, axis=-1, keepdims=True)
+    )
+
+
+def gelu_parts(u):
+    bell = jnp.exp(-0.5 * u * u)
+    t = 1.0 / (1.0 + (0.3275911 * 0.5**0.5) * jnp.abs(u))
+    poly = 1.061405429 * t - 1.453152027
+    poly = poly * t + 1.421413741
+    poly = poly * t - 0.284496736
+    poly = poly * t + 0.254829592
+    tail = 0.5 * poly * t * bell
+    below = jnp.where(u < 0.0, tail, 1.0 - tail)
+    return u * below, below + u * bell * 0.3989422804014327
 
 
 class Sender:
@@ -123,15 +151,32 @@
     )
 
 
+def spread_vectors(small, par, hid):
+    for i in range(8):
+        for j in range(4):
+            row = small[j, i : i + 1].astype(HIGH)
+            at = (i * 4 + j) * 32
+            for k in range(8):
+                par[k : k + 1, at : at + 32] = row[:, k * 32 : k * 32 + 32]
+            hid[:, at * 4 : at * 4 + 128] = row[:, 256:384]
+
+
 def front_kernel(
     x,
-    win,
-    w1,
+    segment,
+    present,
+    input_weight,
+    gains,
+    biases,
+    hidden_bias,
+    expand,
+    out_w_in,
     w2,
     X_out,
     W1,
     W2,
-    rows_att,
+    act_out,
+    slope_out,
     wfull,
     small,
     qh,
@@ -139,21 +184,34 @@
     v,
     att,
     lse,
+    branch_in,
+    n1,
+    r1,
+    normed_low,
+    par,
     X,
     W,
+    win,
+    w1,
+    rows_att,
+    w1v,
+    act,
+    slope,
+    hid,
     send,
     recv,
     asend,
     arecv,
     lsem,
     osem,
+    wsem,
+    csem,
 ):
     b, z = position()
     bx, by, bd, bc = b ^ 2, b ^ 4, b ^ 6, b ^ 1
     count = X.shape[1] - 16
+    hidden, width = expand.shape[1], x.shape[1]
     slots, rows = qh.shape[2:4]
-    greet([(b ^ d, z) for d in range(1, 8)] + [(b, z ^ d) for d in range(1, 4)])
-    s = Sender(send, recv)
     locs = []
 
     def local(src, dst):
@@ -161,10 +219,28 @@
         copy.start()
         locs.append(copy)
 
-    local(win.at[b], W.at[z, b])
-    local(x, X.at[b])
-    local(w1, W1.at[b, z])
+    local(x, X.at[b, pl.ds(0, count)])
+    local(expand, w1.at[:, pl.ds(0, hidden)])
+    local(out_w_in, w1.at[:, pl.ds(hidden, width)])
     local(w2, W2.at[b, z])
+    shard = input_weight.shape[0]
+    n = gains.shape[1]
+    win[...] = jnp.zeros_like(win)
+    for i in range(8):
+        for k in range(3):
+            at = k * width + i * 128
+            win[i, 0:shard, k * 128 : (k + 1) * 128] = input_weight[:, at : at + 128]
+    rows_small = [gains[k : k + 1] for k in range(2)] + [biases[k : k + 1] for k in range(6)]
+    line = jnp.concatenate(rows_small + [hidden_bias[...]], axis=1)
+    for i in range(8):
+        win[i, shard : shard + 16] = jnp.broadcast_to(line, (16, line.shape[1]))
+    W[z, b] = win[b]
+    codes = (segment[...] + 4 * (1 - present[...])).astype(HIGH).astype(LOW)
+    codes = jnp.concatenate([codes[k : k + 1] for k in range(slots)], axis=1)
+    X[b, pl.ds(count, 16), 0:count] = jnp.broadcast_to(codes, (16, count))
+    X[b, pl.ds(count, 16), count:width] = jnp.zeros((16, width - count), LOW)
+    greet([(b ^ d, z) for d in range(1, 8)] + [(b, z ^ d) for d in range(1, 4)])
+    s = Sender(send, recv)
     to_x, to_y, to_core = (bx, z), (by, z), (bc, z)
 
     def token_core(src, bb):
@@ -212,10 +288,8 @@
             copy.go()
 
     def first(d):
-        if d:
+        if d in (1, 3):
             z1[d - 1].wait_recv()
-        if d == 2:
-            z1[2].go()
         start(*hop1[d][0], core1[0, d])
 
     def second(d):
@@ -257,17 +331,17 @@
     columns = [
         s.go(win.at[b ^ d], W.at[z, b], (b ^ d, z), W.at[z, b ^ d]) for d in range(1, 8)
     ]
-    start(*hop2[0])
-    token_x = s.go(x, X.at[b], to_x, X.at[bx])
-    token_y = s.go(x, X.at[b], to_y, X.at[by])
-    token_c = token_core(x, b)
+    locs[0].wait()
+    token_x = s.go(X.at[b], X.at[b], to_x, X.at[bx])
+    token_y = s.go(X.at[b], X.at[b], to_y, X.at[by])
+    token_c = token_core(X.at[b], b)
     token_c.go()
+    for copy in locs[1:3]:
+        copy.wait()
+    local(w1, W1.at[b, z])
     start(z1[0], z1[1])
-    spread(0)
-    first(0)
     for copy in columns:
         copy.wait_recv()
-    locs[0].wait()
     for i in range(8):
         small[z, i : i + 1] = W[z, i, 32:33]
     trimmed = lambda zz: W.at[zz, :, pl.ds(0, 32)]
@@ -277,7 +351,7 @@
         for at in (trimmed, lambda zz: small.at[zz])
     )
     start(*columns[:2], *vectors[:2])
-    second2()
+    spread(0)
     token_x.wait_recv()
     piece = half(X.at[bx], 0)
     token_one = s.go(piece, piece, to_y, half(X.at[bd], 0))
@@ -289,19 +363,20 @@
     token_yc = token_core(X.at[by], by)
     token_yc.go()
     token_dc = token_core(X.at[bd], bd)
-    first(2)
-    first(1)
+    start(*hop2[0])
     columns[1].wait_recv()
     columns[2].go()
     vectors[1].wait_recv()
     vectors[2].go()
-    third2()
+    z1[1].wait_recv()
+    z1[2].go()
     for copy in (columns[0], columns[2], vectors[0], vectors[2]):
         copy.wait_recv()
     for i in range(8):
         for j in range(4):
             at = (i * 4 + j) * 32
             wfull[at : at + 32] = W[j, i, 0:32]
+    spread_vectors(small, par, hid)
     chosen = lax.broadcasted_iota(jnp.int32, (16, 128), 0) == b
     bias = [[], []]
     for j in range(4):
@@ -321,25 +396,27 @@
             kh[head, i] = keys[head].reshape(slots, rows, 128)
         v[i] = values.reshape(slots, rows, 128)
 
-    locs[1].wait()
     mix(b)
     token_c.wait_recv()
     mix(bc)
     mix(bx)
     token_xc.wait_recv()
     mix(bx ^ 1)
-    first(3)
     mix(by)
-    token_yc.wait_recv()
-    mix(by ^ 1)
     token_one.wait_recv()
     token_two.wait_recv()
     token_dc.go()
-    arrive2(0)
+    first(0)
+    first(2)
+    first(1)
+    second2()
+    first(3)
+    token_yc.wait_recv()
+    mix(by ^ 1)
     mix(bd)
     token_dc.wait_recv()
     mix(bd ^ 1)
-    second(0)
+    arrive2(0)
 
     def piece_of(slot):
         return pl.ds(pl.multiple_of(slot * rows, rows), rows)
@@ -360,21 +437,19 @@
         )
 
     events = {
-        0: (second, 1),
-        1: (arrive2, 1),
-        2: (arrive2, 2),
-        3: (second, 2),
-        4: (third, 0),
-        5: (second, 3),
-        6: (arrive2, 3),
-        8: (third, 1),
-        9: (last2, 0),
-        10: (third, 2),
-        12: (last2, 1),
-        13: (last2, 2),
-        14: (last2, 3),
-        15: (third, 3),
+        0: (second, 0),
+        1: (third2,),
+        2: (second, 2),
+        4: (second, 1),
+        5: (arrive2, 1),
+        6: (arrive2, 2),
+        7: (third, 0),
+        9: (second, 3),
+        10: (arrive2, 3),
+        12: (third, 2),
+        14: (third, 1),
     }
+    late_events = {1: (last2, 0), 3: (last2, 1), 5: (last2, 2), 7: (last2, 3)}
 
     @pl.loop(0, 8 * slots)
     def _(step):
@@ -396,13 +471,23 @@
         for at, (event, *what) in events.items():
             pl.when(step == at)(functools.partial(event, *what))
 
-    for copy in [*core1.values(), *core2.values()]:
+    third(3)
+    for copy in core1.values():
         copy.wait_recv()
+    locs[4].wait()
+    chunk = 512
+    steps = hidden // chunk
+
+    def load(c, size=chunk):
+        cols = pl.ds(pl.multiple_of(c * chunk, chunk), size)
+        return pltpu.make_async_copy(W1.at[:, :, :, cols], w1v.at[:, :, :, cols], wsem.at[c])
+
+    load(steps, width).start()
+    for c in range(steps):
+        load(c).start()
     for slot in range(slots):
         keep_att(slot).wait()
         for d in range(1, 8):
-            copy = send_att(slot, d)
-            copy.wait_send()
             pltpu.make_async_remote_copy(
                 src_ref=rows_att.at[b ^ d, piece_of(slot)],
                 dst_ref=rows_att.at[b ^ d, piece_of(slot)],
@@ -411,9 +496,42 @@
                 device_id=(b ^ d, z),
                 device_id_type=MESH,
             ).wait_recv()
+    branch_in[...] = jnp.concatenate([rows_att[i] for i in range(8)], axis=1)
+    load(steps, width).wait()
+    out_w = w1v[:, :, :, hidden:].reshape(width, width)
+    branch = product(branch_in[...], out_w) + par[4:5]
+    normal, inverse = normalize(X[b, 0:count].astype(HIGH) + branch)
+    n1[...] = normal
+    r1[...] = jnp.broadcast_to(inverse, r1.shape)
+    normed_low[...] = (normal * par[0:1] + par[5:6]).astype(LOW)
+
+    def store(c, ref, out, which):
+        cols = pl.ds(pl.multiple_of(c * chunk, chunk), chunk)
+        return pltpu.make_async_copy(ref.at[:, cols], out.at[:, cols], csem.at[which, c])
+
+    @pl.loop(0, steps)
+    def _(c):
+        cols = pl.ds(pl.multiple_of(c * chunk, chunk), chunk)
+        load(c).wait()
+        pre = product(normed_low[...], w1v[:, :, :, cols].reshape(width, chunk))
+        value, rate = gelu_parts(pre + hid[:, cols])
+        act[:, cols] = value.astype(LOW)
+        slope[:, cols] = rate.astype(LOW)
+        store(c, act, act_out, 0).start()
+        store(c, slope, slope_out, 1).start()
+        for at, (event, *what) in late_events.items():
+            pl.when(c == at)(functools.partial(event, *what))
+
+    for copy in core2.values():
+        copy.wait_recv()
+    for slot in range(slots):
+        for d in range(1, 8):
+            send_att(slot, d).wait_send()
+    for c in range(steps):
+        store(c, act, act_out, 0).wait()
+        store(c, slope, slope_out, 1).wait()
     s.drain()
-    for copy in locs[2:]:
-        copy.wait()
+    locs[3].wait()
     for i in range(8):
         pltpu.make_async_copy(X.at[i], X_out.at[i], osem.at[i]).wait()
 
@@ -426,37 +544,57 @@
     return [pltpu.SemaphoreType.DMA((count,)), pltpu.SemaphoreType.DMA((count,))]
 
 
-def front(x, win, w1, w2, slots):
-    count, width = x.shape[0] - 16, x.shape[1]
-    rows = count // slots
+def front(x, segment, present, input_weight, gains, biases, hidden_bias, expand, out_w, w2):
+    slots = segment.shape[0]
+    count, width = x.shape
+    rows, hidden = count // slots, expand.shape[1]
+    shard = expand.shape[0]
     shape = lambda *s: jax.ShapeDtypeStruct(s, LOW)
+    wide = lambda *s: jax.ShapeDtypeStruct(s, HIGH)
     vmem = pl.BlockSpec(memory_space=pltpu.VMEM)
     return pl.pallas_call(
         front_kernel,
         out_shape=(
-            shape(8, *x.shape),
-            shape(8, 4, *w1.shape),
+            shape(8, count + 16, width),
+            shape(8, 4, shard, hidden + width),
             shape(8, 4, *w2.shape),
-            shape(8, count, 128),
-            shape(width, win.shape[2]),
-            shape(4, 16, win.shape[2]),
+            shape(count, hidden),
+            shape(count, hidden),
+            shape(width, 384),
+            shape(4, 16, 384),
             shape(2, 8, slots, rows, 128),
             shape(2, 8, slots, rows, 128),
             shape(8, slots, rows, 128),
             shape(8, slots, rows, 128),
-            jax.ShapeDtypeStruct((slots, 8, 8 * rows), HIGH),
+            wide(slots, 8, 8 * rows),
+            shape(count, width),
+            wide(count, width),
+            wide(count, 128),
+            shape(count, width),
+            wide(8, width),
         ),
-        in_specs=in_hbm(4),
-        out_specs=tuple(in_hbm(4)) + (vmem,) * 7,
-        scratch_shapes=[pltpu.VMEM((8, *x.shape), LOW), pltpu.VMEM((4, *win.shape), LOW)]
+        in_specs=in_hbm(1) + [vmem] * 6 + in_hbm(3),
+        out_specs=tuple(in_hbm(5)) + (vmem,) * 12,
+        scratch_shapes=[
+            pltpu.VMEM((8, count + 16, width), LOW),
+            pltpu.VMEM((4, 8, shard + 16, 384), LOW),
+            pltpu.VMEM((8, shard + 16, 384), LOW),
+            pltpu.VMEM((shard, hidden + width), LOW),
+            pltpu.VMEM((8, count, 128), LOW),
+            pltpu.VMEM((8, 4, shard, hidden + width), LOW),
+            pltpu.VMEM((count, hidden), LOW),
+            pltpu.VMEM((count, hidden), LOW),
+            pltpu.VMEM((1, hidden), HIGH),
+        ]
         + pair_of_semaphores(116)
         + pair_of_semaphores(8 * slots)
-        + [pltpu.SemaphoreType.DMA((4,)), pltpu.SemaphoreType.DMA((8 + slots,))],
+        + [pltpu.SemaphoreType.DMA((5,)), pltpu.SemaphoreType.DMA((8 + slots,))]
+        + [pltpu.SemaphoreType.DMA((hidden // 512 + 1,)), pltpu.SemaphoreType.DMA((2, hidden // 512))],
         compiler_params=pltpu.CompilerParams(
             collective_id=1, has_side_effects=True, vmem_limit_bytes=VMEM_LIMIT
         ),
         name="front",
-    )(x, win, w1, w2)
+    )(x, segment, present, input_weight, gains, biases, hidden_bias, expand, out_w, w2)
 
 
 def add_rows(out, one, two):
@@ -734,39 +872,174 @@
     )(qh, o, g, lse, kh, v)
 
 
+class TokenSums:
+    COPIES = 4 + 2 + 4
+
+    def __init__(self, s, piece, sent, C, S, H, Q, A):
+        b, z = position()
+        to_x, to_y, to_core = (b ^ 2, z), (b ^ 4, z), (b ^ 1, z)
+        self.b, self.piece = b, piece
+        self.sent, self.C, self.S, self.H, self.Q, self.A = sent, C, S, H, Q, A
+        self.other = [s.plan(sent.at[e], C.at[e], to_core, C.at[e]) for e in range(4)]
+
+        def send(e, part, to, where):
+            return s.plan(half(S.at[e - 1], part), where, to, where)
+
+        self.halves = [send(3, 0, to_x, H.at[0]), send(3, 1, to_y, H.at[1])]
+        self.ahead = [
+            send(2, 1, to_y, half(Q.at[1], 1)),
+            send(1, 0, to_x, half(Q.at[0], 0)),
+        ]
+        self.rest = [
+            send(2, 0, to_y, half(Q.at[1], 0)),
+            send(1, 1, to_x, half(Q.at[0], 1)),
+        ]
+
+    def give(self, e):
+        self.sent[e] = self.piece(self.b ^ 1 ^ (2 * e)).astype(LOW)
+        self.other[e].go()
+
+    def take(self, e):
+        mine = self.piece(self.b ^ (2 * e))
+        self.other[e].wait_recv()
+        mine = mine + self.C[e].astype(HIGH)
+        if e:
+            self.S[e - 1] = mine.astype(LOW)
+        else:
+            self.A[...] = mine
+        for copy in {3: self.halves, 1: self.ahead[1:], 2: self.ahead[:1], 0: []}[e]:
+            copy.go()
+
+    def relay(self):
+        for i, e in ((0, 2), (1, 1)):
+            self.halves[i].wait_recv()
+            part = half(self.S.at[e - 1], i)
+            add_rows(part, part, self.H.at[i])
+            self.rest[i].go()
+
+    def total(self):
+        for copy in self.ahead + self.rest:
+            copy.wait_recv()
+        return self.A[...] + self.Q[0].astype(HIGH) + self.Q[1].astype(HIGH)
+
+    @staticmethod
+    def scratch(rows, width):
+        low = lambda *s: pltpu.VMEM((*s, width), LOW)
+        return [low(4, rows), low(4, rows), low(3, rows), low(2, rows // 2), low(2, rows)] + [
+            pltpu.VMEM((rows, width), HIGH)
+        ]
+
+
 def back_kernel(
-    d_att, qh, kh, v, att, lse, g1, dq, dk, dv, o1, grads, acc, delta, C, S, H, Q, Z, lsem, send, recv
+    d_att,
+    qh_in,
+    kh_in,
+    v_in,
+    att_in,
+    lse_in,
+    w_in,
+    first,
+    g1,
+    dq,
+    dk,
+    dv,
+    o1,
+    out_o,
+    tok,
+    qh,
+    kh,
+    v,
+    att,
+    lse,
+    w,
+    first_rows,
+    tail,
+    grads,
+    acc,
+    delta,
+    lsem,
+    send,
+    recv,
+    *buffers,
 ):
     b, z = position()
     blocks, slots, rows, _ = v.shape
-    count = slots * rows
+    loads = [
+        pltpu.make_async_copy(src, dst, lsem.at[i])
+        for i, (src, dst) in enumerate(
+            (
+                (d_att.at[b], grads.at[b]),
+                (qh_in, qh),
+                (kh_in, kh),
+                (v_in, v),
+                (att_in, att),
+                (lse_in, lse),
+                (w_in, w),
+                (first.at[pl.ds(0, rows)], first_rows),
+            )
+        )
+    ]
+    for load in loads:
+        load.start()
     greet([(b ^ d, z) for d in range(1, 8)] + [(b, z ^ d) for d in (1, 2, 3)])
     s = Sender(send, recv)
     arriving = [
-        s.go(d_att.at[b ^ d], grads.at[b], (b ^ d, z), grads.at[b ^ d]) for d in range(1, 8)
+        [
+            s.go(d_att.at[b ^ d, part], grads.at[b, part], (b ^ d, z), grads.at[b ^ d, part])
+            for d in range(1, 8)
+        ]
+        for part in (pl.ds(slot * rows, rows) for slot in range(slots))
     ]
-    sums = Reducer(s, lambda bb, zz: g1.at[bb, zz], o1, C, S, H, Q, Z, lsem)
+
+    def arrive(slot):
+        for copy in arriving[slot]:
+            copy.wait_recv()
+
+    most = o1.shape[1] - tail.shape[1] + out_o.shape[1]
+    sums = Reducer(
+        s, lambda bb, zz: g1.at[bb, zz, :, pl.ds(0, most)], o1.at[:, pl.ds(0, most)], *buffers[:6]
+    )
+    late = ReducerAlongZ(
+        s, lambda bb, zz: g1.at[bb, zz, :, pl.ds(most, tail.shape[1])], tail, *buffers[6:12]
+    )
+
+    def piece(i):
+        mixed = jnp.concatenate([ref[i, 0] for ref in (dq, dk, dv)], axis=-1)
+        return product_nt(mixed, w[...])
+
+    tokens = TokenSums(s, piece, *buffers[12:])
+    late.start()
     sums.start()
-    grads[b] = d_att[b]
+    late.fold(3)
+    late.fold(1)
     sums.fold(3)
+    late.fold(2)
+    late.fold(0)
     sums.fold(2)
-    for copy in arriving:
-        copy.wait_recv()
+    arrive(0)
+    for load in loads:
+        load.wait()
 
     def grad_rows(slot):
         part = pl.ds(pl.multiple_of(slot * rows, rows), rows)
         return rows_of(grads[:, part])
 
     events = {
-        1: (sums.relay, 3),
-        3: (sums.fold, 1),
-        4: (sums.relay, 2),
-        5: (sums.collect, 3),
-        6: (sums.fold, 0),
-        8: (sums.relay, 1),
-        9: (sums.collect, 2),
-        11: (sums.relay, 0),
-        13: (sums.collect, 1),
+        0: [(late.relay, 3), (late.relay, 1)],
+        1: [(sums.relay, 3)],
+        2: [(late.relay, 2), (late.relay, 0)],
+        3: [(sums.fold, 1)],
+        4: [(sums.relay, 2), (late.collect, 3)],
+        5: [(sums.collect, 3)],
+        6: [(sums.fold, 0), (late.collect, 1)],
+        7: [(late.collect, 2), (arrive, 1)],
+        8: [(tokens.give, 3), (sums.relay, 1)],
+        9: [(tokens.give, 2), (tokens.take, 3), (sums.collect, 2)],
+        10: [(tokens.give, 1), (tokens.take, 2)],
+        11: [(tokens.give, 0), (tokens.take, 1), (sums.relay, 0)],
+        12: [(tokens.take, 0), (late.cross,)],
+        13: [(sums.collect, 1), (tokens.relay,)],
+        14: [(late.collect, 0)],
     }
 
     @pl.loop(0, blocks * slots)
@@ -793,63 +1066,59 @@
         def _():
             dq[:, slot] = (acc[...].T * 0.125).astype(LOW).reshape(blocks, rows, 128)
 
-        for at, (event, what) in events.items():
-            pl.when(step == at)(functools.partial(event, what))
+        for at, some in events.items():
+
+            @pl.when(step == at)
+            def _(some=some):
+                for event, *what in some:
+                    event(*what)
 
     sums.collect(0)
+    late.total()
+    rest = o1.shape[1] - most
+    o1[:, most:] = tail[:, :rest]
+    out_o[...] = tail[:, rest:]
     sums.total()
+    tok[...] = first_rows[...] + tokens.total()
     s.drain()
 
 
-def back(d_att, qh, kh, v, att, lse, g1):
+def back(d_att, qh, kh, v, att, lse, w, d_first, g1):
     blocks, slots, rows, lanes = v.shape
     shape = jax.ShapeDtypeStruct
+    shard, total = g1.shape[2:]
+    width = w.shape[0]
+    late = 2 * width
     vmem = pl.BlockSpec(memory_space=pltpu.VMEM)
+    scratch = lambda a: pltpu.VMEM(a.shape, a.dtype)
     return pl.pallas_call(
         back_kernel,
-        out_shape=(shape(v.shape, LOW),) * 3 + (shape(g1.shape[2:], HIGH),),
-        in_specs=[vmem] * 6 + in_hbm(1),
-        out_specs=(vmem,) * 4,
-        scratch_shapes=[
+        out_shape=(shape(v.shape, LOW),) * 3
+        + (
+            shape((shard, total - width), HIGH),
+            shape((shard, width), HIGH),
+            shape((rows, width), HIGH),
+        ),
+        in_specs=in_hbm(9),
+        out_specs=(vmem,) * 6,
+        scratch_shapes=[scratch(a) for a in (qh, kh, v, att, lse, w)]
+        + [
+            pltpu.VMEM((rows, width), HIGH),
+            pltpu.VMEM((shard, late), HIGH),
             pltpu.VMEM(d_att.shape, LOW),
             pltpu.VMEM((lanes, blocks * rows), HIGH),
             pltpu.VMEM((8, blocks * rows), HIGH),
+            pltpu.SemaphoreType.DMA((8,)),
         ]
-        + Reducer.scratch(*g1.shape[2:])
-        + pair_of_semaphores(7 + Reducer.COPIES),
+        + pair_of_semaphores(7 * slots + Reducer.COPIES + ReducerAlongZ.COPIES + TokenSums.COPIES)
+        + Reducer.scratch(shard, total - late)
+        + ReducerAlongZ.scratch(shard, late)
+        + TokenSums.scratch(rows, width),
         compiler_params=pltpu.CompilerParams(
             collective_id=2, has_side_effects=True, vmem_limit_bytes=VMEM_LIMIT
         ),
         name="back",
-    )(d_att, qh, kh, v, att, lse, g1)
-
-
-def normalize(values):
-    mean = jnp.mean(values, axis=-1, keepdims=True)
-    centred = values - mean
-    spread = jnp.mean(centred * centred, axis=-1, keepdims=True)
-    inverse = lax.rsqrt(spread + EPSILON)
-    return centred * inverse, inverse
-
-
-def normalize_back(grad, normal, inverse):
-    return inverse * (
-        grad
-        - jnp.mean(grad, axis=-1, keepdims=True)
-        - normal * jnp.mean(grad * normal, axis=-1, keepdims=True)
-    )
-
-
-def gelu_parts(u):
-    bell = jnp.exp(-0.5 * u * u)
-    t = 1.0 / (1.0 + (0.3275911 * 0.5**0.5) * jnp.abs(u))
-    poly = 1.061405429 * t - 1.453152027
-    poly = poly * t + 1.421413741
-    poly = poly * t - 0.284496736
-    poly = poly * t + 0.254829592
-    tail = 0.5 * poly * t * bell
-    below = jnp.where(u < 0.0, tail, 1.0 - tail)
-    return u * below, below + u * bell * 0.3989422804014327
+    )(d_att, qh, kh, v, att, lse, w, d_first, g1)
 
 
 def column_sum(block):
@@ -858,36 +1127,37 @@
 
 def middle_kernel(
     chunk,
-    tok_ref,
-    att_ref,
+    small_rows,
+    att,
+    n1,
+    r1,
+    normed_low,
     cot_ref,
     par_ref,
-    hid_ref,
+    act_hbm,
+    slope_hbm,
     w1_hbm,
     w2_hbm,
     out_ref,
     first_ref,
     d_att_ref,
-    sums_ref,
-    d_hid_ref,
+    small_ref,
     g1_hbm,
     g2_hbm,
     w1,
     w2,
-    att,
-    normed_low,
-    n1,
-    n2,
     act,
     slope,
     acc,
     low,
+    sums_ref,
+    d_hid_ref,
     wsem,
     gsem,
 ):
     hidden, width = w2.shape
     steps = hidden // chunk
-    pieces, _, held = att_ref.shape
+    pieces, _, held = d_att_ref.shape
 
     def columns(c):
         return pl.ds(pl.multiple_of(c * chunk, chunk), chunk)
@@ -898,36 +1168,34 @@
     def load2(c):
         return pltpu.make_async_copy(w2_hbm.at[columns(c)], w2.at[columns(c)], wsem.at[1, c])
 
+    def load_act(c):
+        return pltpu.make_async_copy(act_hbm.at[:, columns(c)], act.at[:, columns(c)], wsem.at[2, c])
+
+    def load_slope(c):
+        return pltpu.make_async_copy(
+            slope_hbm.at[:, columns(c)], slope.at[:, columns(c)], wsem.at[3, c]
+        )
+
     last = pl.ds(hidden, width)
+    for c in range(steps):
+        load_act(c).start()
+        load2(c).start()
+    for c in range(steps):
+        load_slope(c).start()
+        load1(c).start()
     load_out = pltpu.make_async_copy(w1_hbm.at[:, last], w1.at[:, last], wsem.at[0, steps])
     load_out.start()
-    for c in range(steps):
-        load1(c).start()
-        load2(c).start()
     gain1, gain2 = par_ref[0:1], par_ref[1:2]
     bias = lambda i: par_ref[2 + i : 3 + i]
-    for i in range(pieces):
-        att[:, i * held : (i + 1) * held] = att_ref[i]
-    load_out.wait()
-    first_sum = tok_ref[...].astype(HIGH) + product(att[...], w1[:, hidden:]) + bias(2)
-    normal, inverse1 = normalize(first_sum)
-    n1[...] = normal
-    normed = normal * gain1 + bias(3)
-    normed_low[...] = normed.astype(LOW)
-    acc[...] = normed + bias(4)
+    acc[...] = n1[...] * gain1 + (bias(3) + bias(4))
 
     @pl.loop(0, steps)
     def _(c):
-        load1(c).wait()
-        pre = product(normed_low[...], w1[:, columns(c)]) + hid_ref[:, columns(c)]
-        value, rate = gelu_parts(pre)
-        act[:, columns(c)] = value.astype(LOW)
-        slope[:, columns(c)] = rate.astype(LOW)
+        load_act(c).wait()
         load2(c).wait()
-        acc[...] += product(value.astype(LOW), w2[columns(c), :])
+        acc[...] += product(act[:, columns(c)], w2[columns(c), :])
 
     normal, inverse2 = normalize(acc[...])
-    n2[...] = normal
     out_ref[...] = (normal * gain2 + bias(5)).astype(LOW)
     cot = cot_ref[...].astype(HIGH)
     d_second = normalize_back(cot * gain2, normal, inverse2)
@@ -945,6 +1213,8 @@
 
     @pl.loop(0, steps)
     def _(c):
+        load_slope(c).wait()
+        load1(c).wait()
         d_act = product_nt(low[...], w2[columns(c), :])
         d_pre = (d_act * slope[:, columns(c)].astype(HIGH)).astype(LOW)
         d_hid_ref[:, columns(c)] = column_sum(d_pre)
@@ -956,61 +1226,70 @@
 
     d_normed = acc[...]
     normal = n1[...]
-    d_first = normalize_back(d_normed * gain1, normal, inverse1)
+    d_first = normalize_back(d_normed * gain1, normal, r1[:, 0:1])
     first_ref[...] = d_first
     low[...] = d_first.astype(LOW)
     sums_ref[0:1] = column_sum(d_normed * normal)
     sums_ref[2:3] = column_sum(low[...])
     sums_ref[3:4] = column_sum(d_normed)
+    load_out.wait()
     d_att = product_nt(low[...], w1[:, hidden:]).astype(LOW)
     for i in range(pieces):
         d_att_ref[i] = d_att[:, i * held : (i + 1) * held]
     w1[:, hidden:] = product_tn(att[...], low[...]).astype(LOW)
     store_out = pltpu.make_async_copy(w1.at[:, last], g1_hbm.at[:, last], gsem.at[0, steps])
     store_out.start()
+    blocks, planes, _ = small_ref.shape
+    small_ref[...] = jnp.zeros_like(small_ref)
+    owners = [(i, j) for i in range(blocks) for j in range(width // (blocks * small_rows))]
+    for at, (i, j) in enumerate(owners):
+        for k in range(6):
+            small_ref[i, j : j + 1, k * small_rows : (k + 1) * small_rows] = sums_ref[
+                k : k + 1, at * small_rows : (at + 1) * small_rows
+            ]
+        part = hidden // len(owners)
+        small_ref[i, j : j + 1, 6 * small_rows : 6 * small_rows + part] = d_hid_ref[
+            :, at * part : (at + 1) * part
+        ]
     for c in range(steps):
         store1(c).wait()
         store2(c).wait()
     store_out.wait()
 
 
-def middle(tokens, att, cot, par, hid, w1, w2):
-    count, width = tokens.shape
+def middle(att, n1, r1, normed_low, cot, par, act, slope, w1, w2, pieces, planes):
+    count, width = cot.shape
     hidden = w2.shape[0]
-    pieces = att.shape[0]
     chunk = 512
     shape = jax.ShapeDtypeStruct
     vmem = pl.BlockSpec(memory_space=pltpu.VMEM)
     return pl.pallas_call(
-        functools.partial(middle_kernel, chunk),
+        functools.partial(middle_kernel, chunk, width // (pieces * planes)),
         out_shape=(
             shape((count, width), LOW),
             shape((count, width), HIGH),
-            shape(att.shape, LOW),
-            shape((8, width), HIGH),
-            shape((1, hidden), HIGH),
+            shape((pieces, count, width // pieces), LOW),
+            shape((pieces, -(-planes // 8) * 8, 384), HIGH),
             shape(w1.shape, LOW),
             shape(w2.shape, LOW),
         ),
-        in_specs=[vmem] * 5 + in_hbm(2),
-        out_specs=(vmem,) * 5 + tuple(in_hbm(2)),
+        in_specs=[vmem] * 6 + in_hbm(4),
+        out_specs=(vmem,) * 4 + tuple(in_hbm(2)),
         scratch_shapes=[
             pltpu.VMEM(w1.shape, LOW),
             pltpu.VMEM(w2.shape, LOW),
-            pltpu.VMEM((count, width), LOW),
-            pltpu.VMEM((count, width), LOW),
-            pltpu.VMEM((count, width), HIGH),
-            pltpu.VMEM((count, width), HIGH),
             pltpu.VMEM((count, hidden), LOW),
             pltpu.VMEM((count, hidden), LOW),
             pltpu.VMEM((count, width), HIGH),
             pltpu.VMEM((count, width), LOW),
-            pltpu.SemaphoreType.DMA((2, hidden // chunk + 1)),
+            pltpu.VMEM((8, width), HIGH),
+            pltpu.VMEM((1, hidden), HIGH),
+            pltpu.SemaphoreType.DMA((4, hidden // chunk + 1)),
             pltpu.SemaphoreType.DMA((2, hidden // chunk + 1)),
         ],
         compiler_params=pltpu.CompilerParams(vmem_limit_bytes=VMEM_LIMIT),
         name="middle",
-    )(tokens, att, cot, par, hid, w1, w2)
+    )(att, n1, r1, normed_low, cot, par, act, slope, w1, w2)
 
 
 def finish_kernel(
@@ -1018,21 +1297,19 @@
     dk,
     dv,
     w,
-    d_first,
+    first,
+    tok0,
     small,
     x_hbm,
     g2,
     tok_out,
     in_out,
-    small_out,
+    gains_out,
+    biases_out,
+    hidden_out,
     o2,
+    first_rows,
     x,
-    sent,
-    C,
-    S,
-    A,
-    H,
-    Q,
     D,
     R,
     Z,
@@ -1042,66 +1319,54 @@
     lsem,
     send,
     recv,
-    *reducing,
+    *buffers,
 ):
     b, z = position()
-    count, width = d_first.shape
+    rows, width = tok0.shape
     blocks = dq.shape[0]
-    to_x, to_y, to_core = (b ^ 2, z), (b ^ 4, z), (b ^ 1, z)
-    loads = []
-    for i in range(blocks):
-        load = pltpu.make_async_copy(x_hbm.at[i, pl.ds(0, count)], x.at[i], lsem.at[i])
+    count = 2 * rows
+    loads = [
+        pltpu.make_async_copy(x_hbm.at[i, pl.ds(0, count)], x.at[i], lsem.at[i])
+        for i in range(blocks)
+    ]
+    loads.append(pltpu.make_async_copy(first.at[pl.ds(rows, rows)], first_rows, lsem.at[blocks]))
+    loads.append(pltpu.make_async_copy(tok0, tok_out.at[pl.ds(0, rows)], lsem.at[blocks + 1]))
+    for load in loads:
         load.start()
-        loads.append(load)
     greet([(b ^ d, z) for d in range(1, 8)] + [(b, z ^ d) for d in (1, 2, 3)])
     s = Sender(send, recv)
-    cut = o2.shape[0] // 2
-    lower, upper = pl.ds(0, cut), pl.ds(cut, cut)
-    sums = Reducer(s, lambda bb, zz: g2.at[bb, zz, lower], o2.at[lower], *reducing[:6])
-    late = ReducerAlongZ(s, lambda bb, zz: g2.at[bb, zz, upper], o2.at[upper], *reducing[6:])
+    cut = buffers[0].shape[2]
+    lower, upper = pl.ds(0, cut), pl.ds(cut, o2.shape[0] - cut)
+    sums = Reducer(s, lambda bb, zz: g2.at[bb, zz, lower], o2.at[lower], *buffers[:6])
+    late = ReducerAlongZ(s, lambda bb, zz: g2.at[bb, zz, upper], o2.at[upper], *buffers[6:12])
+
+    def piece(i):
+        mixed = jnp.concatenate([ref[i, 1] for ref in (dq, dk, dv)], axis=-1)
+        return product_nt(mixed, w[...])
+
+    tokens = TokenSums(s, piece, *buffers[12:])
     small_in = [
         s.go(small.at[b ^ d], M.at[d - 1], (b ^ d, z), M.at[d - 1]) for d in range(1, 8)
     ]
-
-    def mixed(i):
-        return jnp.concatenate([ref[i].reshape(count, -1) for ref in (dq, dk, dv)], axis=-1)
-
-    def piece(i):
-        return product_nt(mixed(i), w[...])
-
-    other = {}
-    for e in (3, 1, 2, 0):
-        sent[e] = piece(b ^ 1 ^ (2 * e)).astype(LOW)
-        other[e] = s.go(sent.at[e], C.at[e], to_core, C.at[e])
-        if e == 3:
-            late.start()
-        if e == 1:
-            sums.start()
+    late.start()
+    tokens.give(3)
+    sums.start()
+    tokens.give(2)
+    tokens.give(1)
+    tokens.give(0)
     late.fold(3)
+    late.fold(1)
+    tokens.take(3)
     sums.fold(3)
-    late.fold(1)
-
-    def own(e):
-        mine = piece(b ^ (2 * e))
-        other[e].wait_recv()
-        return mine + C[e].astype(HIGH)
-
-    S[3] = own(3).astype(LOW)
-    halves = [
-        s.go(half(S.at[3], 0), H.at[0], to_x, H.at[0]),
-        s.go(half(S.at[3], 1), H.at[1], to_y, H.at[1]),
-    ]
     late.relay(3)
     late.fold(2)
     sums.fold(2)
-    S[2] = own(2).astype(LOW)
-    pieces = [s.go(half(S.at[2], 1), half(Q.at[1], 1), to_y, half(Q.at[1], 1))]
+    tokens.take(2)
     sums.relay(3)
     late.fold(0)
     late.relay(1)
-    S[1] = own(1).astype(LOW)
-    pieces.append(s.go(half(S.at[1], 0), half(Q.at[0], 0), to_x, half(Q.at[0], 0)))
-    A[...] = own(0) + d_first[...]
+    tokens.take(1)
+    tokens.take(0)
     sums.fold(1)
     sums.relay(2)
     late.relay(2)
@@ -1110,7 +1375,8 @@
     total = jnp.zeros((width, w.shape[1]), HIGH)
     for i in range(blocks):
         loads[i].wait()
-        total = total + product_tn(x[i], mixed(i))
+        mixed = jnp.concatenate([ref[i].reshape(count, -1) for ref in (dq, dk, dv)], axis=-1)
+        total = total + product_tn(x[i], mixed)
     D[...] = total.astype(LOW).reshape(D.shape)
     grads_in = [
         s.go(D.at[b ^ d], R.at[b], (b ^ d, z), R.at[b ^ d]) for d in range(1, 8)
@@ -1119,16 +1385,7 @@
     sums.collect(3)
     sums.fold(0)
     late.relay(0)
-
-    halves[0].wait_recv()
-    part = half(S.at[2], 0)
-    part[...] = part[...] + H[0]
-    pieces.append(s.go(part, half(Q.at[1], 0), to_y, half(Q.at[1], 0)))
-    halves[1].wait_recv()
-    part = half(S.at[1], 1)
-    part[...] = part[...] + H[1]
-    pieces.append(s.go(part, half(Q.at[0], 1), to_x, half(Q.at[0], 1)))
-
+    tokens.relay()
     sums.relay(1)
     late.collect(1)
     sums.collect(2)
@@ -1149,72 +1406,92 @@
     late.cross()
     for copy in grads_in:
         copy.wait_recv()
-    rows = R.shape[1] // 4
+    share_rows = R.shape[1] // 4
 
     def share(d):
-        return R.at[:, pl.ds(pl.multiple_of((z ^ d) * rows, rows), rows)]
+        return R.at[:, pl.ds(pl.multiple_of((z ^ d) * share_rows, share_rows), share_rows)]
 
     in_z = [s.go(share(d), Z.at[d - 1], (b, z ^ d), Z.at[d - 1]) for d in (1, 2, 3)]
     sums.collect(1)
     for copy in small_z:
         copy.wait_recv()
-    small_out[...] = ((N[...] + T[0]) + T[1]) + T[2]
+    vectors = ((N[...] + T[0]) + T[1]) + T[2]
+    planes = lax.broadcasted_iota(jnp.int32, vectors.shape, 0)
+    row = jnp.sum(jnp.where(planes == z, vectors, 0.0), axis=0, keepdims=True)
+    n = gains_out.shape[1]
+    for k in range(2):
+        gains_out[k : k + 1] = row[:, k * n : (k + 1) * n]
+        own = vectors[4 + k : 5 + k]
+        parts = [jnp.where(z == j, own[:, j * n : (j + 1) * n], 0.0) for j in range(4)]
+        biases_out[k : k + 1] = (parts[0] + parts[1]) + (parts[2] + parts[3])
+    for k in range(2, 6):
+        biases_out[k : k + 1] = row[:, k * n : (k + 1) * n]
+    hidden_out[...] = row[:, 6 * n : 6 * n + hidden_out.shape[1]]
     for copy in in_z:
         copy.wait_recv()
-    in_out[...] = ((share(0)[...].astype(HIGH) + Z[0].astype(HIGH)) + Z[1].astype(HIGH)) + Z[
-        2
-    ].astype(HIGH)
-    for copy in pieces:
-        copy.wait_recv()
-    tok_out[...] = A[...] + Q[0].astype(HIGH) + Q[1].astype(HIGH)
+    terms = [share(0), Z.at[0], Z.at[1], Z.at[2]]
+    for i in range(blocks):
+        block = terms[0][i].astype(HIGH)
+        for term in terms[1:]:
+            block = block + term[i].astype(HIGH)
+        for k in range(3):
+            at = k * width + i * 128
+            in_out[:, at : at + 128] = block[:, k * 128 : (k + 1) * 128]
     late.collect(0)
     sums.collect(0)
     sums.total()
     late.total()
+    for load in loads[blocks:]:
+        load.wait()
+    tok_out[rows:] = first_rows[...] + tokens.total()
     s.drain()
 
 
-def finish(dq, dk, dv, w, d_first, small, x, g2):
-    count, width = d_first.shape
+def finish(dq, dk, dv, w, d_first, tok0, small, x, g2):
+    rows, width = tok0.shape
     blocks, columns = dq.shape[0], w.shape[1]
     share = width // (4 * blocks)
+    shard = g2.shape[2]
+    late = shard // 4
     vmem = pl.BlockSpec(memory_space=pltpu.VMEM)
-    shape = jax.ShapeDtypeStruct
+    shape = lambda *s: jax.ShapeDtypeStruct(s, HIGH)
     low = lambda *s: pltpu.VMEM(s, LOW)
+    wide = lambda *s: pltpu.VMEM(s, HIGH)
+    tile = small.shape[1:]
     return pl.pallas_call(
         finish_kernel,
         out_shape=(
-            shape((count, width), HIGH),
-            shape((blocks, share, columns), HIGH),
-            shape(small.shape[1:], HIGH),
-            shape(g2.shape[2:], HIGH),
+            shape(2 * rows, width),
+            shape(share, 3 * width),
+            shape(2, share),
+            shape(6, share),
+            shape(1, shard),
+            shape(shard, width),
         ),
-        in_specs=[vmem] * 6 + in_hbm(2),
-        out_specs=(vmem,) * 4,
+        in_specs=[vmem] * 4 + in_hbm(2) + [vmem] + in_hbm(2),
+        out_specs=(vmem,) * 6,
         scratch_shapes=[
-            low(blocks, count, width),
-            low(4, count, width),
-            low(4, count, width),
-            low(4, count, width),
-            pltpu.VMEM((count, width), HIGH),
-            low(2, count // 2, width),
-            low(2, count, width),
+            wide(rows, width),
+            low(blocks, 2 * rows, width),
             low(blocks, 4 * share, columns),
             low(blocks, 4 * share, columns),
             low(3, blocks, share, columns),
-            pltpu.VMEM((7, *small.shape[1:]), HIGH),
-            pltpu.VMEM(small.shape[1:], HIGH),
-            pltpu.VMEM((3, *small.shape[1:]), HIGH),
+            wide(7, *tile),
+            wide(*tile),
+            wide(3, *tile),
+            pltpu.SemaphoreType.DMA((blocks + 2,)),
         ]
-        + [pltpu.SemaphoreType.DMA((blocks,))]
-        + pair_of_semaphores(32 + Reducer.COPIES + ReducerAlongZ.COPIES)
-        + Reducer.scratch(g2.shape[2] // 2, width)
-        + ReducerAlongZ.scratch(g2.shape[2] // 2, width),
+        + pair_of_semaphores(
+            20 + Reducer.COPIES + ReducerAlongZ.COPIES + TokenSums.COPIES
+        )
+        + Reducer.scratch(shard - late, width)
+        + ReducerAlongZ.scratch(late, width)
+        + TokenSums.scratch(rows, width),
         compiler_params=pltpu.CompilerParams(
             collective_id=3, has_side_effects=True, vmem_limit_bytes=VMEM_LIMIT
         ),
         name="finish",
-    )(dq, dk, dv, w, d_first, small, x, g2)
+    )(dq, dk, dv, w, d_first, tok0, small, x, g2)
 
 
 def swap(pieces):
@@ -1270,87 +1547,92 @@
     count = slots * rows
     flat = tokens.reshape(count, width)
 
-    code = segment + 4 * (1 - present)
-    code_rows = jnp.zeros((16, width), LOW).at[0, :count].set(code.reshape(count).astype(LOW))
-    sent_tokens = jnp.concatenate([flat, code_rows], axis=0)
-    columns = input_weight.reshape(shard, 3, n_blk, held).transpose(2, 0, 1, 3)
-    columns = columns.reshape(n_blk, shard, 3 * held)
-    small = jnp.concatenate([gains.reshape(-1), biases.reshape(-1), hidden_bias])
-    both = jnp.concatenate([expand_weight, output_weight], axis=1)
     if fast:
-        small = jnp.concatenate([small[None], jnp.zeros((15, small.shape[0]), LOW)], axis=0)
-        small = jnp.broadcast_to(small, (n_blk, *small.shape))
-        win = jnp.concatenate([columns, small], axis=1)
-        X, W1, W2, rows_att, W, small, qh, kh, v, att, lse = front(
-            sent_tokens, win, both, reduce_weight, slots
+        front_out = front(
+            flat,
+            segment,
+            present,
+            input_weight,
+            gains,
+            biases,
+            hidden_bias[None],
+            expand_weight,
+            output_weight,
+            reduce_weight,
         )
-        small = small[:, :n_blk].transpose(1, 0, 2).reshape(shards, 3 * held)
+        X, W1, W2, act, slope, W, _, qh, kh, v, att, lse = front_out[:12]
+        attended, n1, r1, normed_low, cuts = front_out[12:]
         W1, W2 = W1.reshape(width, -1), W2.reshape(hidden, width)
     else:
-        X = lax.all_gather(sent_tokens, "blk")
+        code = (segment + 4 * (1 - present)).reshape(1, count).astype(LOW)
+        code_rows = jnp.pad(jnp.broadcast_to(code, (16, count)), ((0, 0), (0, width - count)))
+        columns = input_weight.reshape(shard, 3, n_blk, held).transpose(2, 0, 1, 3)
+        columns = columns.reshape(n_blk, shard, 3 * held)
+        small = jnp.concatenate([gains.reshape(-1), biases.reshape(-1), hidden_bias])
+        X = lax.all_gather(jnp.concatenate([flat, code_rows], axis=0), "blk")
         W = lax.all_gather(swap(columns), "dp", axis=1).reshape(width, 3 * held)
         small = lax.all_gather(small, BOTH)
-        W1 = lax.all_gather(both, BOTH, axis=0, tiled=True)
+        W1 = jnp.concatenate([expand_weight, output_weight], axis=1)
+        W1 = lax.all_gather(W1, BOTH, axis=0, tiled=True)
         W2 = lax.all_gather(reduce_weight, BOTH, axis=0, tiled=True)
-    part = width // shards
-    cuts = small[:, : 8 * part].reshape(shards, 8, part).transpose(1, 0, 2).reshape(8, width)
-    cuts = cuts.astype(HIGH)
-    gain, bias = cuts[:2], cuts[2:]
-    hidden_full = small[:, 8 * part :].reshape(hidden).astype(HIGH)
-
-    all_tokens = X[:, :count]
-    if not fast:
+        part = width // shards
+        cuts = small[:, : 8 * part].reshape(shards, 8, part).transpose(1, 0, 2)
+        cuts = cuts.reshape(8, width).astype(HIGH)
+        hidden_full = small[:, 8 * part :].reshape(hidden).astype(HIGH)
+        gain, bias = cuts[:2], cuts[2:]
         qh, kh, v, att, lse, rows_att = front_apart(X, W, bias, slots)
+        attended = rows_att.transpose(1, 0, 2).reshape(count, width)
+        branch = product(attended, W1[:, hidden:]) + bias[2]
+        n1, r1 = normalize(flat.astype(HIGH) + branch)
+        r1 = jnp.broadcast_to(r1, (count, 128))
+        normed_low = (n1 * gain[0] + bias[3]).astype(LOW)
+        act, slope = gelu_parts(product(normed_low, W1[:, :hidden]) + hidden_full)
+        act, slope = act.astype(LOW), slope.astype(LOW)
+    cot = cotangent.reshape(count, width)
     middle_out = middle(
-        flat,
-        rows_att,
-        cotangent.reshape(count, width),
-        cuts,
-        hidden_full[None],
-        W1,
-        W2,
+        attended, n1, r1, normed_low, cot, cuts, act, slope, W1, W2, n_blk, n_dp
     )
-    output, d_first, d_att, sums, d_hidden, grad_both, grad_reduce = middle_out
+    output, d_first, d_att, small_rows, grad_both, grad_reduce = middle_out
     output = output.reshape(slots, rows, width)
     if fast:
-        dq, dk, dv, sum_both = back(
-            d_att, qh, kh, v, att, lse, grad_both.reshape(n_blk, n_dp, shard, -1)
+        grad_both = grad_both.reshape(n_blk, n_dp, shard, -1)
+        grad_reduce = grad_reduce.reshape(n_blk, n_dp, -1, width)
+        dq, dk, dv, sum_expand, sum_output, tok0 = back(
+            d_att, qh, kh, v, att, lse, W, d_first, grad_both
         )
-        grad_reduce = grad_reduce.reshape(n_blk, n_dp, -1, width)
-    else:
-        sum_both = lax.psum_scatter(grad_both, BOTH, scatter_dimension=0, tiled=True).astype(HIGH)
-        sum_reduce = lax.psum_scatter(grad_reduce, BOTH, scatter_dimension=0, tiled=True)
-        sum_reduce = sum_reduce.astype(HIGH)
-        dq, dk, dv = attend_back(qh, att, by_slot(swap(d_att), slots), lse, kh, v)
-    small_rows = sums[:6].reshape(6, shards, part).transpose(1, 0, 2).reshape(shards, 6 * part)
-    small_rows = jnp.concatenate([small_rows, d_hidden.reshape(shards, -1)], axis=1)
-    if fast:
-        lanes = small_rows.shape[1]
-        small_rows = small_rows.reshape(n_blk, n_dp, lanes)
-        small_rows = jnp.pad(small_rows, ((0, 0), (0, 4), (0, 3 * held - lanes)))
-        grad_tokens, d_input, small_sum, sum_reduce = finish(
-            dq, dk, dv, W, d_first, small_rows, X, grad_reduce
+        grad_tokens, grad_input, d_gains, d_biases, d_hidden, sum_reduce = finish(
+            dq, dk, dv, W, d_first, tok0, small_rows, X, grad_reduce
         )
-        grad_input = d_input.reshape(n_blk, shard, 3, held).transpose(1, 2, 0, 3)
-        grad_input = grad_input.reshape(shard, 3 * width)
-        me_dp = lax.axis_index("dp")
-        own_cols = lax.dynamic_slice(small_sum, (4, me_dp * part), (2, part))
-        small_sum = lax.dynamic_slice(small_sum, (me_dp, 0), (1, lanes))[0]
-    else:
-        d_mixed = jnp.concatenate([dq[..., :held], dk[..., :held], dv[..., :held]], axis=-1)
-        d_mixed = d_mixed.reshape(n_blk * count, 3 * held)
-        d_input = product_tn(all_tokens.reshape(n_blk * count, width), d_mixed).astype(LOW)
-        d_tokens = product_nt(d_mixed, W).astype(LOW)
-        d_tokens = lax.psum_scatter(d_tokens, "blk", scatter_dimension=0, tiled=True)
-        grad_tokens = d_first + d_tokens.astype(HIGH)
-        d_input = swap(d_input.reshape(n_blk, n_dp * shard, 3 * held))
-        d_input = d_input.reshape(n_blk, n_dp, shard, 3, held).transpose(1, 2, 3, 0, 4)
-        d_input = d_input.reshape(n_dp, shard, 3 * width).astype(HIGH)
-        grad_input = lax.psum_scatter(d_input, "dp", scatter_dimension=0, tiled=False)
-        col = lambda a: jnp.sum(a.astype(HIGH), axis=0)
-        own_cols = jnp.stack([col(d_mixed[:, :held]), col(d_mixed[:, 2 * held :])])
-        own_cols = lax.psum_scatter(own_cols, "dp", scatter_dimension=1, tiled=True)
-        small_sum = lax.psum_scatter(small_rows, BOTH, scatter_dimension=0, tiled=False)
+        return (
+            output,
+            grad_tokens.reshape(slots, rows, width),
+            grad_input,
+            sum_output,
+            sum_expand,
+            sum_reduce,
+            d_gains,
+            d_biases,
+            d_hidden.reshape(-1),
+        )
+    sum_both = lax.psum_scatter(grad_both, BOTH, scatter_dimension=0, tiled=True).astype(HIGH)
+    sum_reduce = lax.psum_scatter(grad_reduce, BOTH, scatter_dimension=0, tiled=True)
+    dq, dk, dv = attend_back(qh, att, by_slot(swap(d_att), slots), lse, kh, v)
+    d_mixed = jnp.concatenate([dq[..., :held], dk[..., :held], dv[..., :held]], axis=-1)
+    d_mixed = d_mixed.reshape(n_blk * count, 3 * held)
+    all_tokens = X[:, :count].reshape(n_blk * count, width)
+    d_input = product_tn(all_tokens, d_mixed).astype(LOW)
+    d_tokens = product_nt(d_mixed, W).astype(LOW)
+    d_tokens = lax.psum_scatter(d_tokens, "blk", scatter_dimension=0, tiled=True)
+    grad_tokens = d_first + d_tokens.astype(HIGH)
+    d_input = swap(d_input.reshape(n_blk, n_dp * shard, 3 * held))
+    d_input = d_input.reshape(n_blk, n_dp, shard, 3, held).transpose(1, 2, 3, 0, 4)
+    d_input = d_input.reshape(n_dp, shard, 3 * width).astype(HIGH)
+    grad_input = lax.psum_scatter(d_input, "dp", scatter_dimension=0, tiled=False)
+    col = lambda a: jnp.sum(a.astype(HIGH), axis=0)
+    own_cols = jnp.stack([col(d_mixed[:, :held]), col(d_mixed[:, 2 * held :])])
+    own_cols = lax.psum_scatter(own_cols, "dp", scatter_dimension=1, tiled=True)
+    small_rows = small_rows[:, :n_dp].reshape(shards, -1)
+    small_sum = lax.psum_scatter(small_rows, BOTH, scatter_dimension=0, tiled=False)
     vectors = small_sum[: 6 * part].reshape(6, part)
     return (
         output,
@@ -1358,10 +1640,10 @@
         grad_input,
         sum_both[:, hidden:],
         sum_both[:, :hidden],
-        sum_reduce,
+        sum_reduce.astype(HIGH),
         vectors[:2],
         jnp.concatenate([own_cols, vectors[2:]], axis=0),
-        small_sum[6 * part :],
+        small_sum[6 * part : 6 * part + hidden // shards],
     )
 
 

time: 369 us -> 349 us (0.946)
  other arithmetic: 7.34 us -> 0 us
  Pallas kernels: 342 us -> 336 us
  local copies, waits for them, and re-layouts: 12.7 us -> 7.95 us
    pallas_call x3, Pallas kernels: 266 us -> 248 us  [the longest x1 136 us: front(): pl.pallas_call(front_kernel, out_shape=(shape(8, count + 16, width), shap...]
    pallas_call x1, Pallas kernels: 76.6 us -> 87.7 us  [back(): pl.pallas_call(back_kernel, out_shape=(shape(v.shape, LOW),) * 3 + (shape...]
    concatenate x6 -> x0, other arithmetic: 5.9 us -> none  [the longest x1 2.28 us: on_device(): sent_tokens = jnp.concatenate([flat, code_rows], axis=0)]
    unnamed x23 -> x22, local copies, waits for them, and re-layouts: 3.07 us -> 7.95 us
    slice x6 -> x0, local copies, waits for them, and re-layouts: 4.38 us -> none  [the longest x1 1.46 us: on_device(): small_sum[6 * part:]]
where the time goes in v6:
time: 349 us; the launch traced here: 345 us
  Pallas kernels  336 us (96%)
  local copies, waits for them, and re-layouts  7.95 us (2%)
    pallas_call x1, Pallas kernels, front(): pl.pallas_call(front_kernel, out_shape=(shape(8, count + 16, width), shap...  136 us
    pallas_call x1, Pallas kernels, back(): pl.pallas_call(back_kernel, out_shape=(shape(v.shape, LOW),) * 3 + (shape...  87.7 us
    pallas_call x1, Pallas kernels, finish(): pl.pallas_call(finish_kernel, out_shape=(shape(2 * rows, width), shape(sh...  73.5 us
    pallas_call x1, Pallas kernels, middle(): pl.pallas_call(functools.partial(middle_kernel, chunk, width // (pieces *...  38.5 us
    unnamed x22, local copies, waits for them, and re-layouts  7.95 us

profile of v6, /device:TPU:0, one launch (start us, length us, event | category | flops | bytes accessed | tf_op | source)
XLA Modules:
  0.0 344.7 jit_solution(8974681403430148820)
XLA Ops:
  0.6 135.8 %front.1 = (bf16[8,528,1024]{2,1,0:T(8,128)(2,1)}, bf16[8,4,32,5120]{3,2,1,0:T(8,128)(2,1)}, bf16[8,4,128,1024]{3,2,1,0:T(8,128)(2,1)}, bf16[512,4096]{1,0:T(8,1...) custom-call(bf16[512,1024]{1,0:T(8,128)(2,1)} %bitcast.16, ...), custom_call_target="tpu_custom_call" | custom-call | tf_op jit(solution)/shard_map/front/pallas_call | solution.py:555
  136.4 38.5 %middle.1 = (bf16[512,1024]{1,0:T(8,128)(2,1)}, f32[512,1024]{1,0:T(8,128)}, bf16[8,512,128]{2,1,0:T(8,128)(2,1)}, f32[8,8,384]{2,1,0:T(8,128)}, bf16[1024,5120]{1,0:T(8,128)(2,1)}, /*index=5*/bf16[4096,1024]{1,0:T(8,128)(2,1)}) custom-call(bf16[512,1024]{1,0:T(8,128)(2,1)} %get-tuple-element.43.att, f32[512,1024]{1,0:T(8,128)} %get-tuple-element.44.n1, ...), custom_call_target="tpu_custom_call" | custom-call | tf_op jit(solution)/shard_map/middle/pallas_call | solution.py:1266
  175.0 87.7 %back.1 = (bf16[8,2,256,128]{3,2,1,0:T(8,128)(2,1)}, bf16[8,2,256,128]{3,2,1,0:T(8,128)(2,1)}, bf16[8,2,256,128]{3,2,1,0:T(8,128)(2,1)}, f32[32,4096]{1,0:T(8,12...) custom-call(bf16[8,512,128]{2,1,0:T(8,128)(2,1)} %get-tuple-element.53.d_att, ...), custom_call_target="tpu_custom_call" | custom-call | tf_op jit(solution)/shard_map/back/pallas_call | solution.py:1094
  262.7 73.5 %finish.1 = (f32[512,1024]{1,0:T(8,128)}, f32[32,3072]{1,0:T(8,128)}, f32[2,32]{1,0:T(2,128)}, f32[6,32]{1,0:T(8,128)}, f32[1,128]{1,0:T(1,128)}, /*index=5*/f32[128,1024]{1,0:T(8,128)}) custom-call(bf16[8,2,256,128]{3,2,1,0:T(8,128)(2,1)} %get-tuple-element.62.dq, bf16[8,2,256,128]{3,2,1,0:T(8,128)(2,1)} %get-tuple-element.63.dk, ...), custom_call_target="tpu_custom_call" | custom-call | tf_op jit(solution)/shard_map/finish/pallas_call | solution.py:1461
  336.2 0.0 copy-start.2
  336.2 0.0 copy-start.3
  336.2 0.0 copy-start
  336.3 0.0 copy-start.1
  336.3 0.0 copy-start.5
  336.3 0.0 copy-start.4
  336.3 0.0 copy-start.6
  336.3 3.3 copy.28
  339.6 0.0 copy-done.2
  339.6 0.7 copy.29
  340.3 0.0 copy-done.3
  340.3 0.7 copy.30
  341.0 0.0 copy-done
  341.0 0.8 copy.31
  341.8 0.0 copy-done.1
  341.8 0.8 copy.32
  342.6 0.0 copy-done.5
  342.6 0.6 copy.33
  343.1 0.0 copy-done.4
  343.1 0.6 copy.34
  343.7 0.0 copy-done.6
  343.7 0.5 copy.35
Async XLA Ops:
  336.2 3.3 copy-start.2
  336.2 4.1 %copy-start.3 = (f32[32,1024]{1,0:T(8,128)S(1)}, f32[32,1024]{1,0:T(8,128)}, u32[]{:S(2)}) copy-start(f32[32,1024]{1,0:T(8,128)} %get-tuple-element.89) | copy-start | bytes 393220
  336.2 4.7 %copy-start = (f32[32,4096]{1,0:T(8,128)S(1)}, f32[32,4096]{1,0:T(8,128)}, u32[]{:S(2)}) copy-start(f32[32,4096]{1,0:T(8,128)} %get-tuple-element.90) | copy-start | bytes 1572868
  336.3 5.5 %copy-start.1 = (f32[128,1024]{1,0:T(8,128)S(1)}, f32[128,1024]{1,0:T(8,128)}, u32[]{:S(2)}) copy-start(f32[128,1024]{1,0:T(8,128)} %get-tuple-element.91) | copy-start | bytes 1572868
  336.3 6.3 %copy-start.5 = (f32[2,32]{1,0:T(2,128)S(1)}, f32[2,32]{1,0:T(2,128)}, u32[]{:S(2)}) copy-start(f32[2,32]{1,0:T(2,128)} %get-tuple-element.92) | copy-start | bytes 772
  336.3 6.9 %copy-start.4 = (f32[6,32]{1,0:T(8,128)S(1)}, f32[6,32]{1,0:T(8,128)}, u32[]{:S(2)}) copy-start(f32[6,32]{1,0:T(8,128)} %get-tuple-element.93) | copy-start | bytes 2308
  336.3 7.4 %copy-start.6 = (f32[1,128]{1,0:T(1,128)S(1)}, f32[1,128]{1,0:T(1,128)}, u32[]{:S(2)}) copy-start(f32[1,128]{1,0:T(1,128)} %get-tuple-element.76) | copy-start | bytes 1540

commit v7 on v6

--- a/solution.py
+++ b/solution.py
@@ -45,9 +45,15 @@
     )
 
 
-def gelu_parts(u):
+def quick_reciprocal(x):
+    first = pl.reciprocal(x, approx=True)
+    return first * (2.0 - x * first)
+
+
+def gelu_parts(u, reciprocal=lambda x: 1.0 / x):
     bell = jnp.exp(-0.5 * u * u)
-    t = 1.0 / (1.0 + (0.3275911 * 0.5**0.5) * jnp.abs(u))
+    below = 1.0 + (0.3275911 * 0.5**0.5) * jnp.abs(u)
+    t = reciprocal(below)
     poly = 1.061405429 * t - 1.453152027
     poly = poly * t + 1.421413741
     poly = poly * t - 0.284496736
@@ -187,8 +193,9 @@
     branch_in,
     n1,
     r1,
+    normed_t,
+    par,
     normed_low,
-    par,
     X,
     W,
     win,
@@ -503,7 +510,9 @@
     normal, inverse = normalize(X[b, 0:count].astype(HIGH) + branch)
     n1[...] = normal
     r1[...] = jnp.broadcast_to(inverse, r1.shape)
-    normed_low[...] = (normal * par[0:1] + par[5:6]).astype(LOW)
+    normed = (normal * par[0:1] + par[5:6]).astype(LOW)
+    normed_low[...] = normed
+    normed_t[...] = normed.T
 
     def store(c, ref, out, which):
         cols = pl.ds(pl.multiple_of(c * chunk, chunk), chunk)
@@ -514,7 +523,7 @@
         cols = pl.ds(pl.multiple_of(c * chunk, chunk), chunk)
         load(c).wait()
         pre = product(normed_low[...], w1v[:, :, :, cols].reshape(width, chunk))
-        value, rate = gelu_parts(pre + hid[:, cols])
+        value, rate = gelu_parts(pre + hid[:, cols], quick_reciprocal)
         act[:, cols] = value.astype(LOW)
         slope[:, cols] = rate.astype(LOW)
         store(c, act, act_out, 0).start()
@@ -570,12 +579,13 @@
             shape(count, width),
             wide(count, width),
             wide(count, 128),
-            shape(count, width),
+            shape(width, count),
             wide(8, width),
         ),
         in_specs=in_hbm(1) + [vmem] * 6 + in_hbm(3),
         out_specs=tuple(in_hbm(5)) + (vmem,) * 12,
         scratch_shapes=[
+            pltpu.VMEM((count, width), LOW),
             pltpu.VMEM((8, count + 16, width), LOW),
             pltpu.VMEM((4, 8, shard + 16, 384), LOW),
             pltpu.VMEM((8, shard + 16, 384), LOW),
@@ -618,22 +628,24 @@
     ORDER = (3, 2, 1, 0)
     COPIES = 16 + 4 * 6 + 3
 
-    def __init__(self, s, share, out, C, S, H, Q, Z, lsem):
+    def __init__(self, s, share, out, C, H, Q, Z, S=None, lsem=None):
         b, z = position()
         to_x, to_y, to_core = (b ^ 2, z), (b ^ 4, z), (b ^ 1, z)
-        self.out, self.C, self.S, self.H, self.Q, self.Z = out, C, S, H, Q, Z
+        self.out, self.C, self.H, self.Q, self.Z = out, C, H, Q, Z
+        self.at = at = lambda e, d: share(b ^ (2 * e), z ^ d) if S is None else S.at[e, d]
         self.mine, self.other, self.halves, self.ahead, self.rest, self.last = ({} for _ in range(6))
         for d in self.ORDER:
             for e in (3, 1, 2, 0):
-                self.mine[d, e] = pltpu.make_async_copy(
-                    share(b ^ (2 * e), z ^ d), S.at[e, d], lsem.at[d * 4 + e]
-                )
+                if S is not None:
+                    self.mine[d, e] = pltpu.make_async_copy(
+                        share(b ^ (2 * e), z ^ d), S.at[e, d], lsem.at[d * 4 + e]
+                    )
                 self.other[d, e] = s.plan(
                     share(b ^ 1 ^ (2 * e), z ^ d), C.at[e, d], to_core, C.at[e, d]
                 )
 
             def send(e, part, to, where):
-                return s.plan(half(S.at[e, d], part), where, to, where)
+                return s.plan(half(at(e, d), part), where, to, where)
 
             self.halves[d] = [send(3, 0, to_x, H.at[d, 0]), send(3, 1, to_y, H.at[d, 1])]
             self.ahead[d] = [
@@ -646,7 +658,7 @@
             ]
             if d:
                 to = (b, z ^ (2 if d == 2 else 1))
-                self.last[d] = s.plan(S.at[0, d], Z.at[d - 1], to, Z.at[d - 1])
+                self.last[d] = s.plan(at(0, d), Z.at[d - 1], to, Z.at[d - 1])
 
     def start(self):
         for d in self.ORDER:
@@ -654,25 +666,34 @@
                 self.mine[d, e].start()
                 self.other[d, e].go()
 
-    def fold(self, d):
-        for e in (3, 1, 2, 0):
-            self.mine[d, e].wait()
+    def give(self, e):
+        for d in self.ORDER:
+            self.other[d, e].go()
+
+    def fold(self, d, chips=(3, 1, 2, 0)):
+        for e in chips:
+            if self.mine:
+                self.mine[d, e].wait()
             self.other[d, e].wait_recv()
-            add_rows(self.S.at[e, d], self.S.at[e, d], self.C.at[e, d])
+            add_rows(self.at(e, d), self.at(e, d), self.C.at[e, d])
             for copy in {3: self.halves[d], 1: self.ahead[d][1:], 2: self.ahead[d][:1], 0: []}[e]:
                 copy.go()
+
+    def fold_chip(self, e):
+        for d in self.ORDER:
+            self.fold(d, (e,))
 
     def relay(self, d):
         for i, e in ((0, 2), (1, 1)):
             self.halves[d][i].wait_recv()
-            part = half(self.S.at[e, d], i)
+            part = half(self.at(e, d), i)
             add_rows(part, part, self.H.at[d, i])
             self.rest[d][i].go()
 
     def collect(self, d):
         for copy in self.ahead[d] + self.rest[d]:
             copy.wait_recv()
-        total = self.S.at[0, d]
+        total = self.at(0, d)
         for i in (0, 1):
             add_rows(total, total, self.Q.at[d, i])
         if d == 2:
@@ -684,37 +705,42 @@
     def total(self):
         for d in (1, 2):
             self.last[d].wait_recv()
-        sum_rows(self.out, self.S.at[0, 0], self.Z.at[0], self.Z.at[1])
-
-    @staticmethod
-    def scratch(rows, columns):
-        lead = (((4, 4), 1), ((4, 4), 1), ((4, 2), 2), ((4, 2), 1), ((3,), 1))
-        shapes = [pltpu.VMEM((*n, rows // cut, columns), LOW) for n, cut in lead]
-        return shapes + [pltpu.SemaphoreType.DMA((16,))]
-
-
-class ReducerAlongZ:
+        sum_rows(self.out, self.at(0, 0), self.Z.at[0], self.Z.at[1])
+
+    LEAD = (((4, 4), 1), ((4, 2), 2), ((4, 2), 1), ((3,), 1))
+
+    @classmethod
+    def scratch(cls, rows, columns, in_place=False):
+        shapes = [pltpu.VMEM((*n, rows // cut, columns), LOW) for n, cut in cls.LEAD]
+        if in_place:
+            return shapes
+        return shapes + [pltpu.VMEM((4, 4, rows, columns), LOW), pltpu.SemaphoreType.DMA((16,))]
+
+
+class ReducerAlongZ(Reducer):
     COPIES = 16 + 4 * 3 + 6
 
-    def __init__(self, s, share, out, C, S, H, Q, Z, lsem):
+    def __init__(self, s, share, out, C, H, Q, Z, S=None, lsem=None):
         b, z = position()
         to_x, to_y, to_core = (b ^ 2, z), (b ^ 4, z), (b ^ 1, z)
-        self.out, self.C, self.S, self.H, self.Q, self.Z = out, C, S, H, Q, Z
+        self.out, self.C, self.H, self.Q, self.Z = out, C, H, Q, Z
+        self.at = at = lambda e, d: share(b ^ (2 * e), z ^ d) if S is None else S.at[e, d]
         self.mine, self.other, self.along = {}, {}, {}
         for e in (3, 1, 2, 0):
             for d in (3, 2, 1, 0):
-                self.mine[e, d] = pltpu.make_async_copy(
-                    share(b ^ (2 * e), z ^ d), S.at[e, d], lsem.at[d * 4 + e]
-                )
+                if S is not None:
+                    self.mine[e, d] = pltpu.make_async_copy(
+                        share(b ^ (2 * e), z ^ d), S.at[e, d], lsem.at[d * 4 + e]
+                    )
                 self.other[e, d] = s.plan(
                     share(b ^ 1 ^ (2 * e), z ^ d), C.at[e, d], to_core, C.at[e, d]
                 )
                 if d:
                     to = (b, z ^ (2 if d == 2 else 1))
-                    self.along[e, d] = s.plan(S.at[e, d], Z.at[e, d - 1], to, Z.at[e, d - 1])
+                    self.along[e, d] = s.plan(at(e, d), Z.at[e, d - 1], to, Z.at[e, d - 1])
 
         def send(e, part, to, where):
-            return s.plan(half(S.at[e, 0], part), where, to, where)
+            return s.plan(half(at(e, 0), part), where, to, where)
 
         self.halves = [send(3, 0, to_x, H.at[0]), send(3, 1, to_y, H.at[1])]
         self.ahead = [
@@ -731,21 +757,26 @@
             self.mine[at].start()
             self.other[at].go()
 
+    def give(self, e):
+        for d in (3, 2, 1, 0):
+            self.other[e, d].go()
+
     def fold(self, e):
         for d in (3, 1, 2, 0):
-            self.mine[e, d].wait()
+            if self.mine:
+                self.mine[e, d].wait()
             self.other[e, d].wait_recv()
-            add_rows(self.S.at[e, d], self.S.at[e, d], self.C.at[e, d])
+            add_rows(self.at(e, d), self.at(e, d), self.C.at[e, d])
             if d in (1, 3):
                 self.along[e, d].go()
 
     def relay(self, e):
         self.along[e, 3].wait_recv()
-        add_rows(self.S.at[e, 2], self.S.at[e, 2], self.Z.at[e, 2])
+        add_rows(self.at(e, 2), self.at(e, 2), self.Z.at[e, 2])
         self.along[e, 2].go()
 
     def collect(self, e):
-        total = self.S.at[e, 0]
+        total = self.at(e, 0)
         for d in (1, 2):
             self.along[e, d].wait_recv()
             add_rows(total, total, self.Z.at[e, d - 1])
@@ -755,20 +786,16 @@
     def cross(self):
         for i, e in ((0, 2), (1, 1)):
             self.halves[i].wait_recv()
-            part = half(self.S.at[e, 0], i)
+            part = half(self.at(e, 0), i)
             add_rows(part, part, self.H.at[i])
             self.rest[i].go()
 
     def total(self):
         for copy in self.ahead + self.rest:
             copy.wait_recv()
-        sum_rows(self.out, self.S.at[0, 0], self.Q.at[0], self.Q.at[1])
-
-    @staticmethod
-    def scratch(rows, columns):
-        lead = (((4, 4), 1), ((4, 4), 1), ((2,), 2), ((2,), 1), ((4, 3), 1))
-        shapes = [pltpu.VMEM((*n, rows // cut, columns), LOW) for n, cut in lead]
-        return shapes + [pltpu.SemaphoreType.DMA((16,))]
+        sum_rows(self.out, self.at(0, 0), self.Q.at[0], self.Q.at[1])
+
+    LEAD = (((4, 4), 1), ((2,), 2), ((2,), 1), ((4, 3), 1))
 
 
 def attend_kernel(qh_ref, kh_ref, v_ref, out_ref, lse_ref):
@@ -1012,10 +1039,8 @@
     sums.start()
     late.fold(3)
     late.fold(1)
+    late.fold(2)
     sums.fold(3)
-    late.fold(2)
-    late.fold(0)
-    sums.fold(2)
     arrive(0)
     for load in loads:
         load.wait()
@@ -1025,21 +1050,21 @@
         return rows_of(grads[:, part])
 
     events = {
-        0: [(late.relay, 3), (late.relay, 1)],
-        1: [(sums.relay, 3)],
-        2: [(late.relay, 2), (late.relay, 0)],
-        3: [(sums.fold, 1)],
-        4: [(sums.relay, 2), (late.collect, 3)],
-        5: [(sums.collect, 3)],
-        6: [(sums.fold, 0), (late.collect, 1)],
-        7: [(late.collect, 2), (arrive, 1)],
-        8: [(tokens.give, 3), (sums.relay, 1)],
-        9: [(tokens.give, 2), (tokens.take, 3), (sums.collect, 2)],
-        10: [(tokens.give, 1), (tokens.take, 2)],
-        11: [(tokens.give, 0), (tokens.take, 1), (sums.relay, 0)],
-        12: [(tokens.take, 0), (late.cross,)],
+        0: [(late.fold, 0)],
+        1: [(sums.fold, 2), (late.relay, 3)],
+        2: [(late.relay, 1)],
+        3: [(sums.fold, 1), (sums.relay, 3)],
+        4: [(late.relay, 2)],
+        5: [(late.relay, 0), (sums.relay, 2)],
+        6: [(sums.fold, 0), (late.collect, 3), (arrive, 1)],
+        7: [(sums.collect, 3), (late.collect, 1)],
+        8: [(sums.relay, 1), (late.collect, 2), (tokens.give, 3), (tokens.give, 2)],
+        9: [(sums.collect, 2), (tokens.give, 1), (tokens.take, 3)],
+        10: [(tokens.give, 0), (tokens.take, 2)],
+        11: [(sums.relay, 0), (late.cross,), (tokens.take, 1)],
+        12: [(tokens.take, 0)],
         13: [(sums.collect, 1), (tokens.relay,)],
-        14: [(late.collect, 0)],
+        15: [(late.collect, 0)],
     }
 
     @pl.loop(0, blocks * slots)
@@ -1128,10 +1153,11 @@
 def middle_kernel(
     chunk,
     small_rows,
+    remote,
     att,
     n1,
     r1,
-    normed_low,
+    normed_t,
     cot_ref,
     par_ref,
     act_hbm,
@@ -1143,7 +1169,7 @@
     d_att_ref,
     small_ref,
     g1_hbm,
-    g2_hbm,
+    g2_out,
     w1,
     w2,
     act,
@@ -1154,6 +1180,7 @@
     d_hid_ref,
     wsem,
     gsem,
+    *buffers,
 ):
     hidden, width = w2.shape
     steps = hidden // chunk
@@ -1176,6 +1203,12 @@
             slope_hbm.at[:, columns(c)], slope.at[:, columns(c)], wsem.at[3, c]
         )
 
+    if remote:
+        b, z = position()
+        barrier = pltpu.get_barrier_semaphore()
+        peers = [(b ^ d, z) for d in (1, 2, 4)] + [(b, z ^ d) for d in (1, 2)]
+        for peer in peers:
+            pl.semaphore_signal(barrier, inc=1, device_id=peer, device_id_type=MESH)
     last = pl.ds(hidden, width)
     for c in range(steps):
         load_act(c).start()
@@ -1209,20 +1242,68 @@
         return pltpu.make_async_copy(w1.at[:, columns(c)], g1_hbm.at[:, columns(c)], gsem.at[0, c])
 
     def store2(c):
-        return pltpu.make_async_copy(w2.at[columns(c)], g2_hbm.at[columns(c)], gsem.at[1, c])
+        return pltpu.make_async_copy(w2.at[columns(c)], g2_out.at[columns(c)], gsem.at[1, c])
+
+    first_events, second_events = {}, {}
+    if remote:
+        pl.semaphore_wait(barrier, len(peers))
+        s = Sender(*buffers[:2])
+        each = w2.shape[0] // (8 * 4)
+        cut = buffers[2].shape[2]
+        plain = lambda bb, zz: w2.at[pl.ds(pl.multiple_of((bb * 4 + zz) * each, each), cut)]
+        upper = lambda bb, zz: w2.at[
+            pl.ds(pl.multiple_of((bb * 4 + zz) * each + cut, 16), each - cut)
+        ]
+        sums = Reducer(s, plain, g2_out.at[pl.ds(0, cut)], *buffers[2:6])
+        late = ReducerAlongZ(s, upper, g2_out.at[pl.ds(cut, each - cut)], *buffers[6:])
+        first_events = {
+            0: [(late.give, 3), (sums.give, 3)],
+            2: [(late.give, 2), (sums.give, 2)],
+            3: [(late.fold, 3), (sums.fold_chip, 3)],
+            4: [(late.give, 1), (sums.give, 1)],
+            6: [(late.give, 0), (sums.give, 0), (late.relay, 3)],
+            7: [(late.fold, 2), (sums.fold_chip, 2)],
+        }
+        second_events = {
+            0: [(late.fold, 1), (sums.fold_chip, 1)],
+            1: [(late.relay, 2), (sums.relay, 3)],
+            2: [(late.relay, 1), (sums.relay, 2)],
+            3: [(late.fold, 0), (sums.fold_chip, 0), (late.collect, 3)],
+            4: [(late.relay, 0), (sums.relay, 1), (sums.collect, 3)],
+            5: [(late.collect, 2), (sums.relay, 0)],
+            6: [(sums.collect, 2), (late.collect, 1)],
+            7: [(late.cross,)],
+        }
+
+    def run(events, step):
+        for at, some in events.items():
+
+            @pl.when(step == at)
+            def _(some=some):
+                for event, *what in some:
+                    event(*what)
 
     @pl.loop(0, steps)
-    def _(c):
+    def _(step):
+        c = b ^ (7 - step) if remote else step
         load_slope(c).wait()
-        load1(c).wait()
         d_act = product_nt(low[...], w2[columns(c), :])
         d_pre = (d_act * slope[:, columns(c)].astype(HIGH)).astype(LOW)
         d_hid_ref[:, columns(c)] = column_sum(d_pre)
+        slope[:, columns(c)] = d_pre
+        w2[columns(c), :] = product_tn(act[:, columns(c)], low[...]).astype(LOW)
+        if not remote:
+            store2(c).start()
+        run(first_events, step)
+
+    @pl.loop(0, steps)
+    def _(c):
+        load1(c).wait()
+        d_pre = slope[:, columns(c)]
         acc[...] += product_nt(d_pre, w1[:, columns(c)])
-        w2[columns(c), :] = product_tn(act[:, columns(c)], low[...]).astype(LOW)
-        store2(c).start()
-        w1[:, columns(c)] = product_tn(normed_low[...], d_pre).astype(LOW)
+        w1[:, columns(c)] = product(normed_t[...], d_pre).astype(LOW)
         store1(c).start()
+        run(second_events, c)
 
     d_normed = acc[...]
     normal = n1[...]
@@ -1251,30 +1332,46 @@
         small_ref[i, j : j + 1, 6 * small_rows : 6 * small_rows + part] = d_hid_ref[
             :, at * part : (at + 1) * part
         ]
+    if remote:
+        sums.collect(1)
+        late.collect(0)
+        sums.collect(0)
+        sums.total()
+        late.total()
+        s.drain()
     for c in range(steps):
         store1(c).wait()
-        store2(c).wait()
+        if not remote:
+            store2(c).wait()
     store_out.wait()
 
 
-def middle(att, n1, r1, normed_low, cot, par, act, slope, w1, w2, pieces, planes):
+def middle(att, n1, r1, normed_t, cot, par, act, slope, w1, w2, pieces, planes, remote):
     count, width = cot.shape
     hidden = w2.shape[0]
     chunk = 512
     shape = jax.ShapeDtypeStruct
     vmem = pl.BlockSpec(memory_space=pltpu.VMEM)
+    shard = hidden // (pieces * planes)
+    late = shard // 4
+    buffers, params = [], {}
+    if remote:
+        buffers = pair_of_semaphores(Reducer.COPIES + ReducerAlongZ.COPIES)
+        buffers += Reducer.scratch(shard - late, width, in_place=True)
+        buffers += ReducerAlongZ.scratch(late, width, in_place=True)
+        params = dict(collective_id=4, has_side_effects=True)
     return pl.pallas_call(
-        functools.partial(middle_kernel, chunk, width // (pieces * planes)),
+        functools.partial(middle_kernel, chunk, width // (pieces * planes), remote),
         out_shape=(
             shape((count, width), LOW),
             shape((count, width), HIGH),
             shape((pieces, count, width // pieces), LOW),
             shape((pieces, -(-planes // 8) * 8, 384), HIGH),
             shape(w1.shape, LOW),
-            shape(w2.shape, LOW),
+            shape((shard, width), HIGH) if remote else shape(w2.shape, LOW),
         ),
         in_specs=[vmem] * 6 + in_hbm(4),
-        out_specs=(vmem,) * 4 + tuple(in_hbm(2)),
+        out_specs=(vmem,) * 4 + tuple(in_hbm(1)) + ((vmem,) if remote else tuple(in_hbm(1))),
         scratch_shapes=[
             pltpu.VMEM(w1.shape, LOW),
             pltpu.VMEM(w2.shape, LOW),
@@ -1286,10 +1383,11 @@
             pltpu.VMEM((1, hidden), HIGH),
             pltpu.SemaphoreType.DMA((4, hidden // chunk + 1)),
             pltpu.SemaphoreType.DMA((2, hidden // chunk + 1)),
-        ],
-        compiler_params=pltpu.CompilerParams(vmem_limit_bytes=VMEM_LIMIT),
+        ]
+        + buffers,
+        compiler_params=pltpu.CompilerParams(vmem_limit_bytes=VMEM_LIMIT, **params),
         name="middle",
-    )(att, n1, r1, normed_low, cot, par, act, slope, w1, w2)
+    )(att, n1, r1, normed_t, cot, par, act, slope, w1, w2)
 
 
 def finish_kernel(
@@ -1301,16 +1399,15 @@
     tok0,
     small,
     x_hbm,
-    g2,
     tok_out,
     in_out,
     gains_out,
     biases_out,
     hidden_out,
-    o2,
     first_rows,
     x,
     D,
+    P,
     R,
     Z,
     M,
@@ -1335,61 +1432,31 @@
         load.start()
     greet([(b ^ d, z) for d in range(1, 8)] + [(b, z ^ d) for d in (1, 2, 3)])
     s = Sender(send, recv)
-    cut = buffers[0].shape[2]
-    lower, upper = pl.ds(0, cut), pl.ds(cut, o2.shape[0] - cut)
-    sums = Reducer(s, lambda bb, zz: g2.at[bb, zz, lower], o2.at[lower], *buffers[:6])
-    late = ReducerAlongZ(s, lambda bb, zz: g2.at[bb, zz, upper], o2.at[upper], *buffers[6:12])
 
     def piece(i):
         mixed = jnp.concatenate([ref[i, 1] for ref in (dq, dk, dv)], axis=-1)
         return product_nt(mixed, w[...])
 
-    tokens = TokenSums(s, piece, *buffers[12:])
+    tokens = TokenSums(s, piece, *buffers)
     small_in = [
         s.go(small.at[b ^ d], M.at[d - 1], (b ^ d, z), M.at[d - 1]) for d in range(1, 8)
     ]
-    late.start()
-    tokens.give(3)
-    sums.start()
-    tokens.give(2)
-    tokens.give(1)
-    tokens.give(0)
-    late.fold(3)
-    late.fold(1)
-    tokens.take(3)
-    sums.fold(3)
-    late.relay(3)
-    late.fold(2)
-    sums.fold(2)
-    tokens.take(2)
-    sums.relay(3)
-    late.fold(0)
-    late.relay(1)
-    tokens.take(1)
-    tokens.take(0)
-    sums.fold(1)
-    sums.relay(2)
-    late.relay(2)
-    late.collect(3)
-
     total = jnp.zeros((width, w.shape[1]), HIGH)
     for i in range(blocks):
         loads[i].wait()
         mixed = jnp.concatenate([ref[i].reshape(count, -1) for ref in (dq, dk, dv)], axis=-1)
         total = total + product_tn(x[i], mixed)
     D[...] = total.astype(LOW).reshape(D.shape)
-    grads_in = [
-        s.go(D.at[b ^ d], R.at[b], (b ^ d, z), R.at[b ^ d]) for d in range(1, 8)
-    ]
-    R[b] = D[b]
-    sums.collect(3)
-    sums.fold(0)
-    late.relay(0)
-    tokens.relay()
-    sums.relay(1)
-    late.collect(1)
-    sums.collect(2)
-    late.collect(2)
+    share_rows = D.shape[1] // 4
+
+    def share(d):
+        return D.at[:, pl.ds(pl.multiple_of((z ^ d) * share_rows, share_rows), share_rows)]
+
+    in_z = [s.go(share(d), Z.at[d - 1], (b, z ^ d), Z.at[d - 1]) for d in (1, 2, 3)]
+    for e in (3, 2, 1, 0):
+        tokens.give(e)
+    for e in (3, 2, 1, 0):
+        tokens.take(e)
 
     N[...] = small[b]
     for i in range(7):
@@ -1402,17 +1469,17 @@
         N[row : row + 1, 0:128] = whole
     small_z = [s.go(N, T.at[d - 1], (b, z ^ d), T.at[d - 1]) for d in (1, 2, 3)]
 
-    sums.relay(0)
-    late.cross()
-    for copy in grads_in:
+    for copy in in_z:
         copy.wait_recv()
-    share_rows = R.shape[1] // 4
-
-    def share(d):
-        return R.at[:, pl.ds(pl.multiple_of((z ^ d) * share_rows, share_rows), share_rows)]
-
-    in_z = [s.go(share(d), Z.at[d - 1], (b, z ^ d), Z.at[d - 1]) for d in (1, 2, 3)]
-    sums.collect(1)
+    plane = share(0)[...].astype(HIGH)
+    for i in range(3):
+        plane = plane + Z[i].astype(HIGH)
+    P[...] = plane
+    grads_in = [
+        s.go(P.at[b ^ d], R.at[b], (b ^ d, z), R.at[b ^ d]) for d in range(1, 8)
+    ]
+    R[b] = P[b]
+    tokens.relay()
     for copy in small_z:
         copy.wait_recv()
     vectors = ((N[...] + T[0]) + T[1]) + T[2]
@@ -1427,32 +1494,22 @@
     for k in range(2, 6):
         biases_out[k : k + 1] = row[:, k * n : (k + 1) * n]
     hidden_out[...] = row[:, 6 * n : 6 * n + hidden_out.shape[1]]
-    for copy in in_z:
+    for copy in grads_in:
         copy.wait_recv()
-    terms = [share(0), Z.at[0], Z.at[1], Z.at[2]]
     for i in range(blocks):
-        block = terms[0][i].astype(HIGH)
-        for term in terms[1:]:
-            block = block + term[i].astype(HIGH)
         for k in range(3):
             at = k * width + i * 128
-            in_out[:, at : at + 128] = block[:, k * 128 : (k + 1) * 128]
-    late.collect(0)
-    sums.collect(0)
-    sums.total()
-    late.total()
+            in_out[:, at : at + 128] = R[i, :, k * 128 : (k + 1) * 128]
     for load in loads[blocks:]:
         load.wait()
     tok_out[rows:] = first_rows[...] + tokens.total()
     s.drain()
 
 
-def finish(dq, dk, dv, w, d_first, tok0, small, x, g2):
+def finish(dq, dk, dv, w, d_first, tok0, small, x):
     rows, width = tok0.shape
     blocks, columns = dq.shape[0], w.shape[1]
     share = width // (4 * blocks)
-    shard = g2.shape[2]
-    late = shard // 4
     vmem = pl.BlockSpec(memory_space=pltpu.VMEM)
     shape = lambda *s: jax.ShapeDtypeStruct(s, HIGH)
     low = lambda *s: pltpu.VMEM(s, LOW)
@@ -1465,33 +1522,29 @@
             shape(share, 3 * width),
             shape(2, share),
             shape(6, share),
-            shape(1, shard),
-            shape(shard, width),
+            shape(1, 4 * share),
         ),
-        in_specs=[vmem] * 4 + in_hbm(2) + [vmem] + in_hbm(2),
-        out_specs=(vmem,) * 6,
+        in_specs=[vmem] * 4 + in_hbm(2) + [vmem] + in_hbm(1),
+        out_specs=(vmem,) * 5,
         scratch_shapes=[
             wide(rows, width),
             low(blocks, 2 * rows, width),
             low(blocks, 4 * share, columns),
-            low(blocks, 4 * share, columns),
+            wide(blocks, share, columns),
+            wide(blocks, share, columns),
             low(3, blocks, share, columns),
             wide(7, *tile),
             wide(*tile),
             wide(3, *tile),
             pltpu.SemaphoreType.DMA((blocks + 2,)),
         ]
-        + pair_of_semaphores(
-            20 + Reducer.COPIES + ReducerAlongZ.COPIES + TokenSums.COPIES
-        )
-        + Reducer.scratch(shard - late, width)
-        + ReducerAlongZ.scratch(late, width)
+        + pair_of_semaphores(20 + TokenSums.COPIES)
         + TokenSums.scratch(rows, width),
         compiler_params=pltpu.CompilerParams(
             collective_id=3, has_side_effects=True, vmem_limit_bytes=VMEM_LIMIT
         ),
         name="finish",
-    )(dq, dk, dv, w, d_first, tok0, small, x, g2)
+    )(dq, dk, dv, w, d_first, tok0, small, x)
 
 
 def swap(pieces):
@@ -1561,7 +1614,7 @@
             reduce_weight,
         )
         X, W1, W2, act, slope, W, _, qh, kh, v, att, lse = front_out[:12]
-        attended, n1, r1, normed_low, cuts = front_out[12:]
+        attended, n1, r1, normed_t, cuts = front_out[12:]
         W1, W2 = W1.reshape(width, -1), W2.reshape(hidden, width)
     else:
         code = (segment + 4 * (1 - present)).reshape(1, count).astype(LOW)
@@ -1588,20 +1641,20 @@
         normed_low = (n1 * gain[0] + bias[3]).astype(LOW)
         act, slope = gelu_parts(product(normed_low, W1[:, :hidden]) + hidden_full)
         act, slope = act.astype(LOW), slope.astype(LOW)
+        normed_t = normed_low.T
     cot = cotangent.reshape(count, width)
     middle_out = middle(
-        attended, n1, r1, normed_low, cot, cuts, act, slope, W1, W2, n_blk, n_dp
+        attended, n1, r1, normed_t, cot, cuts, act, slope, W1, W2, n_blk, n_dp, fast
     )
     output, d_first, d_att, small_rows, grad_both, grad_reduce = middle_out
     output = output.reshape(slots, rows, width)
     if fast:
         grad_both = grad_both.reshape(n_blk, n_dp, shard, -1)
-        grad_reduce = grad_reduce.reshape(n_blk, n_dp, -1, width)
         dq, dk, dv, sum_expand, sum_output, tok0 = back(
             d_att, qh, kh, v, att, lse, W, d_first, grad_both
         )
-        grad_tokens, grad_input, d_gains, d_biases, d_hidden, sum_reduce = finish(
-            dq, dk, dv, W, d_first, tok0, small_rows, X, grad_reduce
+        grad_tokens, grad_input, d_gains, d_biases, d_hidden = finish(
+            dq, dk, dv, W, d_first, tok0, small_rows, X
         )
         return (
             output,
@@ -1609,7 +1662,7 @@
             grad_input,
             sum_output,
             sum_expand,
-            sum_reduce,
+            grad_reduce,
             d_gains,
             d_biases,
             d_hidden.reshape(-1),

time: 349 us -> 330 us (0.946)
  Pallas kernels: 336 us -> 315 us
    pallas_call x1, Pallas kernels: 73.5 us -> 37.8 us  [finish(): pl.pallas_call(finish_kernel, out_shape=(shape(2 * rows, width), shape(sh...]
    pallas_call x1, Pallas kernels: 38.5 us -> 60.1 us  [middle(): pl.pallas_call(functools.partial(middle_kernel, chunk, width // (pieces *...]
    pallas_call x1, Pallas kernels: 87.7 us -> 80.6 us  [back(): pl.pallas_call(back_kernel, out_shape=(shape(v.shape, LOW),) * 3 + (shape...]
    unnamed x22 -> x25, local copies, waits for them, and re-layouts: 7.95 us -> 8.82 us
where the time goes in v7:
time: 330 us; the launch traced here: 325 us
  Pallas kernels  315 us (95%)
  local copies, waits for them, and re-layouts  8.82 us (3%)
    pallas_call x1, Pallas kernels, front(): pl.pallas_call(front_kernel, out_shape=(shape(8, count + 16, width), shap...  137 us
    pallas_call x1, Pallas kernels, back(): pl.pallas_call(back_kernel, out_shape=(shape(v.shape, LOW),) * 3 + (shape...  80.6 us
    pallas_call x1, Pallas kernels, middle(): pl.pallas_call(functools.partial(middle_kernel, chunk, width // (pieces *...  60.1 us
    pallas_call x1, Pallas kernels, finish(): pl.pallas_call(finish_kernel, out_shape=(shape(2 * rows, width), shape(sh...  37.8 us
    unnamed x25, local copies, waits for them, and re-layouts  8.82 us

profile of v7, /device:TPU:0, one launch (start us, length us, event | category | flops | bytes accessed | tf_op | source)
XLA Modules:
  0.0 325.3 jit_solution(13107321248582098966)
XLA Ops:
  0.6 136.8 %front.1 = (bf16[8,528,1024]{2,1,0:T(8,128)(2,1)}, bf16[8,4,32,5120]{3,2,1,0:T(8,128)(2,1)}, bf16[8,4,128,1024]{3,2,1,0:T(8,128)(2,1)}, bf16[512,4096]{1,0:T(8,1...) custom-call(bf16[512,1024]{1,0:T(8,128)(2,1)} %bitcast.14, ...), custom_call_target="tpu_custom_call" | custom-call | tf_op jit(solution)/shard_map/front/pallas_call | solution.py:564
  137.4 60.1 %middle.1 = (bf16[512,1024]{1,0:T(8,128)(2,1)}, f32[512,1024]{1,0:T(8,128)}, bf16[8,512,128]{2,1,0:T(8,128)(2,1)}, f32[8,8,384]{2,1,0:T(8,128)}, bf16[1024,5120]{1,0:T(8,128)(2,1)}, /*index=5*/f32[128,1024]{1,0:T(8,128)}) custom-call(bf16[512,1024]{1,0:T(8,128)(2,1)} %get-tuple-element.42.att, f32[512,1024]{1,0:T(8,128)} %get-tuple-element.43.n1, ...), custom_call_target="tpu_custom_call" | custom-call | tf_op jit(solution)/shard_map/middle/pallas_call | solution.py:1363
  197.5 80.6 %back.1 = (bf16[8,2,256,128]{3,2,1,0:T(8,128)(2,1)}, bf16[8,2,256,128]{3,2,1,0:T(8,128)(2,1)}, bf16[8,2,256,128]{3,2,1,0:T(8,128)(2,1)}, f32[32,4096]{1,0:T(8,12...) custom-call(bf16[8,512,128]{2,1,0:T(8,128)(2,1)} %get-tuple-element.52.d_att, ...), custom_call_target="tpu_custom_call" | custom-call | tf_op jit(solution)/shard_map/back/pallas_call | solution.py:1119
  278.1 0.0 copy-start
  278.2 37.8 %finish.1 = (f32[512,1024]{1,0:T(8,128)}, f32[32,3072]{1,0:T(8,128)}, f32[2,32]{1,0:T(2,128)}, f32[6,32]{1,0:T(8,128)}, f32[1,128]{1,0:T(1,128)}) custom-call(bf16[8,2,256,128]{3,2,1,0:T(8,128)(2,1)} %get-tuple-element.61.dq, bf16[8,2,256,128]{3,2,1,0:T(8,128)(2,1)} %get-tuple-element.62.dk, bf16[8,2,256,128]{3,2,1,0:T(8,128)(2,1)} %get-tuple-element.63.dv, ...), custom_call_target="tpu_custom_call" | custom-call | tf_op jit(solution)/shard_map/finish/pallas_call | solution.py:1518
  316.0 0.0 copy-start.3
  316.0 0.0 copy-start.4
  316.0 0.0 copy-start.2
  316.0 0.0 copy-done
  316.0 0.0 copy-start.1
  316.1 1.0 copy.29
  317.0 0.0 copy-start.6
  317.0 0.0 copy-start.5
  317.0 0.0 copy-start.7
  317.0 3.2 copy.30
  320.2 0.0 copy-done.3
  320.2 0.7 copy.31
  320.9 0.0 copy-done.4
  320.9 0.7 copy.32
  321.6 0.0 copy-done.2
  321.6 0.8 copy.33
  322.4 0.0 copy-done.1
  322.4 0.8 copy.34
  323.2 0.0 copy-done.6
  323.2 0.6 copy.35
  323.8 0.0 copy-done.5
  323.8 0.6 copy.36
  324.4 0.0 copy-done.7
  324.4 0.5 copy.37
Async XLA Ops:
  278.1 37.9 %copy-start = (bf16[512,1024]{1,0:T(8,128)(2,1)S(1)}, bf16[512,1024]{1,0:T(8,128)(2,1)}, u32[]{:S(2)}) copy-start(bf16[512,1024]{1,0:T(8,128)(2,1)} %get-tuple-element.51) | copy-start | bytes 3145732
  316.0 4.2 %copy-start.3 = (f32[32,3072]{1,0:T(8,128)S(1)}, f32[32,3072]{1,0:T(8,128)}, u32[]{:S(2)}) copy-start(f32[32,3072]{1,0:T(8,128)} %get-tuple-element.86) | copy-start | bytes 1179652
  316.0 4.9 %copy-start.4 = (f32[32,1024]{1,0:T(8,128)S(1)}, f32[32,1024]{1,0:T(8,128)}, u32[]{:S(2)}) copy-start(f32[32,1024]{1,0:T(8,128)} %get-tuple-element.87) | copy-start | bytes 393220
  316.0 5.6 %copy-start.2 = (f32[32,4096]{1,0:T(8,128)S(1)}, f32[32,4096]{1,0:T(8,128)}, u32[]{:S(2)}) copy-start(f32[32,4096]{1,0:T(8,128)} %get-tuple-element.88) | copy-start | bytes 1572868
  316.0 6.4 %copy-start.1 = (f32[128,1024]{1,0:T(8,128)S(1)}, f32[128,1024]{1,0:T(8,128)}, u32[]{:S(2)}) copy-start(f32[128,1024]{1,0:T(8,128)} %get-tuple-element.89) | copy-start | bytes 1572868
  317.0 6.2 %copy-start.6 = (f32[2,32]{1,0:T(2,128)S(1)}, f32[2,32]{1,0:T(2,128)}, u32[]{:S(2)}) copy-start(f32[2,32]{1,0:T(2,128)} %get-tuple-element.90) | copy-start | bytes 772
  317.0 6.7 %copy-start.5 = (f32[6,32]{1,0:T(8,128)S(1)}, f32[6,32]{1,0:T(8,128)}, u32[]{:S(2)}) copy-start(f32[6,32]{1,0:T(8,128)} %get-tuple-element.91) | copy-start | bytes 2308
  317.0 7.3 %copy-start.7 = (f32[1,128]{1,0:T(1,128)S(1)}, f32[1,128]{1,0:T(1,128)}, u32[]{:S(2)}) copy-start(f32[1,128]{1,0:T(1,128)} %get-tuple-element.74) | copy-start | bytes 1540

commit v8 on v7

--- a/solution.py
+++ b/solution.py
@@ -628,7 +628,7 @@
     ORDER = (3, 2, 1, 0)
     COPIES = 16 + 4 * 6 + 3
 
-    def __init__(self, s, share, out, C, H, Q, Z, S=None, lsem=None):
+    def __init__(self, s, share, out, C, H, Q, Z=None, S=None, lsem=None):
         b, z = position()
         to_x, to_y, to_core = (b ^ 2, z), (b ^ 4, z), (b ^ 1, z)
         self.out, self.C, self.H, self.Q, self.Z = out, C, H, Q, Z
@@ -656,9 +656,18 @@
                 send(2, 0, to_y, half(Q.at[d, 1], 0)),
                 send(1, 1, to_x, half(Q.at[d, 0], 1)),
             ]
-            if d:
+            if d and Z is not None:
                 to = (b, z ^ (2 if d == 2 else 1))
                 self.last[d] = s.plan(at(0, d), Z.at[d - 1], to, Z.at[d - 1])
+
+    def keep_for_later(self, sems):
+        self.keep = [
+            pltpu.make_async_copy(self.at(*self.kept(d)), self.out.at[d], sems.at[d])
+            for d in range(4)
+        ]
+
+    def kept(self, d):
+        return 0, d
 
     def start(self):
         for d in self.ORDER:
@@ -696,6 +705,9 @@
         total = self.at(0, d)
         for i in (0, 1):
             add_rows(total, total, self.Q.at[d, i])
+        if self.Z is None:
+            self.keep[d].start()
+            return
         if d == 2:
             self.last[3].wait_recv()
             add_rows(total, total, self.Z.at[2])
@@ -721,6 +733,7 @@
     COPIES = 16 + 4 * 3 + 6
 
     def __init__(self, s, share, out, C, H, Q, Z, S=None, lsem=None):
+        self.partial = H is None
         b, z = position()
         to_x, to_y, to_core = (b ^ 2, z), (b ^ 4, z), (b ^ 1, z)
         self.out, self.C, self.H, self.Q, self.Z = out, C, H, Q, Z
@@ -739,6 +752,9 @@
                     to = (b, z ^ (2 if d == 2 else 1))
                     self.along[e, d] = s.plan(at(e, d), Z.at[e, d - 1], to, Z.at[e, d - 1])
 
+        if self.partial:
+            return
+
         def send(e, part, to, where):
             return s.plan(half(at(e, 0), part), where, to, where)
 
@@ -780,8 +796,14 @@
         for d in (1, 2):
             self.along[e, d].wait_recv()
             add_rows(total, total, self.Z.at[e, d - 1])
+        if self.partial:
+            self.keep[e].start()
+            return
         for copy in {3: self.halves, 1: self.ahead[1:], 2: self.ahead[:1], 0: []}[e]:
             copy.go()
+
+    def kept(self, e):
+        return e, 0
 
     def cross(self):
         for i, e in ((0, 2), (1, 1)):
@@ -796,6 +818,79 @@
         sum_rows(self.out, self.at(0, 0), self.Q.at[0], self.Q.at[1])
 
     LEAD = (((4, 4), 1), ((2,), 2), ((2,), 1), ((4, 3), 1))
+
+
+class PlaneSums:
+    COPIES = 3
+
+    def __init__(self, s, out, T, Z):
+        b, z = position()
+        self.out, self.T, self.Z = out, T, Z
+        self.last = {
+            d: s.plan(T.at[d], Z.at[d - 1], (b, z ^ (2 if d == 2 else 1)), Z.at[d - 1])
+            for d in (3, 2, 1)
+        }
+
+    def start(self):
+        self.last[3].go()
+        self.last[1].go()
+
+    def relay(self):
+        self.last[3].wait_recv()
+        add_rows(self.T.at[2], self.T.at[2], self.Z.at[2])
+        self.last[2].go()
+
+    def total(self):
+        for d in (1, 2):
+            self.last[d].wait_recv()
+        sum_rows(self.out, self.T.at[0], self.Z.at[0], self.Z.at[1])
+
+    @staticmethod
+    def scratch(rows, columns):
+        return [pltpu.VMEM((n, rows, columns), LOW) for n in (4, 3)]
+
+
+class ChipSums:
+    COPIES = 6
+
+    def __init__(self, s, out, U, H, Q):
+        b, z = position()
+        to_x, to_y = (b ^ 2, z), (b ^ 4, z)
+        self.out, self.U, self.H, self.Q = out, U, H, Q
+
+        def send(e, part, to, where):
+            return s.plan(half(U.at[e], part), where, to, where)
+
+        self.halves = [send(3, 0, to_x, H.at[0]), send(3, 1, to_y, H.at[1])]
+        self.ahead = [
+            send(2, 1, to_y, half(Q.at[1], 1)),
+            send(1, 0, to_x, half(Q.at[0], 0)),
+        ]
+        self.rest = [
+            send(2, 0, to_y, half(Q.at[1], 0)),
+            send(1, 1, to_x, half(Q.at[0], 1)),
+        ]
+
+    def start(self):
+        for copy in self.halves + self.ahead:
+            copy.go()
+
+    def relay(self):
+        for i, e in ((0, 2), (1, 1)):
+            self.halves[i].wait_recv()
+            part = half(self.U.at[e], i)
+            add_rows(part, part, self.H.at[i])
+            self.rest[i].go()
+
+    def total(self):
+        for copy in self.ahead + self.rest:
+            copy.wait_recv()
+        sum_rows(self.out, self.U.at[0], self.Q.at[0], self.Q.at[1])
+
+    @staticmethod
+    def scratch(rows, columns):
+        shapes = (4, rows), (2, rows // 2), (2, rows)
+        return [pltpu.VMEM((*n, columns), LOW) for n in shapes]
 
 
 def attend_kernel(qh_ref, kh_ref, v_ref, out_ref, lse_ref):
@@ -967,11 +1062,14 @@
     w_in,
     first,
     g1,
+    g2_planes,
+    g2_late,
     dq,
     dk,
     dv,
     o1,
     out_o,
+    o2,
     tok,
     qh,
     kh,
@@ -1003,6 +1101,8 @@
                 (lse_in, lse),
                 (w_in, w),
                 (first.at[pl.ds(0, rows)], first_rows),
+                (g2_planes, buffers[18]),
+                (g2_late, buffers[20]),
             )
         )
     ]
@@ -1034,7 +1134,10 @@
         mixed = jnp.concatenate([ref[i, 0] for ref in (dq, dk, dv)], axis=-1)
         return product_nt(mixed, w[...])
 
-    tokens = TokenSums(s, piece, *buffers[12:])
+    tokens = TokenSums(s, piece, *buffers[12:18])
+    cut = g2_planes.shape[1]
+    planes = PlaneSums(s, o2.at[pl.ds(0, cut)], *buffers[18:20])
+    chips = ChipSums(s, o2.at[pl.ds(cut, g2_late.shape[1])], *buffers[20:])
     late.start()
     sums.start()
     late.fold(3)
@@ -1057,14 +1160,14 @@
         4: [(late.relay, 2)],
         5: [(late.relay, 0), (sums.relay, 2)],
         6: [(sums.fold, 0), (late.collect, 3), (arrive, 1)],
-        7: [(sums.collect, 3), (late.collect, 1)],
+        7: [(sums.collect, 3), (late.collect, 1), (planes.start,), (chips.start,)],
         8: [(sums.relay, 1), (late.collect, 2), (tokens.give, 3), (tokens.give, 2)],
-        9: [(sums.collect, 2), (tokens.give, 1), (tokens.take, 3)],
+        9: [(sums.collect, 2), (tokens.give, 1), (tokens.take, 3), (chips.relay,)],
         10: [(tokens.give, 0), (tokens.take, 2)],
-        11: [(sums.relay, 0), (late.cross,), (tokens.take, 1)],
+        11: [(sums.relay, 0), (late.cross,), (tokens.take, 1), (planes.relay,)],
         12: [(tokens.take, 0)],
         13: [(sums.collect, 1), (tokens.relay,)],
-        15: [(late.collect, 0)],
+        15: [(late.collect, 0), (planes.total,), (chips.total,)],
     }
 
     @pl.loop(0, blocks * slots)
@@ -1108,7 +1211,7 @@
     s.drain()
 
 
-def back(d_att, qh, kh, v, att, lse, w, d_first, g1):
+def back(d_att, qh, kh, v, att, lse, w, d_first, g1, g2_planes, g2_late):
     blocks, slots, rows, lanes = v.shape
     shape = jax.ShapeDtypeStruct
     shard, total = g1.shape[2:]
@@ -1122,10 +1225,11 @@
         + (
             shape((shard, total - width), HIGH),
             shape((shard, width), HIGH),
+            shape((g2_planes.shape[1] + g2_late.shape[1], width), HIGH),
             shape((rows, width), HIGH),
         ),
-        in_specs=in_hbm(9),
-        out_specs=(vmem,) * 6,
+        in_specs=in_hbm(11),
+        out_specs=(vmem,) * 7,
         scratch_shapes=[scratch(a) for a in (qh, kh, v, att, lse, w)]
         + [
             pltpu.VMEM((rows, width), HIGH),
@@ -1133,17 +1237,22 @@
             pltpu.VMEM(d_att.shape, LOW),
             pltpu.VMEM((lanes, blocks * rows), HIGH),
             pltpu.VMEM((8, blocks * rows), HIGH),
-            pltpu.SemaphoreType.DMA((8,)),
+            pltpu.SemaphoreType.DMA((10,)),
         ]
-        + pair_of_semaphores(7 * slots + Reducer.COPIES + ReducerAlongZ.COPIES + TokenSums.COPIES)
+        + pair_of_semaphores(
+            7 * slots
+            + sum(c.COPIES for c in (Reducer, ReducerAlongZ, TokenSums, PlaneSums, ChipSums))
+        )
         + Reducer.scratch(shard, total - late)
         + ReducerAlongZ.scratch(shard, late)
-        + TokenSums.scratch(rows, width),
+        + TokenSums.scratch(rows, width)
+        + PlaneSums.scratch(*g2_planes.shape[1:])
+        + ChipSums.scratch(*g2_late.shape[1:]),
         compiler_params=pltpu.CompilerParams(
             collective_id=2, has_side_effects=True, vmem_limit_bytes=VMEM_LIMIT
         ),
         name="back",
-    )(d_att, qh, kh, v, att, lse, w, d_first, g1)
+    )(d_att, qh, kh, v, att, lse, w, d_first, g1, g2_planes, g2_late)
 
 
 def column_sum(block):
@@ -1170,18 +1279,11 @@
     small_ref,
     g1_hbm,
     g2_out,
-    w1,
-    w2,
-    act,
-    slope,
-    acc,
-    low,
-    sums_ref,
-    d_hid_ref,
-    wsem,
-    gsem,
-    *buffers,
+    *rest,
 ):
+    if remote:
+        g2_late, *rest = rest
+    w1, w2, act, slope, acc, low, sums_ref, d_hid_ref, wsem, gsem, *buffers = rest
     hidden, width = w2.shape
     steps = hidden // chunk
     pieces, _, held = d_att_ref.shape
@@ -1254,25 +1356,28 @@
         upper = lambda bb, zz: w2.at[
             pl.ds(pl.multiple_of((bb * 4 + zz) * each + cut, 16), each - cut)
         ]
-        sums = Reducer(s, plain, g2_out.at[pl.ds(0, cut)], *buffers[2:6])
-        late = ReducerAlongZ(s, upper, g2_out.at[pl.ds(cut, each - cut)], *buffers[6:])
+        sums = Reducer(s, plain, g2_out, *buffers[2:5])
+        late = ReducerAlongZ(s, upper, g2_late, buffers[5], None, None, buffers[6])
+        sums.keep_for_later(buffers[7])
+        late.keep_for_later(buffers[8])
         first_events = {
             0: [(late.give, 3), (sums.give, 3)],
             2: [(late.give, 2), (sums.give, 2)],
             3: [(late.fold, 3), (sums.fold_chip, 3)],
             4: [(late.give, 1), (sums.give, 1)],
+            5: [(late.fold, 2), (sums.fold_chip, 2)],
             6: [(late.give, 0), (sums.give, 0), (late.relay, 3)],
-            7: [(late.fold, 2), (sums.fold_chip, 2)],
+            7: [(late.fold, 1), (sums.fold_chip, 1)],
         }
         second_events = {
-            0: [(late.fold, 1), (sums.fold_chip, 1)],
-            1: [(late.relay, 2), (sums.relay, 3)],
-            2: [(late.relay, 1), (sums.relay, 2)],
-            3: [(late.fold, 0), (sums.fold_chip, 0), (late.collect, 3)],
-            4: [(late.relay, 0), (sums.relay, 1), (sums.collect, 3)],
-            5: [(late.collect, 2), (sums.relay, 0)],
-            6: [(sums.collect, 2), (late.collect, 1)],
-            7: [(late.cross,)],
+            0: [(late.relay, 2)],
+            1: [(late.fold, 0), (sums.fold_chip, 0), (late.relay, 1)],
+            2: [(sums.relay, 3), (sums.relay, 2)],
+            3: [(late.relay, 0), (sums.relay, 1)],
+            4: [(sums.relay, 0), (late.collect, 3)],
+            5: [(late.collect, 2)],
+            6: [(late.collect, 1), (sums.collect, 3)],
+            7: [(sums.collect, 2)],
         }
 
     def run(events, step):
@@ -1336,8 +1441,8 @@
         sums.collect(1)
         late.collect(0)
         sums.collect(0)
-        sums.total()
-        late.total()
+        for copy in sums.keep + late.keep:
+            copy.wait()
         s.drain()
     for c in range(steps):
         store1(c).wait()
@@ -1355,10 +1460,13 @@
     shard = hidden // (pieces * planes)
     late = shard // 4
     buffers, params = [], {}
+    g2_shape = [shape(w2.shape, LOW)]
     if remote:
+        g2_shape = [shape((4, shard - late, width), LOW), shape((4, late, width), LOW)]
         buffers = pair_of_semaphores(Reducer.COPIES + ReducerAlongZ.COPIES)
-        buffers += Reducer.scratch(shard - late, width, in_place=True)
-        buffers += ReducerAlongZ.scratch(late, width, in_place=True)
+        buffers += Reducer.scratch(shard - late, width, in_place=True)[:3]
+        buffers += ReducerAlongZ.scratch(late, width, in_place=True)[::3]
+        buffers += [pltpu.SemaphoreType.DMA((4,)), pltpu.SemaphoreType.DMA((4,))]
         params = dict(collective_id=4, has_side_effects=True)
     return pl.pallas_call(
         functools.partial(middle_kernel, chunk, width // (pieces * planes), remote),
@@ -1368,10 +1476,10 @@
             shape((pieces, count, width // pieces), LOW),
             shape((pieces, -(-planes // 8) * 8, 384), HIGH),
             shape(w1.shape, LOW),
-            shape((shard, width), HIGH) if remote else shape(w2.shape, LOW),
+            *g2_shape,
         ),
         in_specs=[vmem] * 6 + in_hbm(4),
-        out_specs=(vmem,) * 4 + tuple(in_hbm(1)) + ((vmem,) if remote else tuple(in_hbm(1))),
+        out_specs=(vmem,) * 4 + tuple(in_hbm(1 + len(g2_shape))),
         scratch_shapes=[
             pltpu.VMEM(w1.shape, LOW),
             pltpu.VMEM(w2.shape, LOW),
@@ -1646,12 +1754,12 @@
     middle_out = middle(
         attended, n1, r1, normed_t, cot, cuts, act, slope, W1, W2, n_blk, n_dp, fast
     )
-    output, d_first, d_att, small_rows, grad_both, grad_reduce = middle_out
+    output, d_first, d_att, small_rows, grad_both, grad_reduce = middle_out[:6]
     output = output.reshape(slots, rows, width)
     if fast:
         grad_both = grad_both.reshape(n_blk, n_dp, shard, -1)
-        dq, dk, dv, sum_expand, sum_output, tok0 = back(
-            d_att, qh, kh, v, att, lse, W, d_first, grad_both
+        dq, dk, dv, sum_expand, sum_output, sum_reduce, tok0 = back(
+            d_att, qh, kh, v, att, lse, W, d_first, grad_both, grad_reduce, middle_out[6]
         )
         grad_tokens, grad_input, d_gains, d_biases, d_hidden = finish(
             dq, dk, dv, W, d_first, tok0, small_rows, X
@@ -1662,7 +1770,7 @@
             grad_input,
             sum_output,
             sum_expand,
-            grad_reduce,
+            sum_reduce,
             d_gains,
             d_biases,
             d_hidden.reshape(-1),

time: 330 us -> 319 us (0.967)
  Pallas kernels: 315 us -> 304 us
    pallas_call x1, Pallas kernels: 60.1 us -> 50 us  [middle(): pl.pallas_call(functools.partial(middle_kernel, chunk, width // (pieces *...]
where the time goes in v8:
time: 319 us; the launch traced here: 314 us
  Pallas kernels  304 us (95%)
  local copies, waits for them, and re-layouts  8.82 us (3%)
    pallas_call x1, Pallas kernels, front(): pl.pallas_call(front_kernel, out_shape=(shape(8, count + 16, width), shap...  137 us
    pallas_call x1, Pallas kernels, back(): pl.pallas_call(back_kernel, out_shape=(shape(v.shape, LOW),) * 3 + (shape...  78.9 us
    pallas_call x1, Pallas kernels, middle(): pl.pallas_call(functools.partial(middle_kernel, chunk, width // (pieces *...  50 us
    pallas_call x1, Pallas kernels, finish(): pl.pallas_call(finish_kernel, out_shape=(shape(2 * rows, width), shape(sh...  38.8 us
    unnamed x25, local copies, waits for them, and re-layouts  8.82 us

profile of v8, /device:TPU:0, one launch (start us, length us, event | category | flops | bytes accessed | tf_op | source)
XLA Modules:
  0.0 314.4 jit_solution(11284170839258973508)
XLA Ops:
  0.6 136.7 %front.1 = (bf16[8,528,1024]{2,1,0:T(8,128)(2,1)}, bf16[8,4,32,5120]{3,2,1,0:T(8,128)(2,1)}, bf16[8,4,128,1024]{3,2,1,0:T(8,128)(2,1)}, bf16[512,4096]{1,0:T(8,1...) custom-call(bf16[512,1024]{1,0:T(8,128)(2,1)} %bitcast.14, ...), custom_call_target="tpu_custom_call" | custom-call | tf_op jit(solution)/shard_map/front/pallas_call | solution.py:564
  137.4 50.0 %middle.1 = (bf16[512,1024]{1,0:T(8,128)(2,1)}, f32[512,1024]{1,0:T(8,128)}, bf16[8,512,128]{2,1,0:T(8,128)(2,1)}, f32[8,8,384]{2,1,0:T(8,128)}, bf16[1024,5120]...) custom-call(bf16[512,1024]{1,0:T(8,128)(2,1)} %get-tuple-element.44.att, ...), custom_call_target="tpu_custom_call" | custom-call | tf_op jit(solution)/shard_map/middle/pallas_call | solution.py:1471
  187.4 78.9 %back.1 = (bf16[8,2,256,128]{3,2,1,0:T(8,128)(2,1)}, bf16[8,2,256,128]{3,2,1,0:T(8,128)(2,1)}, bf16[8,2,256,128]{3,2,1,0:T(8,128)(2,1)}, f32[32,4096]{1,0:T(8,12...) custom-call(bf16[8,512,128]{2,1,0:T(8,128)(2,1)} %get-tuple-element.54.d_att, ...), custom_call_target="tpu_custom_call" | custom-call | tf_op jit(solution)/shard_map/back/pallas_call | solution.py:1222
  266.3 0.0 copy-start
  266.3 38.8 %finish.1 = (f32[512,1024]{1,0:T(8,128)}, f32[32,3072]{1,0:T(8,128)}, f32[2,32]{1,0:T(2,128)}, f32[6,32]{1,0:T(8,128)}, f32[1,128]{1,0:T(1,128)}) custom-call(bf16[8,2,256,128]{3,2,1,0:T(8,128)(2,1)} %get-tuple-element.65.dq, bf16[8,2,256,128]{3,2,1,0:T(8,128)(2,1)} %get-tuple-element.66.dk, bf16[8,2,256,128]{3,2,1,0:T(8,128)(2,1)} %get-tuple-element.67.dv, ...), custom_call_target="tpu_custom_call" | custom-call | tf_op jit(solution)/shard_map/finish/pallas_call | solution.py:1626
  305.1 0.0 copy-start.3
  305.1 0.0 copy-start.4
  305.1 0.0 copy-start.2
  305.1 0.0 copy-done
  305.1 0.0 copy-start.1
  305.1 1.0 copy.29
  306.1 0.0 copy-start.6
  306.1 0.0 copy-start.5
  306.1 0.0 copy-start.7
  306.1 3.2 %copy.30 = f32[2,256,1024]{2,1,0:T(8,128)} copy(f32[2,256,1024]{2,1,0:T(8,128)} %bitcast.12) | data formatting | bytes 4194304
  309.3 0.0 copy-done.3
  309.3 0.7 copy.31
  310.0 0.0 copy-done.4
  310.0 0.7 copy.32
  310.7 0.0 copy-done.2
  310.7 0.8 copy.33
  311.5 0.0 copy-done.1
  311.5 0.8 copy.34
  312.3 0.0 copy-done.6
  312.3 0.6 copy.35
  312.9 0.0 copy-done.5
  312.9 0.6 copy.36
  313.5 0.0 copy-done.7
  313.5 0.5 copy.37
Async XLA Ops:
  266.3 38.8 %copy-start = (bf16[512,1024]{1,0:T(8,128)(2,1)S(1)}, bf16[512,1024]{1,0:T(8,128)(2,1)}, u32[]{:S(2)}) copy-start(bf16[512,1024]{1,0:T(8,128)(2,1)} %get-tuple-element.53) | copy-start | bytes 3145732
  305.1 4.2 %copy-start.3 = (f32[32,3072]{1,0:T(8,128)S(1)}, f32[32,3072]{1,0:T(8,128)}, u32[]{:S(2)}) copy-start(f32[32,3072]{1,0:T(8,128)} %get-tuple-element.90) | copy-start | bytes 1179652
  305.1 4.9 %copy-start.4 = (f32[32,1024]{1,0:T(8,128)S(1)}, f32[32,1024]{1,0:T(8,128)}, u32[]{:S(2)}) copy-start(f32[32,1024]{1,0:T(8,128)} %get-tuple-element.91) | copy-start | bytes 393220
  305.1 5.6 %copy-start.2 = (f32[32,4096]{1,0:T(8,128)S(1)}, f32[32,4096]{1,0:T(8,128)}, u32[]{:S(2)}) copy-start(f32[32,4096]{1,0:T(8,128)} %get-tuple-element.92) | copy-start | bytes 1572868
  305.1 6.4 %copy-start.1 = (f32[128,1024]{1,0:T(8,128)S(1)}, f32[128,1024]{1,0:T(8,128)}, u32[]{:S(2)}) copy-start(f32[128,1024]{1,0:T(8,128)} %get-tuple-element.93) | copy-start | bytes 1572868
  306.1 6.2 %copy-start.6 = (f32[2,32]{1,0:T(2,128)S(1)}, f32[2,32]{1,0:T(2,128)}, u32[]{:S(2)}) copy-start(f32[2,32]{1,0:T(2,128)} %get-tuple-element.94) | copy-start | bytes 772
  306.1 6.7 %copy-start.5 = (f32[6,32]{1,0:T(8,128)S(1)}, f32[6,32]{1,0:T(8,128)}, u32[]{:S(2)}) copy-start(f32[6,32]{1,0:T(8,128)} %get-tuple-element.95) | copy-start | bytes 2308
  306.1 7.3 %copy-start.7 = (f32[1,128]{1,0:T(1,128)S(1)}, f32[1,128]{1,0:T(1,128)}, u32[]{:S(2)}) copy-start(f32[1,128]{1,0:T(1,128)} %get-tuple-element.78) | copy-start | bytes 1540

commit v9 on v8

--- a/solution.py
+++ b/solution.py
@@ -185,6 +185,16 @@
     slope_out,
     wfull,
     small,
+    qh_out,
+    kh_out,
+    v_out,
+    att_out,
+    lse_out,
+    branch_in_out,
+    n1_out,
+    r1_out,
+    normed_t_out,
+    par,
     qh,
     kh,
     v,
@@ -194,7 +204,6 @@
     n1,
     r1,
     normed_t,
-    par,
     normed_low,
     X,
     W,
@@ -213,6 +222,7 @@
     osem,
     wsem,
     csem,
+    fsem,
 ):
     b, z = position()
     bx, by, bd, bc = b ^ 2, b ^ 4, b ^ 6, b ^ 1
@@ -478,6 +488,12 @@
         for at, (event, *what) in events.items():
             pl.when(step == at)(functools.partial(event, *what))
 
+    early = [(qh, qh_out), (kh, kh_out), (v, v_out), (att, att_out), (lse, lse_out)]
+    early += [(branch_in, branch_in_out), (n1, n1_out), (r1, r1_out), (normed_t, normed_t_out)]
+    early = [pltpu.make_async_copy(*pair, fsem.at[i]) for i, pair in enumerate(early)]
+    for copy in early[:5]:
+        copy.start()
+
     third(3)
     for copy in core1.values():
         copy.wait_recv()
@@ -513,6 +529,8 @@
     normed = (normal * par[0:1] + par[5:6]).astype(LOW)
     normed_low[...] = normed
     normed_t[...] = normed.T
+    for copy in early[5:]:
+        copy.start()
 
     def store(c, ref, out, which):
         cols = pl.ds(pl.multiple_of(c * chunk, chunk), chunk)
@@ -540,6 +558,8 @@
         store(c, act, act_out, 0).wait()
         store(c, slope, slope_out, 1).wait()
     s.drain()
+    for copy in early:
+        copy.wait()
     locs[3].wait()
     for i in range(8):
         pltpu.make_async_copy(X.at[i], X_out.at[i], osem.at[i]).wait()
@@ -583,8 +603,17 @@
             wide(8, width),
         ),
         in_specs=in_hbm(1) + [vmem] * 6 + in_hbm(3),
-        out_specs=tuple(in_hbm(5)) + (vmem,) * 12,
+        out_specs=tuple(in_hbm(5)) + (vmem,) * 2 + tuple(in_hbm(9)) + (vmem,),
         scratch_shapes=[
+            pltpu.VMEM((2, 8, slots, rows, 128), LOW),
+            pltpu.VMEM((2, 8, slots, rows, 128), LOW),
+            pltpu.VMEM((8, slots, rows, 128), LOW),
+            pltpu.VMEM((8, slots, rows, 128), LOW),
+            pltpu.VMEM((slots, 8, 8 * rows), HIGH),
+            pltpu.VMEM((count, width), LOW),
+            pltpu.VMEM((count, width), HIGH),
+            pltpu.VMEM((count, 128), HIGH),
+            pltpu.VMEM((width, count), LOW),
             pltpu.VMEM((count, width), LOW),
             pltpu.VMEM((8, count + 16, width), LOW),
             pltpu.VMEM((4, 8, shard + 16, 384), LOW),
@@ -599,7 +628,8 @@
         + pair_of_semaphores(116)
         + pair_of_semaphores(8 * slots)
         + [pltpu.SemaphoreType.DMA((5,)), pltpu.SemaphoreType.DMA((8 + slots,))]
-        + [pltpu.SemaphoreType.DMA((hidden // 512 + 1,)), pltpu.SemaphoreType.DMA((2, hidden // 512))],
+        + [pltpu.SemaphoreType.DMA((hidden // 512 + 1,)), pltpu.SemaphoreType.DMA((2, hidden // 512))]
+        + [pltpu.SemaphoreType.DMA((9,))],
         compiler_params=pltpu.CompilerParams(
             collective_id=1, has_side_effects=True, vmem_limit_bytes=VMEM_LIMIT
         ),
@@ -1263,11 +1293,11 @@
     chunk,
     small_rows,
     remote,
-    att,
+    att_in,
     n1,
-    r1,
-    normed_t,
-    cot_ref,
+    r1_in,
+    normed_in,
+    cot_in,
     par_ref,
     act_hbm,
     slope_hbm,
@@ -1283,7 +1313,10 @@
 ):
     if remote:
         g2_late, *rest = rest
-    w1, w2, act, slope, acc, low, sums_ref, d_hid_ref, wsem, gsem, *buffers = rest
+    w1, w2, act, slope, acc, low, sums_ref, d_hid_ref, wsem, gsem, *rest = rest
+    att, r1, normed_t, cot_ref, isem, *buffers = rest
+    inputs = ((cot_in, cot_ref), (normed_in, normed_t), (r1_in, r1), (att_in, att))
+    inputs = [pltpu.make_async_copy(*pair, isem.at[i]) for i, pair in enumerate(inputs)]
     hidden, width = w2.shape
     steps = hidden // chunk
     pieces, _, held = d_att_ref.shape
@@ -1315,8 +1348,12 @@
     for c in range(steps):
         load_act(c).start()
         load2(c).start()
+    inputs[0].start()
     for c in range(steps):
         load_slope(c).start()
+    for copy in inputs[1:]:
+        copy.start()
+    for c in range(steps):
         load1(c).start()
     load_out = pltpu.make_async_copy(w1_hbm.at[:, last], w1.at[:, last], wsem.at[0, steps])
     load_out.start()
@@ -1331,6 +1368,7 @@
         acc[...] += product(act[:, columns(c)], w2[columns(c), :])
 
     normal, inverse2 = normalize(acc[...])
+    inputs[0].wait()
     out_ref[...] = (normal * gain2 + bias(5)).astype(LOW)
     cot = cot_ref[...].astype(HIGH)
     d_second = normalize_back(cot * gain2, normal, inverse2)
@@ -1400,6 +1438,9 @@
         if not remote:
             store2(c).start()
         run(first_events, step)
+
+    for copy in inputs[1:]:
+        copy.wait()
 
     @pl.loop(0, steps)
     def _(c):
@@ -1478,7 +1519,7 @@
             shape(w1.shape, LOW),
             *g2_shape,
         ),
-        in_specs=[vmem] * 6 + in_hbm(4),
+        in_specs=in_hbm(1) + [vmem] + in_hbm(3) + [vmem] + in_hbm(4),
         out_specs=(vmem,) * 4 + tuple(in_hbm(1 + len(g2_shape))),
         scratch_shapes=[
             pltpu.VMEM(w1.shape, LOW),
@@ -1491,6 +1532,11 @@
             pltpu.VMEM((1, hidden), HIGH),
             pltpu.SemaphoreType.DMA((4, hidden // chunk + 1)),
             pltpu.SemaphoreType.DMA((2, hidden // chunk + 1)),
+            pltpu.VMEM(att.shape, LOW),
+            pltpu.VMEM(r1.shape, HIGH),
+            pltpu.VMEM(normed_t.shape, LOW),
+            pltpu.VMEM(cot.shape, LOW),
+            pltpu.SemaphoreType.DMA((4,)),
         ]
         + buffers,
         compiler_params=pltpu.CompilerParams(vmem_limit_bytes=VMEM_LIMIT, **params),
@@ -1560,10 +1606,20 @@
     def share(d):
         return D.at[:, pl.ds(pl.multiple_of((z ^ d) * share_rows, share_rows), share_rows)]
 
-    in_z = [s.go(share(d), Z.at[d - 1], (b, z ^ d), Z.at[d - 1]) for d in (1, 2, 3)]
+    in_z = {
+        d: s.plan(share(d), Z.at[d - 1], (b, z ^ (2 if d == 2 else 1)), Z.at[d - 1])
+        for d in (3, 1, 2)
+    }
+    in_z[3].go()
+    in_z[1].go()
     for e in (3, 2, 1, 0):
         tokens.give(e)
-    for e in (3, 2, 1, 0):
+    tokens.take(3)
+    in_z[3].wait_recv()
+    onward = share(2)
+    onward[...] = onward[...] + Z[2]
+    in_z[2].go()
+    for e in (2, 1, 0):
         tokens.take(e)
 
     N[...] = small[b]
@@ -1577,10 +1633,10 @@
         N[row : row + 1, 0:128] = whole
     small_z = [s.go(N, T.at[d - 1], (b, z ^ d), T.at[d - 1]) for d in (1, 2, 3)]
 
-    for copy in in_z:
-        copy.wait_recv()
+    in_z[1].wait_recv()
+    in_z[2].wait_recv()
     plane = share(0)[...].astype(HIGH)
-    for i in range(3):
+    for i in range(2):
         plane = plane + Z[i].astype(HIGH)
     P[...] = plane
     grads_in = [

time: 319 us -> 315 us (0.987)
  Pallas kernels: 304 us -> 300 us
    pallas_call x1, Pallas kernels: 137 us -> 133 us  [front(): pl.pallas_call(front_kernel, out_shape=(shape(8, count + 16, width), shap...]
where the time goes in v9:
time: 315 us; the launch traced here: 310 us
  Pallas kernels  300 us (95%)
  local copies, waits for them, and re-layouts  8.82 us (3%)
    pallas_call x1, Pallas kernels, front(): pl.pallas_call(front_kernel, out_shape=(shape(8, count + 16, width), shap...  133 us
    pallas_call x1, Pallas kernels, back(): pl.pallas_call(back_kernel, out_shape=(shape(v.shape, LOW),) * 3 + (shape...  79 us
    pallas_call x1, Pallas kernels, middle(): pl.pallas_call(functools.partial(middle_kernel, chunk, width // (pieces *...  49.2 us
    pallas_call x1, Pallas kernels, finish(): pl.pallas_call(finish_kernel, out_shape=(shape(2 * rows, width), shape(sh...  38.7 us
    unnamed x25, local copies, waits for them, and re-layouts  8.82 us

profile of v9, /device:TPU:0, one launch (start us, length us, event | category | flops | bytes accessed | tf_op | source)
XLA Modules:
  0.0 310.3 jit_solution(4692380310757843409)
XLA Ops:
  0.6 133.5 %front.1 = (bf16[8,528,1024]{2,1,0:T(8,128)(2,1)}, bf16[8,4,32,5120]{3,2,1,0:T(8,128)(2,1)}, bf16[8,4,128,1024]{3,2,1,0:T(8,128)(2,1)}, bf16[512,4096]{1,0:T(8,1...) custom-call(bf16[512,1024]{1,0:T(8,128)(2,1)} %bitcast.14, ...), custom_call_target="tpu_custom_call" | custom-call | tf_op jit(solution)/shard_map/front/pallas_call | solution.py:584
  134.1 49.2 %middle.1 = (bf16[512,1024]{1,0:T(8,128)(2,1)}, f32[512,1024]{1,0:T(8,128)}, bf16[8,512,128]{2,1,0:T(8,128)(2,1)}, f32[8,8,384]{2,1,0:T(8,128)}, bf16[1024,5120]...) custom-call(bf16[512,1024]{1,0:T(8,128)(2,1)} %get-tuple-element.44.att_in, ...), custom_call_target="tpu_custom_call" | custom-call | tf_op jit(solution)/shard_map/middle/pallas_call | solution.py:1512
  183.3 79.0 %back.1 = (bf16[8,2,256,128]{3,2,1,0:T(8,128)(2,1)}, bf16[8,2,256,128]{3,2,1,0:T(8,128)(2,1)}, bf16[8,2,256,128]{3,2,1,0:T(8,128)(2,1)}, f32[32,4096]{1,0:T(8,12...) custom-call(bf16[8,512,128]{2,1,0:T(8,128)(2,1)} %get-tuple-element.54.d_att, ...), custom_call_target="tpu_custom_call" | custom-call | tf_op jit(solution)/shard_map/back/pallas_call | solution.py:1252
  262.3 0.0 copy-start
  262.3 38.7 %finish.1 = (f32[512,1024]{1,0:T(8,128)}, f32[32,3072]{1,0:T(8,128)}, f32[2,32]{1,0:T(2,128)}, f32[6,32]{1,0:T(8,128)}, f32[1,128]{1,0:T(1,128)}) custom-call(bf16[8,2,256,128]{3,2,1,0:T(8,128)(2,1)} %get-tuple-element.65.dq, bf16[8,2,256,128]{3,2,1,0:T(8,128)(2,1)} %get-tuple-element.66.dk, bf16[8,2,256,128]{3,2,1,0:T(8,128)(2,1)} %get-tuple-element.67.dv, ...), custom_call_target="tpu_custom_call" | custom-call | tf_op jit(solution)/shard_map/finish/pallas_call | solution.py:1682
  301.0 0.0 copy-start.3
  301.0 0.0 copy-start.4
  301.0 0.0 copy-start.2
  301.0 0.0 copy-done
  301.1 0.0 copy-start.1
  301.1 1.0 copy.29
  302.0 0.0 copy-start.6
  302.0 0.0 copy-start.5
  302.0 0.0 copy-start.7
  302.0 3.2 %copy.30 = f32[2,256,1024]{2,1,0:T(8,128)} copy(f32[2,256,1024]{2,1,0:T(8,128)} %bitcast.12) | data formatting | bytes 4194304
  305.2 0.0 copy-done.3
  305.2 0.7 copy.31
  306.0 0.0 copy-done.4
  306.0 0.7 copy.32
  306.6 0.0 copy-done.2
  306.6 0.8 copy.33
  307.4 0.0 copy-done.1
  307.4 0.8 copy.34
  308.2 0.0 copy-done.6
  308.2 0.6 copy.35
  308.8 0.0 copy-done.5
  308.8 0.6 copy.36
  309.4 0.0 copy-done.7
  309.4 0.5 copy.37
Async XLA Ops:
  262.3 38.7 %copy-start = (bf16[512,1024]{1,0:T(8,128)(2,1)S(1)}, bf16[512,1024]{1,0:T(8,128)(2,1)}, u32[]{:S(2)}) copy-start(bf16[512,1024]{1,0:T(8,128)(2,1)} %get-tuple-element.53) | copy-start | bytes 3145732
  301.0 4.2 %copy-start.3 = (f32[32,3072]{1,0:T(8,128)S(1)}, f32[32,3072]{1,0:T(8,128)}, u32[]{:S(2)}) copy-start(f32[32,3072]{1,0:T(8,128)} %get-tuple-element.90) | copy-start | bytes 1179652
  301.0 4.9 %copy-start.4 = (f32[32,1024]{1,0:T(8,128)S(1)}, f32[32,1024]{1,0:T(8,128)}, u32[]{:S(2)}) copy-start(f32[32,1024]{1,0:T(8,128)} %get-tuple-element.91) | copy-start | bytes 393220
  301.0 5.6 %copy-start.2 = (f32[32,4096]{1,0:T(8,128)S(1)}, f32[32,4096]{1,0:T(8,128)}, u32[]{:S(2)}) copy-start(f32[32,4096]{1,0:T(8,128)} %get-tuple-element.92) | copy-start | bytes 1572868
  301.1 6.4 %copy-start.1 = (f32[128,1024]{1,0:T(8,128)S(1)}, f32[128,1024]{1,0:T(8,128)}, u32[]{:S(2)}) copy-start(f32[128,1024]{1,0:T(8,128)} %get-tuple-element.93) | copy-start | bytes 1572868
  302.0 6.2 %copy-start.6 = (f32[2,32]{1,0:T(2,128)S(1)}, f32[2,32]{1,0:T(2,128)}, u32[]{:S(2)}) copy-start(f32[2,32]{1,0:T(2,128)} %get-tuple-element.94) | copy-start | bytes 772
  302.0 6.7 %copy-start.5 = (f32[6,32]{1,0:T(8,128)S(1)}, f32[6,32]{1,0:T(8,128)}, u32[]{:S(2)}) copy-start(f32[6,32]{1,0:T(8,128)} %get-tuple-element.95) | copy-start | bytes 2308
  302.0 7.3 %copy-start.7 = (f32[1,128]{1,0:T(1,128)S(1)}, f32[1,128]{1,0:T(1,128)}, u32[]{:S(2)}) copy-start(f32[1,128]{1,0:T(1,128)} %get-tuple-element.78) | copy-start | bytes 1540

commit v10 on v9

--- a/solution.py
+++ b/solution.py
@@ -1094,13 +1094,17 @@
     g1,
     g2_planes,
     g2_late,
-    dq,
-    dk,
-    dv,
+    dq_out,
+    dk_out,
+    dv_out,
     o1,
     out_o,
     o2,
     tok,
+    dq,
+    dk,
+    dv,
+    qsem,
     qh,
     kh,
     v,
@@ -1182,6 +1186,18 @@
         part = pl.ds(pl.multiple_of(slot * rows, rows), rows)
         return rows_of(grads[:, part])
 
+    stores = [
+        [
+            pltpu.make_async_copy(src.at[:, slot], dst.at[:, slot], qsem.at[i, slot])
+            for i, (src, dst) in enumerate(((dq, dq_out), (dk, dk_out), (dv, dv_out)))
+        ]
+        for slot in range(slots)
+    ]
+
+    def store(slot):
+        for copy in stores[slot]:
+            copy.start()
+
     events = {
         0: [(late.fold, 0)],
         1: [(sums.fold, 2), (late.relay, 3)],
@@ -1191,7 +1207,7 @@
         5: [(late.relay, 0), (sums.relay, 2)],
         6: [(sums.fold, 0), (late.collect, 3), (arrive, 1)],
         7: [(sums.collect, 3), (late.collect, 1), (planes.start,), (chips.start,)],
-        8: [(sums.relay, 1), (late.collect, 2), (tokens.give, 3), (tokens.give, 2)],
+        8: [(store, 0), (sums.relay, 1), (late.collect, 2), (tokens.give, 3), (tokens.give, 2)],
         9: [(sums.collect, 2), (tokens.give, 1), (tokens.take, 3), (chips.relay,)],
         10: [(tokens.give, 0), (tokens.take, 2)],
         11: [(sums.relay, 0), (late.cross,), (tokens.take, 1), (planes.relay,)],
@@ -1231,6 +1247,7 @@
                 for event, *what in some:
                     event(*what)
 
+    store(slots - 1)
     sums.collect(0)
     late.total()
     rest = o1.shape[1] - most
@@ -1238,6 +1255,8 @@
     out_o[...] = tail[:, rest:]
     sums.total()
     tok[...] = first_rows[...] + tokens.total()
+    for copy in stores[0] + stores[1]:
+        copy.wait()
     s.drain()
 
 
@@ -1259,8 +1278,10 @@
             shape((rows, width), HIGH),
         ),
         in_specs=in_hbm(11),
-        out_specs=(vmem,) * 7,
-        scratch_shapes=[scratch(a) for a in (qh, kh, v, att, lse, w)]
+        out_specs=tuple(in_hbm(3)) + (vmem,) * 4,
+        scratch_shapes=[pltpu.VMEM(v.shape, LOW)] * 3
+        + [pltpu.SemaphoreType.DMA((3, slots))]
+        + [scratch(a) for a in (qh, kh, v, att, lse, w)]
         + [
             pltpu.VMEM((rows, width), HIGH),
             pltpu.VMEM((shard, late), HIGH),

time: 315 us -> 314 us (level)
  no operation moved by 1% of the time
where the time goes in v10:
time: 314 us; the launch traced here: 309 us
  Pallas kernels  299 us (95%)
  local copies, waits for them, and re-layouts  8.82 us (3%)
    pallas_call x1, Pallas kernels, front(): pl.pallas_call(front_kernel, out_shape=(shape(8, count + 16, width), shap...  133 us
    pallas_call x1, Pallas kernels, back(): pl.pallas_call(back_kernel, out_shape=(shape(v.shape, LOW),) * 3 + (shape...  78.2 us
    pallas_call x1, Pallas kernels, middle(): pl.pallas_call(functools.partial(middle_kernel, chunk, width // (pieces *...  49.2 us
    pallas_call x1, Pallas kernels, finish(): pl.pallas_call(finish_kernel, out_shape=(shape(2 * rows, width), shape(sh...  38.6 us
    unnamed x25, local copies, waits for them, and re-layouts  8.82 us

profile of v10, /device:TPU:0, one launch (start us, length us, event | category | flops | bytes accessed | tf_op | source)
XLA Modules:
  0.0 309.4 jit_solution(5860309803936963314)
XLA Ops:
  0.6 133.5 %front.1 = (bf16[8,528,1024]{2,1,0:T(8,128)(2,1)}, bf16[8,4,32,5120]{3,2,1,0:T(8,128)(2,1)}, bf16[8,4,128,1024]{3,2,1,0:T(8,128)(2,1)}, bf16[512,4096]{1,0:T(8,1...) custom-call(bf16[512,1024]{1,0:T(8,128)(2,1)} %bitcast.14, ...), custom_call_target="tpu_custom_call" | custom-call | tf_op jit(solution)/shard_map/front/pallas_call | solution.py:584
  134.1 49.2 %middle.1 = (bf16[512,1024]{1,0:T(8,128)(2,1)}, f32[512,1024]{1,0:T(8,128)}, bf16[8,512,128]{2,1,0:T(8,128)(2,1)}, f32[8,8,384]{2,1,0:T(8,128)}, bf16[1024,5120]...) custom-call(bf16[512,1024]{1,0:T(8,128)(2,1)} %get-tuple-element.44.att_in, ...), custom_call_target="tpu_custom_call" | custom-call | tf_op jit(solution)/shard_map/middle/pallas_call | solution.py:1533
  183.3 78.2 %back.1 = (bf16[8,2,256,128]{3,2,1,0:T(8,128)(2,1)}, bf16[8,2,256,128]{3,2,1,0:T(8,128)(2,1)}, bf16[8,2,256,128]{3,2,1,0:T(8,128)(2,1)}, f32[32,4096]{1,0:T(8,12...) custom-call(bf16[8,512,128]{2,1,0:T(8,128)(2,1)} %get-tuple-element.54.d_att, ...), custom_call_target="tpu_custom_call" | custom-call | tf_op jit(solution)/shard_map/back/pallas_call | solution.py:1271
  261.5 0.0 copy-start
  261.5 38.6 %finish.1 = (f32[512,1024]{1,0:T(8,128)}, f32[32,3072]{1,0:T(8,128)}, f32[2,32]{1,0:T(2,128)}, f32[6,32]{1,0:T(8,128)}, f32[1,128]{1,0:T(1,128)}) custom-call(bf16[8,2,256,128]{3,2,1,0:T(8,128)(2,1)} %get-tuple-element.65.dq, bf16[8,2,256,128]{3,2,1,0:T(8,128)(2,1)} %get-tuple-element.66.dk, bf16[8,2,256,128]{3,2,1,0:T(8,128)(2,1)} %get-tuple-element.67.dv, ...), custom_call_target="tpu_custom_call" | custom-call | tf_op jit(solution)/shard_map/finish/pallas_call | solution.py:1703
  300.1 0.0 copy-start.3
  300.1 0.0 copy-start.4
  300.1 0.0 copy-start.2
  300.2 0.0 copy-done
  300.2 0.0 copy-start.1
  300.2 1.0 copy.29
  301.1 0.0 copy-start.6
  301.2 0.0 copy-start.5
  301.2 0.0 copy-start.7
  301.2 3.2 %copy.30 = f32[2,256,1024]{2,1,0:T(8,128)} copy(f32[2,256,1024]{2,1,0:T(8,128)} %bitcast.12) | data formatting | bytes 4194304
  304.3 0.0 copy-done.3
  304.3 0.7 copy.31
  305.1 0.0 copy-done.4
  305.1 0.7 copy.32
  305.7 0.0 copy-done.2
  305.7 0.8 copy.33
  306.5 0.0 copy-done.1
  306.5 0.8 copy.34
  307.3 0.0 copy-done.6
  307.3 0.6 copy.35
  307.9 0.0 copy-done.5
  307.9 0.6 copy.36
  308.5 0.0 copy-done.7
  308.5 0.5 copy.37
Async XLA Ops:
  261.5 38.6 %copy-start = (bf16[512,1024]{1,0:T(8,128)(2,1)S(1)}, bf16[512,1024]{1,0:T(8,128)(2,1)}, u32[]{:S(2)}) copy-start(bf16[512,1024]{1,0:T(8,128)(2,1)} %get-tuple-element.53) | copy-start | bytes 3145732
  300.1 4.2 %copy-start.3 = (f32[32,3072]{1,0:T(8,128)S(1)}, f32[32,3072]{1,0:T(8,128)}, u32[]{:S(2)}) copy-start(f32[32,3072]{1,0:T(8,128)} %get-tuple-element.90) | copy-start | bytes 1179652
  300.1 4.9 %copy-start.4 = (f32[32,1024]{1,0:T(8,128)S(1)}, f32[32,1024]{1,0:T(8,128)}, u32[]{:S(2)}) copy-start(f32[32,1024]{1,0:T(8,128)} %get-tuple-element.91) | copy-start | bytes 393220
  300.1 5.6 %copy-start.2 = (f32[32,4096]{1,0:T(8,128)S(1)}, f32[32,4096]{1,0:T(8,128)}, u32[]{:S(2)}) copy-start(f32[32,4096]{1,0:T(8,128)} %get-tuple-element.92) | copy-start | bytes 1572868
  300.2 6.4 %copy-start.1 = (f32[128,1024]{1,0:T(8,128)S(1)}, f32[128,1024]{1,0:T(8,128)}, u32[]{:S(2)}) copy-start(f32[128,1024]{1,0:T(8,128)} %get-tuple-element.93) | copy-start | bytes 1572868
  301.1 6.2 %copy-start.6 = (f32[2,32]{1,0:T(2,128)S(1)}, f32[2,32]{1,0:T(2,128)}, u32[]{:S(2)}) copy-start(f32[2,32]{1,0:T(2,128)} %get-tuple-element.94) | copy-start | bytes 772
  301.2 6.7 %copy-start.5 = (f32[6,32]{1,0:T(8,128)S(1)}, f32[6,32]{1,0:T(8,128)}, u32[]{:S(2)}) copy-start(f32[6,32]{1,0:T(8,128)} %get-tuple-element.95) | copy-start | bytes 2308
  301.2 7.3 %copy-start.7 = (f32[1,128]{1,0:T(1,128)S(1)}, f32[1,128]{1,0:T(1,128)}, u32[]{:S(2)}) copy-start(f32[1,128]{1,0:T(1,128)} %get-tuple-element.78) | copy-start | bytes 1540
